TPU v7x, 128 devices: a whole 4x4x4 slice. The times are simulated.
128 devices in a mesh: tx: 8 (over y_lo, x), ty: 16 (over y_hi, z, core).
Axes of the slice: x: 4, y: 4 (y_hi: 2, y_lo: 2; y = y_hi * 2 + y_lo), z: 4, core: 2. Of those that a mesh axis runs over, the one named last changes fastest.
Arguments:
- far_adjoint: bfloat16 [2, 4096, 8192], P(None, 'tx', 'ty'), may hold values from -6 to 6
- pillar: float32 [4096, 8192], P('tx', 'ty'), may hold values from -1 to 1
- green_blocks: bfloat16 [8, 2, 256, 256], replicated, may hold values from -0.09375 to 0.09375
- pair_src: int32 [8, 16, 24576], P('tx', 'ty'), may hold values from 0 to 1023, as said below
- pair_dst: int32 [8, 16, 24576], P('tx', 'ty'), may hold values from 0 to 3135, as said below
- group_end: int32 [8, 16, 8], P('tx', 'ty'), may hold values from 0 to 24576, as said below
- w_in: float32 [64, 9], replicated, may hold values from -2 to 2
- b_in: float32 [64], replicated, may hold values from -3 to 3
- w_out: float32 [2, 64], replicated, may hold values from -0.75 to 0.75
Outputs:
- grad_pillar: float32 [4096, 8192], P('tx', 'ty')
- grad_w_in: float32 [64, 9], replicated
- grad_b_in: float32 [64], replicated
- grad_w_out: float32 [2, 64], replicated
Inputs may be any that keep to these rules, and one draw needn't show every extreme that they name: `pair_src`: the source block of each slot, numbered row by row over the tile's 32 x 32 blocks. `pair_dst`: the target block of each slot, numbered row by row over the tile's blocks extended by 12 blocks on every side (56 to a row); it lies at most 12 blocks from the slot's source block along each dimension. `group_end`: per tile, nondecreasing ends of the runs of slots that use Green's blocks 0 to 7 in order; the last is the tile's number of live pairs, 3072 or more, and some tile has all 24576 slots live.
All inputs are finite; a program needn't handle non-finite values.
Results may differ from a plain program's by a relative error of at most 0.0003.
Values may be sent and summed in bfloat16 or wider, within the bound.
A program may use at most 128 MiB of HBM per device.

v0:
```python
import jax
import jax.numpy as jnp
from jax import lax
from jax.sharding import PartitionSpec as P

BLK = 16
CONE = 12


highest = lax.Precision.HIGHEST


def with_halo(shard, sides, width):
    for axis, dim in sides:
        count, length = (lax.axis_size(axis), shard.shape[dim])
        up = [(i, (i + 1) % count) for i in range(count - 1)]
        down = [(j, i) for i, j in up]
        last = lax.slice_in_dim(shard, length - width, length, axis=dim)
        first = lax.slice_in_dim(shard, 0, width, axis=dim)
        before = lax.ppermute(last, axis, up)
        after = lax.ppermute(first, axis, down)
        shard = jnp.concatenate([before, shard, after], axis=dim)
    return shard


def green_stack(green_table):
    real_part = green_table[:, 0]
    imag_part = green_table[:, 1]
    upper_half = jnp.concatenate([real_part, -imag_part], axis=2)
    lower_half = jnp.concatenate([imag_part, real_part], axis=2)
    return jnp.concatenate([upper_half, lower_half], axis=1)


def to_blocks(grid_data, block_side):
    channels, extent_x, extent_y = grid_data.shape
    reshaped = grid_data.reshape(
        channels, extent_x // block_side, block_side, extent_y // block_side, block_side
    )
    reshaped = reshaped.transpose(1, 3, 0, 2, 4)
    return reshaped.reshape(
        extent_x // block_side * (extent_y // block_side), channels * block_side * block_side
    )


def from_blocks(blocks, extent_x, extent_y, block_side):
    reshaped = blocks.reshape(
        extent_x // block_side, extent_y // block_side, 2, block_side, block_side
    )
    return reshaped.transpose(2, 0, 3, 1, 4).reshape(2, extent_x, extent_y)


def grouped_adjoint(
    ext_blocks, sources, targets, run_ends, lower_slot, upper_slot, stacks, block_count
):
    piece_rows = min(768, sources.shape[0])
    filler = jnp.zeros((piece_rows,), jnp.int32)
    padded_src = jnp.concatenate([sources, filler])
    padded_dst = jnp.concatenate([targets, filler])
    run_starts = jnp.concatenate([jnp.zeros((1,), jnp.int32), run_ends[:-1]])
    offsets = jnp.arange(piece_rows, dtype=jnp.int32)
    summed = jnp.zeros((block_count, stacks.shape[2]), jnp.float32)
    for group_index in range(stacks.shape[0]):
        first_row = jnp.clip(run_starts[group_index], lower_slot, upper_slot)
        stop_row = jnp.clip(run_ends[group_index], lower_slot, upper_slot)
        piece_count = (stop_row - first_row + piece_rows - 1) // piece_rows

        def one_piece(
            piece_index, running, group_index=group_index, first_row=first_row, stop_row=stop_row
        ):
            start_row = first_row + piece_index * piece_rows
            piece_src = lax.dynamic_slice_in_dim(padded_src, start_row, piece_rows)
            piece_dst = lax.dynamic_slice_in_dim(padded_dst, start_row, piece_rows)
            live_rows = start_row + offsets < stop_row
            gathered = jnp.where(
                live_rows[:, None], ext_blocks[piece_dst], jnp.zeros((), ext_blocks.dtype)
            )
            product = jnp.dot(gathered, stacks[group_index], preferred_element_type=jnp.float32)
            return running.at[piece_src].add(product)

        summed = lax.fori_loop(0, piece_count, one_piece, summed)
    return summed


def cell_pass(pillar_band, near_band, w_in, b_in, w_out):
    band_x = near_band.shape[1]
    band_y = near_band.shape[2]
    feats = jnp.stack(
        [
            pillar_band[1 + shift_x : 1 + shift_x + band_x, 1 + shift_y : 1 + shift_y + band_y]
            for shift_x in (-1, 0, 1)
            for shift_y in (-1, 0, 1)
        ]
    )
    hidden = jnp.tanh(
        jnp.einsum("ks,sij->kij", w_in, feats, precision=highest) + b_in[:, None, None]
    )
    pulled = jnp.einsum("ck,cij->kij", w_out, near_band, precision=highest)
    slope_hidden = pulled * (1.0 - hidden * hidden)
    slopes = jnp.einsum("ks,kij->sij", w_in, slope_hidden, precision=highest)
    return (feats, hidden, slope_hidden, slopes)


def region_sums(feats, hidden, slope_hidden, near_band):
    grad_in = jnp.einsum("kij,sij->ks", slope_hidden, feats, precision=highest)
    grad_bias = jnp.sum(slope_hidden, axis=(1, 2))
    grad_out = jnp.einsum("cij,kij->ck", near_band, hidden, precision=highest)
    return (grad_in, grad_bias, grad_out)


def combine_slopes(slopes):
    band_x = slopes.shape[1] - 2
    band_y = slopes.shape[2] - 2
    summed = jnp.zeros((band_x, band_y), jnp.float32)
    for shift_x in (-1, 0, 1):
        for shift_y in (-1, 0, 1):
            index = 3 * (shift_x + 1) + (shift_y + 1)
            summed = (
                summed
                + slopes[
                    index, 1 - shift_x : 1 - shift_x + band_x, 1 - shift_y : 1 - shift_y + band_y
                ]
            )
    return summed


def add_sums(first_sums, second_sums):
    return (
        first_sums[0] + second_sums[0],
        first_sums[1] + second_sums[1],
        first_sums[2] + second_sums[2],
    )


def local(far_adjoint, pillar, green_blocks, pair_src, pair_dst, group_end, w_in, b_in, w_out):
    channels, rows_x, cols_y = far_adjoint.shape
    rim_cells = CONE * BLK
    extended = with_halo(far_adjoint, (("tx", 1), ("ty", 2)), rim_cells)
    ext_blocks = to_blocks(extended, BLK)
    stacks = green_stack(green_blocks)
    block_count = rows_x // BLK * (cols_y // BLK)
    sources = pair_src.reshape(-1)
    targets = pair_dst.reshape(-1)
    run_ends = group_end.reshape(-1)
    slot_total = sources.shape[0]
    near_blocks = grouped_adjoint(
        ext_blocks, sources, targets, run_ends, 0, slot_total, stacks, block_count
    )
    near = from_blocks(near_blocks, rows_x, cols_y, BLK)
    band_rows = min(32, rows_x)
    band_total = rows_x // band_rows
    hidden_units = w_in.shape[0]
    zero_sums = (
        jnp.zeros((hidden_units, 9), jnp.float32),
        jnp.zeros((hidden_units,), jnp.float32),
        jnp.zeros((2, hidden_units), jnp.float32),
    )
    pillar_ext = with_halo(pillar, (("tx", 0), ("ty", 1)), 1)

    def send_band(band_index, carried):
        slope_field, running_sums = carried
        start_x = band_index * band_rows
        pillar_band = lax.dynamic_slice(pillar_ext, (start_x, 0), (band_rows + 2, cols_y + 2))
        near_band = lax.dynamic_slice(near, (0, start_x, 0), (2, band_rows, cols_y))
        feats, hidden, slope_hidden, slopes = cell_pass(pillar_band, near_band, w_in, b_in, w_out)
        band_sums = region_sums(feats, hidden, slope_hidden, near_band)
        slope_field = lax.dynamic_update_slice(slope_field, slopes, (0, start_x, 0))
        return (slope_field, add_sums(running_sums, band_sums))

    slope_field, local_sums = lax.fori_loop(
        0, band_total, send_band, (jnp.zeros((9, rows_x, cols_y), jnp.float32), zero_sums)
    )
    slope_ext = with_halo(slope_field, (("tx", 1), ("ty", 2)), 1)
    grad_pillar = combine_slopes(slope_ext)
    total_sums = lax.psum((local_sums[0], local_sums[1], local_sums[2]), ("tx", "ty"))
    scale = float(rows_x * cols_y * lax.axis_size("tx") * lax.axis_size("ty")) ** (-0.5)
    return (grad_pillar, total_sums[0] * scale, total_sums[1] * scale, total_sums[2] * scale)


def solution(mesh):
    return jax.shard_map(
        local,
        mesh=mesh,
        in_specs=(
            P(None, "tx", "ty"),
            P("tx", "ty"),
            P(),
            P("tx", "ty", None),
            P("tx", "ty", None),
            P("tx", "ty", None),
            P(),
            P(),
            P(),
        ),
        out_specs=(P("tx", "ty"), P(), P(), P()),
        check_vma=False,
    )
```

profile of v0, /device:TPU:1, one launch (start us, length us, event | category | flops | bytes accessed | tf_op | source)
XLA Modules:
  0.0 1348.3 jit_solution(9088822581531562827)
XLA Ops:
  64.7 20.1 %reshape.129 = bf16[2,56,16,56,16]{4,3,2,1,0:T(8,128)(2,1)} reshape(bf16[2,896,896]{2,1,0:T(8,128)(2,1)S(1)} %copy.103) | data formatting | bytes 6422528 | tf_op jit(solution)/shard_map/reshape | solution.py:36
  84.8 24.7 %copy.104 = bf16[56,56,2,16,16]{1,0,4,3,2:T(8,128)(2,1)} copy(bf16[56,56,2,16,16]{4,1,3,0,2:T(8,128)(2,1)} %bitcast.152) | data formatting | bytes 6422528 | tf_op jit(solution)/shard_map/transpose | solution.py:39
  109.5 9.1 reshape.130
  122.3 16.0 %while.109 = (s32[]{:T(128)}, f32[1024,512]{1,0:T(8,128)S(1)}, s32[]{:T(128)}, s32[25344]{0:T(1024)S(1)}, s32[]{:T(128)}, /*index=5*/s32[25344]{0:T(1024)S(1)}, ...) while((s32[]{:T(128)}, f32[1024,512]{1,0:T(8,128)S(1)}, ...), condition=%wide.region_2.3_spmd.clone, body=%wide.region_0.2_spmd.clone.sunk | while | flops 403446784 | bytes 9202351 | solution.py:80
  130.3 8.0 scatter_fusion
  138.3 32.3 %while.110 = (s32[]{:T(128)}, f32[1024,512]{1,0:T(8,128)S(1)}, s32[]{:T(128)}, s32[]{:T(128)}, s32[25344]{0:T(1024)S(1)}, /*index=5*/s32[]{:T(128)}, s32[25344]{...) while((s32[]{:T(128)}, f32[1024,512]{1,0:T(8,128)S(1)}, ...), condition=%wide.region_5.6_spmd.clone, body=%wide.region_3.5_spmd.clone.sunk | while | flops 403446784 | bytes 9202371 | solution.py:80
  146.6 8.0 scatter_fusion.1
  162.6 8.0 scatter_fusion.1
  170.6 16.0 %while.111 = (s32[]{:T(128)}, f32[1024,512]{1,0:T(8,128)S(1)}, s32[]{:T(128)}, s32[]{:T(128)}, s32[25344]{0:T(1024)S(1)}, /*index=5*/s32[]{:T(128)}, s32[25344]{...) while((s32[]{:T(128)}, f32[1024,512]{1,0:T(8,128)S(1)}, ...), condition=%wide.region_8.9_spmd.clone, body=%wide.region_6.8_spmd.clone.sunk | while | flops 403446784 | bytes 9202371 | solution.py:80
  178.6 8.0 scatter_fusion.2
  186.7 16.4 %while.112 = (s32[]{:T(128)}, f32[1024,512]{1,0:T(8,128)S(1)}, s32[]{:T(128)}, s32[]{:T(128)}, s32[25344]{0:T(1024)S(1)}, /*index=5*/s32[]{:T(128)}, s32[25344]{...) while((s32[]{:T(128)}, f32[1024,512]{1,0:T(8,128)S(1)}, ...), condition=%wide.region_11.12_spmd.clone, body=%wide.region_9.11_spmd.clone.sunk | while | flops 403446784 | bytes 9202371 | solution.py:80
  195.1 8.0 scatter_fusion.3
  203.1 16.0 %while.113 = (s32[]{:T(128)}, f32[1024,512]{1,0:T(8,128)S(1)}, s32[]{:T(128)}, s32[]{:T(128)}, s32[25344]{0:T(1024)S(1)}, /*index=5*/s32[]{:T(128)}, s32[25344]{...) while((s32[]{:T(128)}, f32[1024,512]{1,0:T(8,128)S(1)}, ...), condition=%wide.region_14.15_spmd.clone, body=%wide.region_12.14_spmd.clone.sunk | while | flops 403446784 | bytes 9202371 | solution.py:80
  211.1 8.0 scatter_fusion.4
  219.2 32.2 %while.114 = (s32[]{:T(128)}, f32[1024,512]{1,0:T(8,128)S(1)}, s32[]{:T(128)}, s32[]{:T(128)}, s32[25344]{0:T(1024)S(1)}, /*index=5*/s32[]{:T(128)}, s32[25344]{...) while((s32[]{:T(128)}, f32[1024,512]{1,0:T(8,128)S(1)}, ...), condition=%wide.region_17.18_spmd.clone, body=%wide.region_15.17_spmd.clone.sunk | while | flops 403446784 | bytes 9202371 | solution.py:80
  227.4 8.0 scatter_fusion.5
  243.4 8.0 scatter_fusion.5
  251.4 32.1 %while.115 = (s32[]{:T(128)}, f32[1024,512]{1,0:T(8,128)S(1)}, s32[]{:T(128)}, s32[]{:T(128)}, s32[25344]{0:T(1024)S(1)}, /*index=5*/s32[]{:T(128)}, s32[25344]{...) while((s32[]{:T(128)}, f32[1024,512]{1,0:T(8,128)S(1)}, ...), condition=%wide.region_20.21_spmd.clone, body=%wide.region_18.20_spmd.clone.sunk | while | flops 403446784 | bytes 9202371 | solution.py:80
  259.4 8.0 scatter_fusion.6
  275.5 8.0 scatter_fusion.6
  283.5 16.3 %while.116 = (s32[]{:T(128)}, f32[1024,512]{1,0:T(8,128)S(1)}, s32[]{:T(128)}, s32[]{:T(128)}, s32[25344]{0:T(1024)S(1)}, /*index=5*/s32[]{:T(128)}, s32[25344]{...) while((s32[]{:T(128)}, f32[1024,512]{1,0:T(8,128)S(1)}, ...), condition=%wide.region_23.24_spmd.clone, body=%wide.region_21.23_spmd.clone.sunk | while | flops 403446784 | bytes 9202371 | solution.py:80
  291.7 8.0 scatter_fusion.7
  301.6 6.6 reshape.131
  308.2 12.5 copy.129
  320.7 13.8 %reshape.317 = f32[2,512,512]{2,0,1:T(2,128)} reshape(f32[2,32,16,32,16]{4,3,0,2,1:T(8,128)} %copy.129) | data formatting | bytes 4194304
  334.5 7.9 broadcast_in_dim.150
  342.4 490.7 %while.117 = (s32[]{:T(128)}, f32[9,512,512]{2,0,1:T(8,128)}, f32[64,9]{0,1:T(8,128)S(1)}, f32[64]{0:T(128)S(1)}, f32[2,64]{1,0:T(2,128)S(1)}, /*index=5*/f32[2,...) while((s32[]{:T(128)}, f32[9,512,512]{2,0,1:T(8,128)}, ...), condition=%wide.region_26.27_spmd.clone, body=%wide.region_24.26_spmd.clone.sunk | while | flops 396363200 | bytes 64762228 | solution.py:169
  351.2 7.0 fusion.207
  382.0 7.0 fusion.207
  394.4 5.3 fusion.209
  412.4 7.0 fusion.207
  443.1 7.0 fusion.207
  455.5 5.3 fusion.209
  473.5 7.0 fusion.207
  504.2 7.0 fusion.207
  534.8 7.0 fusion.207
  565.2 7.0 fusion.207
  596.0 7.0 fusion.207
  626.8 7.0 fusion.207
  657.5 7.0 fusion.207
  688.2 7.0 fusion.207
  718.9 7.0 fusion.207
  749.6 7.0 fusion.207
  780.1 7.0 fusion.207
  810.8 7.0 fusion.207
  833.1 462.3 %all-reduce.2 = (f32[64,9]{0,1:T(8,128)S(1)}, f32[64]{0:T(128)S(1)}, f32[2,64]{1,0:T(2,128)S(1)}) all-reduce(f32[64,9]{0,1:T(8,128)S(1)} %get-tuple-element.637, f32[64]{0:T(128)S(1)} %get-tuple-element.638, f32[2,64]{1,0:T(2,128)S(1)} %get-tuple-element.639), channel_id=1, replica_groups=mesh['tx'=8,'ty'=16] {'tx','ty'}, use_global_device_ids=true, to_apply=%region_27.28 | all-reduce | flops 768 | bytes 6144 | tf_op jit(solution)/shard_map/psum | solution.py:174
  1296.0 14.9 %copy.118 = f32[9,512,512]{2,1,0:T(8,128)} copy(f32[9,512,512]{2,0,1:T(8,128)} %get-tuple-element.636) | data formatting | bytes 18874368 | tf_op jit(solution)/shard_map/while | solution.py:169
  1315.9 15.6 %copy.121 = f32[9,512,512]{1,2,0:T(8,128)} copy(f32[9,512,512]{2,0,1:T(8,128)} %get-tuple-element.636) | data formatting | bytes 18874368 | tf_op jit(solution)/shard_map/while | solution.py:169
  (460 shorter events, 538.4 us)
Async XLA Ops:
  0.6 13.2 copy-start.4
  2.6 14.5 %collective-permute-start = (bf16[2,192,512]{1,2,0:T(8,128)(2,1)S(1)}, bf16[2,192,512]{1,2,0:T(8,128)(2,1)S(1)}, u32[]{:S(2)}, u32[]{:S(2)}) collective-permute-start(bf16[2,192,512]{1,2,0:T(8,128)(2,1)S(1)} %get-tuple-element.1294), channel_id=1, source_target_pairs={{0,16},{16,32},{32,48},{48,64},{64,80},{80,96},{96,112},{1,17},{17... | collective-permute-start | bytes 1179656 | tf_op jit(solution)/shard_map/ppermute | solution.py:20
  6.5 14.4 %collective-permute-start.1 = (bf16[2,192,512]{1,2,0:T(8,128)(2,1)S(1)}, bf16[2,192,512]{1,2,0:T(8,128)(2,1)S(1)}, u32[]{:S(2)}, u32[]{:S(2)}) collective-permute-start(bf16[2,192,512]{1,2,0:T(8,128)(2,1)S(1)} %get-tuple-element.1295), channel_id=1, source_target_pairs={{16,0},{32,16},{48,32},{64,48},{80,64},{96,80},{112,96},{17,1},{33... | collective-permute-start | bytes 1179656 | tf_op jit(solution)/shard_map/ppermute | solution.py:21
  8.6 32.2 %collective-permute-start.4 = (f32[1,512]{1,0:T(1,128)S(1)}, f32[1,512]{1,0:T(1,128)S(1)}, u32[]{:S(2)}, u32[]{:S(2)}) collective-permute-start(f32[1,512]{1,0:T(1,128)S(1)} %get-tuple-element.1292), channel_id=1, source_target_pairs={{0,16},{16,32},{32,48},{48,64},{64,80},{80,96},{96,112},{1,17},{17... | collective-permute-start | bytes 6152 | tf_op jit(solution)/shard_map/ppermute | solution.py:20
  12.6 28.2 %collective-permute-start.5 = (f32[1,512]{1,0:T(1,128)S(1)}, f32[1,512]{1,0:T(1,128)S(1)}, u32[]{:S(2)}, u32[]{:S(2)}) collective-permute-start(f32[1,512]{1,0:T(1,128)S(1)} %get-tuple-element.1293), channel_id=1, source_target_pairs={{16,0},{32,16},{48,32},{64,48},{80,64},{96,80},{112,96},{17,1},{33... | collective-permute-start | bytes 6152 | tf_op jit(solution)/shard_map/ppermute | solution.py:21
  16.4 13.6 %copy-start.16 = (s32[1,1,8]{2,1,0:T(1,128)S(1)}, s32[1,1,8]{2,1,0:T(1,128)}, u32[]{:S(2)}) copy-start(s32[1,1,8]{2,1,0:T(1,128)} %param.32) | copy-start | bytes 100
  16.4 17.5 %copy-start.6 = (bf16[8,256,256]{2,1,0:T(8,128)(2,1)S(1)}, bf16[8,256,256]{2,1,0:T(8,128)(2,1)}, u32[]{:S(2)}) copy-start(bf16[8,256,256]{2,1,0:T(8,128)(2,1)} %fusion.107) | copy-start | bytes 3145732
  17.1 3.8 copy-start.7
  22.7 33.3 %collective-permute-start.2 = (bf16[2,896,192]{1,2,0:T(8,128)(2,1)}, bf16[2,896,192]{1,2,0:T(8,128)(2,1)}, u32[]{:S(2)}, u32[]{:S(2)}) collective-permute-start(bf16[2,896,192]{1,2,0:T(8,128)(2,1)} %get-tuple-element.1288), channel_id=1, source_target_pairs={{0,1},{1,2},{2,3},{3,4},{4,5},{5,6},{6,7},{7,8},{8,9},{9,10},{10,1... | collective-permute-start | bytes 2064392 | tf_op jit(solution)/shard_map/ppermute | solution.py:20
  28.0 28.0 %collective-permute-start.3 = (bf16[2,896,192]{1,2,0:T(8,128)(2,1)}, bf16[2,896,192]{1,2,0:T(8,128)(2,1)}, u32[]{:S(2)}, u32[]{:S(2)}) collective-permute-start(bf16[2,896,192]{1,2,0:T(8,128)(2,1)} %get-tuple-element.1289), channel_id=1, source_target_pairs={{1,0},{2,1},{3,2},{4,3},{5,4},{6,5},{7,6},{8,7},{9,8},{10,9},{11,1... | collective-permute-start | bytes 2064392 | tf_op jit(solution)/shard_map/ppermute | solution.py:21
  33.8 6.0 copy-start.13
  33.8 6.9 copy-start.5
  40.8 15.2 %copy-start.8 = (bf16[2,192,512]{1,2,0:T(8,128)(2,1)S(1)}, bf16[2,192,512]{1,2,0:T(8,128)(2,1)}, u32[]{:S(2)}) copy-start(bf16[2,192,512]{1,2,0:T(8,128)(2,1)} %copy-done.7) | copy-start | bytes 1179652
  40.8 15.2 %copy-start.10 = (bf16[2,192,512]{1,2,0:T(8,128)(2,1)S(1)}, bf16[2,192,512]{1,2,0:T(8,128)(2,1)}, u32[]{:S(2)}) copy-start(bf16[2,192,512]{1,2,0:T(8,128)(2,1)} %copy-done.9) | copy-start | bytes 1179652
  41.7 7.3 collective-permute-start.6
  45.3 8.1 collective-permute-start.7
  334.5 7.9 copy-start.11
  334.5 7.9 copy-start.12
  334.5 7.9 copy-start.14
  334.5 7.9 copy-start.15
  334.5 7.9 copy-start.17
  334.5 7.9 copy-start.18
  358.2 2.0 copy-start.1
  363.6 5.4 copy-start
  389.1 2.0 copy-start.1
  394.4 5.4 copy-start
  419.5 2.0 copy-start.1
  424.8 5.4 copy-start
  450.2 2.0 copy-start.1
  455.5 5.4 copy-start
  485.9 5.4 copy-start
  516.6 5.4 copy-start
  547.2 5.4 copy-start
  577.7 5.4 copy-start
  608.5 5.4 copy-start
  639.2 5.4 copy-start
  669.9 5.4 copy-start
  700.6 5.4 copy-start
  731.3 5.4 copy-start
  761.9 5.4 copy-start
  792.5 5.4 copy-start
  823.2 5.4 copy-start
  1311.9 19.6 %collective-permute-start.8 = (f32[9,1,512]{2,1,0:T(1,128)S(1)}, f32[9,1,512]{2,1,0:T(1,128)S(1)}, u32[]{:S(2)}, u32[]{:S(2)}) collective-permute-start(f32[9,1,512]{2,1,0:T(1,128)S(1)} %get-tuple-element.1284), channel_id=1, source_target_pairs={{0,16},{16,32},{32,48},{48,64},{64,80},{80,96},{96,112},{1,17},{17... | collective-permute-start | bytes 55304 | tf_op jit(solution)/shard_map/ppermute | solution.py:20
  1314.0 18.2 %collective-permute-start.9 = (f32[9,1,512]{2,1,0:T(1,128)S(1)}, f32[9,1,512]{2,1,0:T(1,128)S(1)}, u32[]{:S(2)}, u32[]{:S(2)}) collective-permute-start(f32[9,1,512]{2,1,0:T(1,128)S(1)} %get-tuple-element.1285), channel_id=1, source_target_pairs={{16,0},{32,16},{48,32},{64,48},{80,64},{96,80},{112,96},{17,1},{33... | collective-permute-start | bytes 55304 | tf_op jit(solution)/shard_map/ppermute | solution.py:21
  1334.4 8.2 copy-start.2
  1334.4 8.2 copy-start.3
  1335.7 6.5 collective-permute-start.10
  1338.7 3.9 collective-permute-start.11
  (13 other events, 26.2 us)
where the time goes:
time: 1370 us; the launch traced here: 1350 us
  blocking collectives  462 us (34%)
  matrix products  434 us (32%)
  local copies, waits for them, and re-layouts  287 us (21%)
  other arithmetic  111 us (8%)
  starting transfers between devices  32.7 us (2%)
    psum x1, blocking collectives, local(): lax.psum((local_sums[0], local_sums[1], local_sums[2]), ('tx', 'ty'))  462 us
    dot_general x16, matrix products, cell_pass(): pulled = jnp.einsum('ck,cij->kij', w_out, near_band, precision=highest)  113 us
    scatter-add x11, other arithmetic, one_piece(): return running.at[piece_src].add(product)  88.3 us
    dot_general x16, matrix products, region_sums(): grad_in = jnp.einsum('kij,sij->ks', slope_hidden, feats, precision=highest)  85.2 us
    dot_general x16, matrix products, cell_pass(): jnp.einsum('ks,sij->kij', w_in, feats, precision=highest)  81.4 us
    dot_general x16, matrix products, region_sums(): grad_out = jnp.einsum('cij,kij->ck', near_band, hidden, precision=highest)  70.7 us
    gather x11, local copies, waits for them, and re-layouts, one_piece(): ext_blocks[piece_dst]  55.3 us
    dot_general x16, matrix products, cell_pass(): slopes = jnp.einsum('ks,kij->sij', w_in, slope_hidden, precision=highest)  52.9 us
  transfers between devices with their start and end apart: 12, of which 5 were waited for; matrix products, arithmetic and copies ran while one was open for 2% of the time, Pallas kernels for 0%

commit v1 on v0

v1 whole, which is shorter than its diff:
```python
import functools

import jax
import jax.numpy as jnp
from jax import lax
from jax.experimental import pallas as pl
from jax.experimental.pallas import tpu as pltpu
from jax.sharding import PartitionSpec as P

BLK = 16
CONE = 12
SIDE = 512
NB = SIDE // BLK
EXT = NB + 2 * CONE
GROUPS = 8
CHUNK = 512
UNROLL = 32
HIDDEN = 64
PADROWS = 16
SROWS = 24
VMEM_BYTES = 60 * 1024 * 1024

f32 = jnp.float32
bf16 = jnp.bfloat16


def swap_pieces(v):
    sub = lax.broadcasted_iota(jnp.int32, (8, 128), 0)
    lane = lax.broadcasted_iota(jnp.int32, (8, 128), 1) // 16
    for d in (1, 2, 4):
        low_s = (sub & d) == 0
        low_l = (lane & d) == 0
        up = pltpu.roll(pltpu.roll(v, 8 - d, 0), 16 * d, 1)
        if d == 4:
            down = up
        else:
            down = pltpu.roll(pltpu.roll(v, d, 0), 128 - 16 * d, 1)
        v = jnp.where(low_s == low_l, v, jnp.where(low_s, up, down))
    return v


def block_kernel(far_ref, out_ref, flat):
    def row(r, carry):
        for c in range(2):
            strip = far_ref[c, pl.ds(pl.multiple_of(r * BLK, BLK), BLK), :].astype(f32)
            for xh in range(2):
                for t in range(SIDE // 128):
                    v = swap_pieces(strip[8 * xh : 8 * xh + 8, 128 * t : 128 * t + 128])
                    flat[pl.ds(32 * t + 2 * c + xh, 8, stride=4), :] = v
        out_ref[pl.ds(pl.multiple_of(r * 128, 128), 128), :] = flat[...].astype(bf16)
        return carry

    lax.fori_loop(0, NB, row, 0)


def to_block_table(far):
    return pl.pallas_call(
        block_kernel,
        out_shape=jax.ShapeDtypeStruct((NB * NB * 4, 128), bf16),
        in_specs=[pl.BlockSpec(memory_space=pltpu.VMEM)],
        out_specs=pl.BlockSpec(memory_space=pltpu.VMEM),
        scratch_shapes=[pltpu.VMEM((128, 128), f32)],
        compiler_params=pltpu.CompilerParams(vmem_limit_bytes=VMEM_BYTES),
        name="to_blocks",
    )(far)


def sparse_kernel(
    dst_ref, ends_ref, src_ref, ext_ref, green_ref, near_ref, table, rows, rows16, seg, acc
):
    def widen(i, carry):
        at = pl.ds(pl.multiple_of(i * 128, 128), 128)
        table[at, :] = ext_ref[at, :].astype(f32)
        return carry

    lax.fori_loop(0, EXT * EXT * 4 // 128, widen, 0)
    acc[...] = jnp.zeros_like(acc)

    def group(k, carry):
        start = jnp.where(k == 0, 0, ends_ref[jnp.maximum(k - 1, 0)])
        stop = ends_ref[k]
        seg[...] = jnp.zeros_like(seg)

        def chunk(c, inner):
            base = c * CHUNK

            def gather(i, deep):
                for j in range(UNROLL):
                    q = i * UNROLL + j
                    d = pl.multiple_of(dst_ref[base + q], 4)
                    rows[pl.ds(pl.multiple_of(q * 4, 4), 4), :] = table[pl.ds(d, 4), :]
                return deep

            lax.fori_loop(0, CHUNK // UNROLL, gather, 0)
            for j in range(4):
                rows16[:, 128 * j : 128 * j + 128] = rows[
                    pl.ds(j, CHUNK, stride=4), :
                ].astype(bf16)
            slot = base + lax.broadcasted_iota(jnp.int32, (1, CHUNK), 1)
            live = (slot >= start) & (slot < stop)
            source = jnp.where(live, src_ref[c], -1)
            for m in range(4):
                ids = lax.broadcasted_iota(jnp.int32, (256, CHUNK), 0) + 256 * m
                hot = jnp.where(ids == source, 1.0, 0.0).astype(bf16)
                seg[256 * m : 256 * m + 256, :] += jnp.dot(
                    hot, rows16[...], preferred_element_type=f32
                )
            return inner

        lax.fori_loop(start // CHUNK, (stop + CHUNK - 1) // CHUNK, chunk, 0)

        def apply(m, inner):
            at = pl.ds(pl.multiple_of(m * 256, 256), 256)
            value = seg[at, :]
            high = value.astype(bf16)
            low = (value - high.astype(f32)).astype(bf16)
            acc[at, :] += jnp.dot(high, green_ref[k], preferred_element_type=f32) + jnp.dot(
                low, green_ref[k], preferred_element_type=f32
            )
            return inner

        lax.fori_loop(0, 4, apply, 0)
        return carry

    lax.fori_loop(0, GROUPS, group, 0)

    def lay(r, carry):
        for t in range(SIDE // 128):
            for c in range(2):
                for xh in range(2):
                    j = 2 * c + xh
                    v = acc[
                        pl.ds(pl.multiple_of(r * 32 + 8 * t, 8), 8), 128 * j : 128 * j + 128
                    ]
                    near_ref[
                        c,
                        pl.ds(pl.multiple_of(r * 16 + 8 * xh + PADROWS, 8), 8),
                        128 * t : 128 * t + 128,
                    ] = swap_pieces(v)
        return carry

    lax.fori_loop(0, NB, lay, 0)
    for c in range(2):
        near_ref[c, 0:PADROWS, :] = jnp.zeros((PADROWS, SIDE), f32)
        near_ref[c, PADROWS + SIDE : 2 * PADROWS + SIDE, :] = jnp.zeros((PADROWS, SIDE), f32)


def sparse_near(targets, ends, sources, ext, stacks):
    slots = targets.shape[0]
    return pl.pallas_call(
        sparse_kernel,
        out_shape=jax.ShapeDtypeStruct((2, SIDE + 2 * PADROWS, SIDE), f32),
        in_specs=[
            pl.BlockSpec(memory_space=pltpu.SMEM),
            pl.BlockSpec(memory_space=pltpu.SMEM),
            pl.BlockSpec(memory_space=pltpu.VMEM),
            pl.BlockSpec(memory_space=pltpu.VMEM),
            pl.BlockSpec(memory_space=pltpu.VMEM),
        ],
        out_specs=pl.BlockSpec(memory_space=pltpu.VMEM),
        scratch_shapes=[
            pltpu.VMEM((EXT * EXT * 4, 128), f32),
            pltpu.VMEM((CHUNK * 4, 128), f32),
            pltpu.VMEM((CHUNK, 512), bf16),
            pltpu.VMEM((NB * NB, 512), f32),
            pltpu.VMEM((NB * NB, 512), f32),
        ],
        compiler_params=pltpu.CompilerParams(vmem_limit_bytes=VMEM_BYTES),
        name="sparse_near",
    )(targets * 4, ends, sources.reshape(slots // CHUNK, 1, CHUNK), ext, stacks)


def split2(value):
    high = value.astype(bf16).astype(f32)
    return high, value - high


def put(ref, start, stride, value):
    for t in range(SIDE // 128):
        ref[t, pl.ds(start, 8, stride=stride), :] = value[:, 128 * t : 128 * t + 128]


def take(ref, start, stride):
    tiles = [ref[t, pl.ds(start, 8, stride=stride), :] for t in range(SIDE // 128)]
    return jnp.concatenate(tiles, 1)


def cell_kernel(
    p3_ref, near_ref, w1_ref, v_ref, grad_ref, west_ref, east_ref, sums_ref, q32, qs, gs, ps, total
):
    width = SIDE

    def build(i, carry):
        r0 = pl.multiple_of(i * 8, 8)
        for b in range(3):
            x = p3_ref[b, pl.ds(r0, 8), :]
            x1, rest = split2(x)
            x2, x3 = split2(rest)
            for n, piece in enumerate((x1, x1, x2, x2, x3)):
                put(q32, b * 5 + n, 16, piece)
        put(q32, 15, 16, jnp.ones((8, width), f32))
        for t in range(4):
            qs[pl.ds(r0, 8), :, 128 * t : 128 * t + 128] = (
                q32[t].astype(bf16).reshape(8, 16, 128)
            )
        return carry

    lax.fori_loop(0, (SIDE + 8) // 8, build, 0)
    total[...] = jnp.zeros_like(total)
    gs[...] = jnp.zeros_like(gs)
    zero_rows = jnp.zeros((PADROWS * SROWS, 128), f32)
    for t in range(4):
        ps[t, 0 : PADROWS * SROWS, :] = zero_rows
        ps[t, (PADROWS + SIDE) * SROWS : (2 * PADROWS + SIDE) * SROWS, :] = zero_rows

    def strip(i, carry):
        r0 = pl.multiple_of(i * 8, 8)
        n = [near_ref[c, pl.ds(pl.multiple_of(r0 + PADROWS, 8), 8), :] for c in range(2)]
        deep = [p3_ref[b, pl.ds(r0, 16), :] for b in range(3)]
        for a in range(3):
            for b in range(3):
                feat = deep[b][a : a + 8]
                for c in range(2):
                    put(gs, 10 * c + 3 * a + b, SROWS, n[c] * feat)
        for c in range(2):
            put(gs, 10 * c + 9, SROWS, n[c])
        for half in range(2):
            left, right = [], []
            for j in range(4 * half, 4 * half + 4):
                feats = qs[pl.ds(r0 + j, 3)].reshape(48, width)
                h = jnp.tanh(jnp.dot(w1_ref[...], feats, preferred_element_type=f32))
                u = 1.0 - h * h
                u1 = u.astype(bf16)
                u2 = (u - u1.astype(f32)).astype(bf16)
                h1 = h.astype(bf16)
                h2 = (h - h1.astype(f32)).astype(bf16)
                slope = jnp.dot(
                    v_ref[...], jnp.concatenate([u1, u2, u1], 0), preferred_element_type=f32
                )
                at = pl.ds(pl.multiple_of((r0 + PADROWS + j) * SROWS, 8), SROWS)
                for t in range(4):
                    ps[t, at, :] = slope[:SROWS, 128 * t : 128 * t + 128]
                g = jnp.concatenate(
                    [gs[t, SROWS * j : SROWS * j + SROWS, :] for t in range(4)], 1
                )
                g1, g2 = split2(g)
                left.append(jnp.concatenate([u1, u2, h1, h2], 0))
                right.append(jnp.concatenate([g1, g2], 0).astype(bf16))
            total[...] += lax.dot_general(
                jnp.concatenate(left, 1),
                jnp.concatenate(right, 1),
                (((1,), (1,)), ((), ())),
                preferred_element_type=f32,
            )
        return carry

    lax.fori_loop(0, SIDE // 8, strip, 0)
    sums_ref[...] = total[...]

    lane = lax.broadcasted_iota(jnp.int32, (8, width), 1)

    def combine(i, carry):
        parts = []
        deep = [near_ref[c, pl.ds(pl.multiple_of(i * 8, 8), 24), :] for c in range(2)]
        for b in range(3):
            acc = None
            for a in range(3):
                x0 = i * 8 + 9 - a
                for c in range(2):
                    term = deep[c][9 - a : 17 - a] * take(
                        ps, x0 * SROWS + 9 * c + 3 * a + b, SROWS
                    )
                    acc = term if acc is None else acc + term
            parts.append(acc)
        low = jnp.where(lane == width - 1, 0.0, pltpu.roll(parts[0], width - 1, 1))
        high = jnp.where(lane == 0, 0.0, pltpu.roll(parts[2], 1, 1))
        at = pl.ds(pl.multiple_of(i * 8, 8), 8)
        grad_ref[at, :] = parts[1] + low + high
        west_ref[at, :] = parts[0][:, 0:128]
        east_ref[at, :] = parts[2][:, width - 128 : width]
        return carry

    lax.fori_loop(0, SIDE // 8 + 2, combine, 0)


def cell_model(p3, near, first, back):
    rows = SIDE + 16
    return pl.pallas_call(
        cell_kernel,
        out_shape=[
            jax.ShapeDtypeStruct((rows, SIDE), f32),
            jax.ShapeDtypeStruct((rows, 128), f32),
            jax.ShapeDtypeStruct((rows, 128), f32),
            jax.ShapeDtypeStruct((4 * HIDDEN, 2 * SROWS), f32),
        ],
        in_specs=[pl.BlockSpec(memory_space=pltpu.VMEM)] * 4,
        out_specs=[pl.BlockSpec(memory_space=pltpu.VMEM)] * 4,
        scratch_shapes=[
            pltpu.VMEM((4, 128, 128), f32),
            pltpu.VMEM((SIDE + 8, 16, SIDE), bf16),
            pltpu.VMEM((4, 8 * SROWS, 128), f32),
            pltpu.VMEM((4, (SIDE + 2 * PADROWS) * SROWS, 128), f32),
            pltpu.VMEM((4 * HIDDEN, 2 * SROWS), f32),
        ],
        compiler_params=pltpu.CompilerParams(vmem_limit_bytes=VMEM_BYTES),
        name="cell_model",
    )(p3, near, first, back)


def neighbours(axis):
    count = lax.axis_size(axis)
    up = [(i, i + 1) for i in range(count - 1)]
    return up, [(j, i) for i, j in up]


def with_halo(shard, sides):
    for axis, dim, size in sides:
        up, down = neighbours(axis)
        length = shard.shape[dim]
        before = lax.ppermute(
            lax.slice_in_dim(shard, length - size, length, axis=dim), axis, up
        )
        after = lax.ppermute(lax.slice_in_dim(shard, 0, size, axis=dim), axis, down)
        shard = jnp.concatenate([before, shard, after], axis=dim)
    return shard


def green_stack(green_table):
    real_part = green_table[:, 0]
    imag_part = green_table[:, 1]
    upper_half = jnp.concatenate([real_part, -imag_part], axis=2)
    lower_half = jnp.concatenate([imag_part, real_part], axis=2)
    return jnp.concatenate([upper_half, lower_half], axis=1)


def rounded(value):
    return lax.reduce_precision(value, 8, 7)


def first_weights(w_in, b_in):
    w = w_in.reshape(HIDDEN, 3, 3)
    w1 = rounded(w)
    w2 = rounded(w - w1)
    b1 = rounded(b_in)
    b2 = rounded(b_in - b1)
    b3 = b_in - b1 - b2
    cells = jnp.stack([w1, w2, w1, w2, w1], 3).reshape(HIDDEN, 3, 15)
    bias = jnp.stack([b1, b2, b3], 1)[:, :, None]
    return jnp.concatenate([cells, bias], 2).reshape(HIDDEN, 48).astype(bf16)


def back_weights(w_in, w_out):
    v = (w_in.T[None] * w_out[:, None, :]).reshape(18, HIDDEN)
    v1 = rounded(v)
    v2 = v - v1
    both = jnp.concatenate([v1, v1, v2], 1)
    return jnp.pad(both, ((0, 14), (0, 0))).astype(bf16)


def local(far_adjoint, pillar, green_blocks, pair_src, pair_dst, group_end, w_in, b_in, w_out):
    own = to_block_table(far_adjoint).reshape(NB, NB // 4, 16, 128)
    ext = with_halo(own, (("tx", 0, CONE), ("ty", 1, CONE // 4)))
    ext = ext.reshape(EXT * EXT * 4, 128)
    near = sparse_near(
        pair_dst.reshape(-1), group_end.reshape(-1), pair_src.reshape(-1), ext,
        green_stack(green_blocks),
    )
    wide = with_halo(pillar, (("tx", 0, 1), ("ty", 1, 1)))
    wide = jnp.pad(wide, ((0, 6), (0, 0)))
    p3 = jnp.stack([wide[:, b : b + SIDE] for b in range(3)])
    grad, west, east, sums = cell_model(
        p3, near, first_weights(w_in, b_in), back_weights(w_in, w_out)
    )
    grad = exchange_edges(grad, west, east)
    both = sums.reshape(2, 2, HIDDEN, 2, SROWS).sum((1, 3))
    back = both[0]
    grad_in = w_out[0][:, None] * back[:, 0:10] + w_out[1][:, None] * back[:, 10:20]
    packed = jnp.concatenate([grad_in, both[1][:, 9:10], both[1][:, 19:20]], 1)
    count = lax.axis_size("tx") * lax.axis_size("ty")
    scale = float(SIDE * SIDE * count) ** (-0.5)
    packed = lax.psum(packed, ("tx", "ty")) * scale
    return grad, packed[:, 0:9], packed[:, 9], packed[:, 10:12].T


def exchange_edges(grad, west, east):
    up, down = neighbours("tx")
    def line(row):
        return jnp.concatenate([west[row, 0:1], grad[row], east[row, 127:128]])
    from_below = lax.ppermute(line(7), "tx", down)
    from_above = lax.ppermute(line(SIDE + 8), "tx", up)
    core = grad[8 : SIDE + 8]
    core = core.at[SIDE - 1].add(from_below[1 : SIDE + 1]).at[0].add(from_above[1 : SIDE + 1])
    left = west[8 : SIDE + 8, 0]
    left = left.at[SIDE - 1].add(from_below[0]).at[0].add(from_above[0])
    right = east[8 : SIDE + 8, 127]
    right = right.at[SIDE - 1].add(from_below[SIDE + 1]).at[0].add(from_above[SIDE + 1])
    up, down = neighbours("ty")
    from_right = lax.ppermute(left, "ty", down)
    from_left = lax.ppermute(right, "ty", up)
    return core.at[:, SIDE - 1].add(from_right).at[:, 0].add(from_left)


def solution(mesh):
    return jax.shard_map(
        local,
        mesh=mesh,
        in_specs=(
            P(None, "tx", "ty"),
            P("tx", "ty"),
            P(),
            P("tx", "ty", None),
            P("tx", "ty", None),
            P("tx", "ty", None),
            P(),
            P(),
            P(),
        ),
        out_specs=(P("tx", "ty"), P(), P(), P()),
        check_vma=False,
    )
```

time: 1370 us -> 423 us (0.31)
  matrix products: 434 us -> 0 us
  blocking collectives: 462 us -> 114 us
  local copies, waits for them, and re-layouts: 287 us -> 17.5 us
  Pallas kernels: 0 us -> 220 us
  other arithmetic: 111 us -> 22.2 us
    dot_general x91 -> x0, matrix products: 434 us -> none  [the longest x16 113 us: cell_pass(): pulled = jnp.einsum('ck,cij->kij', w_out, near_band, precision=highest)]
    psum x1, blocking collectives: 462 us -> 114 us  [local(): packed = lax.psum(packed, ('tx', 'ty')) * scale]
    pallas_call x0 -> x3, Pallas kernels: none -> 220 us  [the longest x1 156 us: cell_model(): pl.pallas_call(cell_kernel, out_shape=[jax.ShapeDtypeStruct((rows, SIDE),...]
    scatter-add x11 -> x2, other arithmetic: 88.3 us -> 1.53 us  [exchange_edges(): right.at[SIDE - 1].add(from_below[SIDE + 1]).at[0].add(from_above[SIDE + 1])]
    while x67 -> x0, local copies, waits for them, and re-layouts: 64.9 us -> none
    gather x11 -> x0, local copies, waits for them, and re-layouts: 55.3 us -> none  [one_piece(): ext_blocks[piece_dst]]
    reshape x3, local copies, waits for them, and re-layouts: 35.7 us -> 0.14 us  [the longest x1 0.11 us: local(): both = sums.reshape(2, 2, HIDDEN, 2, SROWS).sum((1, 3))]
    unnamed x39 -> x22, local copies, waits for them, and re-layouts: 32.8 us -> 1.01 us
  transfers between devices with their start and end apart: 12 -> 12, of which waited for: 5 -> 2; matrix products, arithmetic and copies ran while one was open for 2% -> 6% of each run, Pallas kernels for 0% -> 2%
where the time goes in v1:
time: 423 us; the launch traced here: 414 us
  Pallas kernels  220 us (52%)
  blocking collectives  114 us (27%)
  starting transfers between devices  34.4 us (8%)
  other arithmetic  22.2 us (5%)
  local copies, waits for them, and re-layouts  17.5 us (4%)
  waiting for transfers between devices  5.13 us (1%)
    pallas_call x1, Pallas kernels, cell_model(): pl.pallas_call(cell_kernel, out_shape=[jax.ShapeDtypeStruct((rows, SIDE),...  156 us
    psum x1, blocking collectives, local(): packed = lax.psum(packed, ('tx', 'ty')) * scale  114 us
    pallas_call x1, Pallas kernels, sparse_near(): pl.pallas_call(sparse_kernel, out_shape=jax.ShapeDtypeStruct((2, SIDE + 2...  53.9 us
    ppermute x4, starting transfers between devices, with_halo(): lax.ppermute(lax.slice_in_dim(shard, length - size, length, axis=dim), ax...  17 us
    pallas_call x1, Pallas kernels, to_block_table(): pl.pallas_call(block_kernel, out_shape=jax.ShapeDtypeStruct((NB * NB * 4,...  9.98 us
  transfers between devices with their start and end apart: 12, of which 2 were waited for; matrix products, arithmetic and copies ran while one was open for 6% of the time, Pallas kernels for 2%

profile of v1, /device:TPU:1, one launch (start us, length us, event | category | flops | bytes accessed | tf_op | source)
XLA Modules:
  0.0 414.4 jit_solution(3939105511929587764)
XLA Ops:
  0.6 1.5 fusion.23
  2.1 4.5 %collective-permute-start = (f32[1,512]{1,0:T(1,128)}, f32[1,512]{1,0:T(1,128)}, u32[]{:S(2)}, u32[]{:S(2)}) collective-permute-start(f32[1,512]{1,0:T(1,128)} %get-tuple-element.121), channel_id=1, source_target_pairs={{0,16},{16,32},{32,48},{48,64},{64,80},{80,96},{96,112},{1,17},{17... | collective-permute-start | bytes 6152 | tf_op jit(solution)/shard_map/ppermute | solution.py:320
  6.6 1.3 collective-permute-start.1
  7.9 10.0 %to_blocks.1 = bf16[4096,128]{1,0:T(8,128)(2,1)} custom-call(bf16[2,512,512]{2,1,0:T(8,128)(2,1)} %far_ref.1), custom_call_target="tpu_custom_call" | custom-call | tf_op jit(solution)/shard_map/to_blocks/pallas_call | solution.py:57
  17.8 2.1 fusion.22
  19.9 4.0 collective-permute-start.4
  23.9 1.4 collective-permute-start.5
  25.4 1.5 slice_bitcast_fusion.3
  27.0 0.7 broadcast_multiply_fusion
  27.8 0.5 slice_bitcast_fusion.8
  28.4 3.9 maximum_maximum_fusion.green_ref
  32.2 0.7 fusion.9.v_ref
  33.0 1.6 pad_maximum_fusion.7
  34.6 4.9 %collective-permute-start.2 = (f32[514,1]{1,0:T(8,128)}, f32[514,1]{1,0:T(8,128)S(1)}, u32[]{:S(2)}, u32[]{:S(2)}) collective-permute-start(f32[514,1]{1,0:T(8,128)} %get-tuple-element.117), channel_id=1, source_target_pairs={{0,1},{1,2},{2,3},{3,4},{4,5},{5,6},{6,7},{7,8},{8,9},{9,10},{10,1... | collective-permute-start | bytes 6176 | tf_op jit(solution)/shard_map/ppermute | solution.py:320
  39.5 1.9 collective-permute-start.3
  41.5 2.2 pad_maximum_fusion.4
  43.7 3.6 collective-permute-start.6
  47.4 1.9 collective-permute-start.7
  49.3 0.7 copy.36.w1_ref
  50.0 0.6 compare_reduce_fusion
  50.6 1.4 select_maximum_fusion
  52.1 0.7 slice_bitcast_fusion.2
  52.7 2.1 pad_maximum_fusion.1.p3_ref
  54.8 0.7 collective-permute-done.6
  55.5 4.4 %collective-permute-done.7 = bf16[56,3,16,128]{3,2,1,0:T(8,128)(2,1)} collective-permute-done((bf16[56,3,16,128]{3,2,1,0:T(8,128)(2,1)}, bf16[56,3,16,128]{3,2,1,0:T(8,128)(2,1)}, u32[]{:S(2)}, u32[]{:S(2)}) %collective-permute-start.7) | collective-permute-done | bytes 688160 | tf_op jit(solution)/shard_map/ppermute | solution.py:323
  59.9 3.0 pad_maximum_fusion
  62.9 53.9 %sparse_near.1.near_ref = f32[2,544,512]{2,1,0:T(8,128)} custom-call(s32[24576]{0:T(1024)} %bitcast.71, s32[8]{0:T(128)} %bitcast.84, s32[48,1,512]{2,1,0:T(1,128)} %bitcast.72, bf16[12544,128]{1,0:T(8,128)(2,1)} %bitcast.70, bf16[8,512,512]{2,1,0:T(8,128)(2,1)} %maximum_maximum_fusion.green_ref), custom_call_target="tpu_custom_call" | custom-call | tf_op jit(solution)/shard_map/sparse_near/pallas_call | solution.py:150
  116.8 155.9 %cell_model.1 = (f32[528,512]{1,0:T(8,128)}, f32[528,128]{1,0:T(8,128)}, f32[528,128]{1,0:T(8,128)}, f32[256,48]{1,0:T(8,128)}) custom-call(f32[3,520,512]{2,1,0:T(8,128)} %pad_maximum_fusion.1.p3_ref, f32[2,544,512]{2,1,0:T(8,128)} %sparse_near.1.near_ref, bf16[64,48]{1,0:T(8,128)(2,1)} %copy.36.w1_ref, bf16[32,192]{1,0:T(8,128)(2,1)} %fusion.9.v_ref), custom_call_target="tpu_custom_call" | custom-call | tf_op jit(solution)/shard_map/cell_model/pallas_call | solution.py:288
  272.6 1.0 copy.39
  273.9 114.5 %psum.7 = f32[64,12]{0,1:T(8,128)S(1)} all-reduce(f32[64,12]{0,1:T(8,128)S(1)} %pad_maximum_fusion.9), channel_id=1, replica_groups=mesh['tx'=8,'ty'=16] {'tx','ty'}, use_global_device_ids=true, to_apply=%region_2.3 | all-reduce | flops 768 | bytes 6144 | tf_op jit(solution)/shard_map/psum | solution.py:381
  388.4 0.6 slice_bitcast_fusion.5
  389.0 0.5 slice_bitcast_fusion.6
  389.5 1.3 slice_reduce_fusion
  390.8 1.4 fusion.24
  392.2 0.7 fusion.21
  393.0 1.2 pad_maximum_fusion.10
  394.2 1.3 collective-permute-start.8
  395.5 1.5 pad_maximum_fusion.11
  396.9 1.3 slice.258
  398.2 4.0 collective-permute-start.9
  402.2 1.4 fusion.18
  403.8 3.5 collective-permute-start.10
  407.4 0.7 slice_add_fusion.2
  408.2 2.0 collective-permute-start.11
  410.6 1.1 scatter-add.34
  411.9 0.6 add_select_fusion
  412.5 0.9 scatter-add.39
  413.5 1.0 copy-done.3
  (63 shorter events, 1.3 us)
Async XLA Ops:
  0.6 24.7 %copy-start.1 = (bf16[8,2,256,256]{3,2,1,0:T(8,128)(2,1)S(1)}, bf16[8,2,256,256]{3,2,1,0:T(8,128)(2,1)}, u32[]{:S(2)}) copy-start(bf16[8,2,256,256]{3,2,1,0:T(8,128)(2,1)} %param.27) | copy-start | bytes 6291460
  2.1 30.9 %collective-permute-start = (f32[1,512]{1,0:T(1,128)}, f32[1,512]{1,0:T(1,128)}, u32[]{:S(2)}, u32[]{:S(2)}) collective-permute-start(f32[1,512]{1,0:T(1,128)} %get-tuple-element.121), channel_id=1, source_target_pairs={{0,16},{16,32},{32,48},{48,64},{64,80},{80,96},{96,112},{1,17},{17... | collective-permute-start | bytes 6152 | tf_op jit(solution)/shard_map/ppermute | solution.py:320
  6.6 26.4 %collective-permute-start.1 = (f32[1,512]{1,0:T(1,128)}, f32[1,512]{1,0:T(1,128)}, u32[]{:S(2)}, u32[]{:S(2)}) collective-permute-start(f32[1,512]{1,0:T(1,128)} %get-tuple-element.122), channel_id=1, source_target_pairs={{16,0},{32,16},{48,32},{64,48},{80,64},{96,80},{112,96},{17,1},{33... | collective-permute-start | bytes 6152 | tf_op jit(solution)/shard_map/ppermute | solution.py:323
  19.9 21.5 %collective-permute-start.4 = (bf16[12,8,16,128]{3,2,1,0:T(8,128)(2,1)}, bf16[12,8,16,128]{3,2,1,0:T(8,128)(2,1)S(1)}, u32[]{:S(2)}, u32[]{:S(2)}) collective-permute-start(bf16[12,8,16,128]{3,2,1,0:T(8,128)(2,1)} %bitcast.6), channel_id=1, source_target_pairs={{0,16},{16,32},{32,48},{48,64},{64,80},{80,96},{96,112},{1,17},{17... | collective-permute-start | bytes 1179656 | tf_op jit(solution)/shard_map/ppermute | solution.py:320
  23.9 3.1 copy-start.4
  23.9 17.5 %collective-permute-start.5 = (bf16[12,8,16,128]{3,2,1,0:T(8,128)(2,1)}, bf16[12,8,16,128]{3,2,1,0:T(8,128)(2,1)}, u32[]{:S(2)}, u32[]{:S(2)}) collective-permute-start(bf16[12,8,16,128]{3,2,1,0:T(8,128)(2,1)} %bitcast.8), channel_id=1, source_target_pairs={{16,0},{32,16},{48,32},{64,48},{80,64},{96,80},{112,96},{17,1},{33... | collective-permute-start | bytes 1179656 | tf_op jit(solution)/shard_map/ppermute | solution.py:323
  26.9 0.8 copy-start.5
  26.9 0.9 copy-start.7
  28.3 3.9 copy-start.10
  28.3 4.6 %copy-start.2 = (f32[512,512]{1,0:T(8,128)S(1)}, f32[512,512]{1,0:T(8,128)}, u32[]{:S(2)}) copy-start(f32[512,512]{1,0:T(8,128)} %param.26) | copy-start | bytes 3145732
  32.2 9.2 %copy-start = (bf16[4096,128]{1,0:T(8,128)(2,1)S(1)}, bf16[4096,128]{1,0:T(8,128)(2,1)}, u32[]{:S(2)}) copy-start(bf16[4096,128]{1,0:T(8,128)(2,1)} %to_blocks.1) | copy-start | bytes 3145732
  34.6 16.1 %collective-permute-start.2 = (f32[514,1]{1,0:T(8,128)}, f32[514,1]{1,0:T(8,128)S(1)}, u32[]{:S(2)}, u32[]{:S(2)}) collective-permute-start(f32[514,1]{1,0:T(8,128)} %get-tuple-element.117), channel_id=1, source_target_pairs={{0,1},{1,2},{2,3},{3,4},{4,5},{5,6},{6,7},{7,8},{8,9},{9,10},{10,1... | collective-permute-start | bytes 6176 | tf_op jit(solution)/shard_map/ppermute | solution.py:320
  39.5 11.1 %collective-permute-start.3 = (f32[514,1]{1,0:T(8,128)}, f32[514,1]{1,0:T(8,128)}, u32[]{:S(2)}, u32[]{:S(2)}) collective-permute-start(f32[514,1]{1,0:T(8,128)} %get-tuple-element.118), channel_id=1, source_target_pairs={{1,0},{2,1},{3,2},{4,3},{5,4},{6,5},{7,6},{8,7},{9,8},{10,9},{11,1... | collective-permute-start | bytes 6176 | tf_op jit(solution)/shard_map/ppermute | solution.py:323
  43.7 11.8 %collective-permute-start.6 = (bf16[56,3,16,128]{3,2,1,0:T(8,128)(2,1)}, bf16[56,3,16,128]{3,2,1,0:T(8,128)(2,1)S(1)}, u32[]{:S(2)}, u32[]{:S(2)}) collective-permute-start(bf16[56,3,16,128]{3,2,1,0:T(8,128)(2,1)} %get-tuple-element.110), channel_id=1, source_target_pairs={{0,1},{1,2},{2,3},{3,4},{4,5},{5,6},{6,7},{7,8},{8,9},{9,10},{10,1... | collective-permute-start | bytes 2064392 | tf_op jit(solution)/shard_map/ppermute | solution.py:320
  47.4 12.6 %collective-permute-start.7 = (bf16[56,3,16,128]{3,2,1,0:T(8,128)(2,1)}, bf16[56,3,16,128]{3,2,1,0:T(8,128)(2,1)}, u32[]{:S(2)}, u32[]{:S(2)}) collective-permute-start(bf16[56,3,16,128]{3,2,1,0:T(8,128)(2,1)} %get-tuple-element.111), channel_id=1, source_target_pairs={{1,0},{2,1},{3,2},{4,3},{5,4},{6,5},{7,6},{8,7},{9,8},{10,9},{11,1... | collective-permute-start | bytes 2064392 | tf_op jit(solution)/shard_map/ppermute | solution.py:323
  116.8 157.1 %copy-start.8 = (f32[64]{0:T(128)S(1)}, f32[64]{0:T(128)}, u32[]{:S(2)}) copy-start(f32[64]{0:T(128)} %get-tuple-element.139) | copy-start | bytes 772
  116.8 157.1 %copy-start.9 = (f32[64]{0:T(128)S(1)}, f32[64]{0:T(128)}, u32[]{:S(2)}) copy-start(f32[64]{0:T(128)} %get-tuple-element.140) | copy-start | bytes 772
  388.4 23.3 %copy-start.6 = (f32[64,12]{0,1:T(8,128)}, f32[64,12]{0,1:T(8,128)S(1)}, u32[]{:S(2)}) copy-start(f32[64,12]{0,1:T(8,128)S(1)} %broadcast_multiply_fusion.2) | copy-start | bytes 9220
  394.2 8.0 %collective-permute-start.8 = (f32[514]{0:T(1024)S(1)}, f32[514]{0:T(1024)S(1)}, u32[]{:S(2)}, u32[]{:S(2)}) collective-permute-start(f32[514]{0:T(1024)S(1)} %pad_maximum_fusion.10), channel_id=1, source_target_pairs={{16,0},{32,16},{48,32},{64,48},{80,64},{96,80},{112,96},{17,1},{33... | collective-permute-start | bytes 6176 | tf_op jit(solution)/shard_map/ppermute | solution.py:389
  398.2 5.5 %collective-permute-start.9 = (f32[514]{0:T(1024)S(1)}, f32[514]{0:T(1024)S(1)}, u32[]{:S(2)}, u32[]{:S(2)}) collective-permute-start(f32[514]{0:T(1024)S(1)} %pad_maximum_fusion.11), channel_id=1, source_target_pairs={{0,16},{16,32},{32,48},{48,64},{64,80},{80,96},{96,112},{1,17},{17... | collective-permute-start | bytes 6176 | tf_op jit(solution)/shard_map/ppermute | solution.py:390
  403.8 6.5 %collective-permute-start.10 = (f32[512]{0:T(512)S(1)}, f32[512]{0:T(512)S(1)}, u32[]{:S(2)}, u32[]{:S(2)}) collective-permute-start(f32[512]{0:T(512)S(1)} %get-tuple-element.136), channel_id=1, source_target_pairs={{1,0},{2,1},{3,2},{4,3},{5,4},{6,5},{7,6},{8,7},{9,8},{10,9},{11,1... | collective-permute-start | bytes 6152 | tf_op jit(solution)/shard_map/ppermute | solution.py:398
  408.2 3.5 collective-permute-start.11
  413.4 1.0 copy-start.3

commit v2 on v1

--- a/solution.py
+++ b/solution.py
@@ -22,6 +22,7 @@
 
 f32 = jnp.float32
 bf16 = jnp.bfloat16
+MESH = pl.DeviceIdType.MESH
 
 
 def swap_pieces(v):
@@ -186,7 +187,21 @@
 
 
 def cell_kernel(
-    p3_ref, near_ref, w1_ref, v_ref, grad_ref, west_ref, east_ref, sums_ref, q32, qs, gs, ps, total
+    p3_ref,
+    near_ref,
+    w1_ref,
+    v_ref,
+    wout_ref,
+    grad_ref,
+    west_ref,
+    east_ref,
+    sums_ref,
+    q32,
+    qs,
+    gs,
+    ps,
+    total,
+    nh,
 ):
     width = SIDE
 
@@ -207,6 +222,7 @@
 
     lax.fori_loop(0, (SIDE + 8) // 8, build, 0)
     total[...] = jnp.zeros_like(total)
+    nh[...] = jnp.zeros_like(nh)
     gs[...] = jnp.zeros_like(gs)
     zero_rows = jnp.zeros((PADROWS * SROWS, 128), f32)
     for t in range(4):
@@ -226,36 +242,60 @@
             put(gs, 10 * c + 9, SROWS, n[c])
         for half in range(2):
             left, right = [], []
-            for j in range(4 * half, 4 * half + 4):
-                feats = qs[pl.ds(r0 + j, 3)].reshape(48, width)
-                h = jnp.tanh(jnp.dot(w1_ref[...], feats, preferred_element_type=f32))
-                u = 1.0 - h * h
-                u1 = u.astype(bf16)
-                u2 = (u - u1.astype(f32)).astype(bf16)
-                h1 = h.astype(bf16)
-                h2 = (h - h1.astype(f32)).astype(bf16)
+            partial = [None, None]
+            feats = qs[pl.ds(r0 + 4 * half, 6)].reshape(96, width)
+            h = jnp.tanh(jnp.dot(w1_ref[...], feats, preferred_element_type=f32))
+            for pair in range(2):
+                pieces = []
+                for r in range(2 * pair, 2 * pair + 2):
+                    j = 4 * half + r
+                    hr = h[HIDDEN * r : HIDDEN * r + HIDDEN]
+                    u = 1.0 - hr * hr
+                    u1 = u.astype(bf16)
+                    u2 = (u - u1.astype(f32)).astype(bf16)
+                    pieces += [u1, u2]
+                    for c in range(2):
+                        for t in range(4):
+                            tile = slice(128 * t, 128 * t + 128)
+                            term = n[c][j : j + 1, tile] * hr[:, tile]
+                            partial[c] = term if partial[c] is None else partial[c] + term
+                    g = jnp.concatenate(
+                        [gs[t, SROWS * j : SROWS * j + SROWS, :] for t in range(4)], 1
+                    )
+                    g1, g2 = split2(g)
+                    left.append(jnp.concatenate([u1, u2], 0))
+                    right.append(jnp.concatenate([g1, g2], 0).astype(bf16))
                 slope = jnp.dot(
-                    v_ref[...], jnp.concatenate([u1, u2, u1], 0), preferred_element_type=f32
+                    v_ref[...], jnp.concatenate(pieces, 0), preferred_element_type=f32
                 )
-                at = pl.ds(pl.multiple_of((r0 + PADROWS + j) * SROWS, 8), SROWS)
-                for t in range(4):
-                    ps[t, at, :] = slope[:SROWS, 128 * t : 128 * t + 128]
-                g = jnp.concatenate(
-                    [gs[t, SROWS * j : SROWS * j + SROWS, :] for t in range(4)], 1
-                )
-                g1, g2 = split2(g)
-                left.append(jnp.concatenate([u1, u2, h1, h2], 0))
-                right.append(jnp.concatenate([g1, g2], 0).astype(bf16))
-            total[...] += lax.dot_general(
+                for r in range(2):
+                    j = 4 * half + 2 * pair + r
+                    one = (
+                        slope[2 * SROWS * r : 2 * SROWS * r + SROWS]
+                        + slope[2 * SROWS * r + SROWS : 2 * SROWS * r + 2 * SROWS]
+                    )
+                    at = pl.ds(pl.multiple_of((r0 + PADROWS + j) * SROWS, 8), SROWS)
+                    for t in range(4):
+                        ps[t, at, :] = one[:, 128 * t : 128 * t + 128]
+            total[:, 0 : 2 * SROWS] += lax.dot_general(
                 jnp.concatenate(left, 1),
                 jnp.concatenate(right, 1),
                 (((1,), (1,)), ((), ())),
                 preferred_element_type=f32,
             )
+            for c in range(2):
+                nh[HIDDEN * c : HIDDEN * c + HIDDEN, :] += partial[c]
         return carry
 
     lax.fori_loop(0, SIDE // 8, strip, 0)
-    sums_ref[...] = total[...]
+    turned = total[...].T
+    turned = turned + pltpu.roll(turned, HIDDEN, 1)
+    pulled = turned[0:SROWS] + turned[SROWS : 2 * SROWS]
+    first = wout_ref[0:1, :] * pulled[0:10] + wout_ref[1:2, :] * pulled[10:20]
+    second = jnp.sum(nh[...].T, axis=0, keepdims=True)
+    sums_ref[...] = jnp.zeros_like(sums_ref)
+    sums_ref[0:10, :] = first
+    sums_ref[10:11, :] = second
 
     lane = lax.broadcasted_iota(jnp.int32, (8, width), 1)
 
@@ -283,7 +323,7 @@
     lax.fori_loop(0, SIDE // 8 + 2, combine, 0)
 
 
-def cell_model(p3, near, first, back):
+def cell_model(p3, near, first, back, out_weights):
     rows = SIDE + 16
     return pl.pallas_call(
         cell_kernel,
@@ -291,20 +331,21 @@
             jax.ShapeDtypeStruct((rows, SIDE), f32),
             jax.ShapeDtypeStruct((rows, 128), f32),
             jax.ShapeDtypeStruct((rows, 128), f32),
-            jax.ShapeDtypeStruct((4 * HIDDEN, 2 * SROWS), f32),
+            jax.ShapeDtypeStruct((16, 128), f32),
         ],
-        in_specs=[pl.BlockSpec(memory_space=pltpu.VMEM)] * 4,
+        in_specs=[pl.BlockSpec(memory_space=pltpu.VMEM)] * 5,
         out_specs=[pl.BlockSpec(memory_space=pltpu.VMEM)] * 4,
         scratch_shapes=[
             pltpu.VMEM((4, 128, 128), f32),
             pltpu.VMEM((SIDE + 8, 16, SIDE), bf16),
             pltpu.VMEM((4, 8 * SROWS, 128), f32),
             pltpu.VMEM((4, (SIDE + 2 * PADROWS) * SROWS, 128), f32),
-            pltpu.VMEM((4 * HIDDEN, 2 * SROWS), f32),
+            pltpu.VMEM((128, 128), f32),
+            pltpu.VMEM((128, 128), f32),
         ],
         compiler_params=pltpu.CompilerParams(vmem_limit_bytes=VMEM_BYTES),
         name="cell_model",
-    )(p3, near, first, back)
+    )(p3, near, first, back, out_weights)
 
 
 def neighbours(axis):
@@ -346,15 +387,26 @@
     b3 = b_in - b1 - b2
     cells = jnp.stack([w1, w2, w1, w2, w1], 3).reshape(HIDDEN, 3, 15)
     bias = jnp.stack([b1, b2, b3], 1)[:, :, None]
-    return jnp.concatenate([cells, bias], 2).reshape(HIDDEN, 48).astype(bf16)
+    one = jnp.concatenate([cells, bias], 2).reshape(HIDDEN, 48)
+    return jnp.concatenate(
+        [jnp.pad(one, ((0, 0), (16 * r, 48 - 16 * r))) for r in range(4)], 0
+    ).astype(bf16)
 
 
 def back_weights(w_in, w_out):
     v = (w_in.T[None] * w_out[:, None, :]).reshape(18, HIDDEN)
     v1 = rounded(v)
     v2 = v - v1
-    both = jnp.concatenate([v1, v1, v2], 1)
-    return jnp.pad(both, ((0, 14), (0, 0))).astype(bf16)
+    wide = jnp.concatenate(
+        [
+            jnp.pad(jnp.concatenate([v1, v1], 1), ((0, 6), (0, 0))),
+            jnp.pad(v2, ((0, 6), (0, HIDDEN))),
+        ],
+        0,
+    )
+    upper = jnp.pad(wide, ((0, 0), (0, 2 * HIDDEN)))
+    lower = jnp.pad(wide, ((0, 0), (2 * HIDDEN, 0)))
+    return jnp.concatenate([upper, lower], 0).astype(bf16)
 
 
 def local(far_adjoint, pillar, green_blocks, pair_src, pair_dst, group_end, w_in, b_in, w_out):
@@ -369,35 +421,213 @@
     wide = jnp.pad(wide, ((0, 6), (0, 0)))
     p3 = jnp.stack([wide[:, b : b + SIDE] for b in range(3)])
     grad, west, east, sums = cell_model(
-        p3, near, first_weights(w_in, b_in), back_weights(w_in, w_out)
+        p3,
+        near,
+        first_weights(w_in, b_in),
+        back_weights(w_in, w_out),
+        jnp.pad(w_out, ((0, 6), (0, HIDDEN))),
     )
-    grad = exchange_edges(grad, west, east)
-    both = sums.reshape(2, 2, HIDDEN, 2, SROWS).sum((1, 3))
-    back = both[0]
-    grad_in = w_out[0][:, None] * back[:, 0:10] + w_out[1][:, None] * back[:, 10:20]
-    packed = jnp.concatenate([grad_in, both[1][:, 9:10], both[1][:, 19:20]], 1)
-    count = lax.axis_size("tx") * lax.axis_size("ty")
-    scale = float(SIDE * SIDE * count) ** (-0.5)
-    packed = lax.psum(packed, ("tx", "ty")) * scale
-    return grad, packed[:, 0:9], packed[:, 9], packed[:, 10:12].T
-
-
-def exchange_edges(grad, west, east):
-    up, down = neighbours("tx")
-    def line(row):
-        return jnp.concatenate([west[row, 0:1], grad[row], east[row, 127:128]])
-    from_below = lax.ppermute(line(7), "tx", down)
-    from_above = lax.ppermute(line(SIDE + 8), "tx", up)
-    core = grad[8 : SIDE + 8]
-    core = core.at[SIDE - 1].add(from_below[1 : SIDE + 1]).at[0].add(from_above[1 : SIDE + 1])
-    left = west[8 : SIDE + 8, 0]
-    left = left.at[SIDE - 1].add(from_below[0]).at[0].add(from_above[0])
-    right = east[8 : SIDE + 8, 127]
-    right = right.at[SIDE - 1].add(from_below[SIDE + 1]).at[0].add(from_above[SIDE + 1])
-    up, down = neighbours("ty")
-    from_right = lax.ppermute(left, "ty", down)
-    from_left = lax.ppermute(right, "ty", up)
-    return core.at[:, SIDE - 1].add(from_right).at[:, 0].add(from_left)
+    grad, sums = finish(grad, west, east, sums)
+    return (
+        grad,
+        sums[0:9, 0:HIDDEN].T,
+        sums[9, 0:HIDDEN],
+        sums[10].reshape(2, HIDDEN),
+    )
+
+
+def finish_kernel(
+    shape,
+    grad_ref,
+    west_ref,
+    east_ref,
+    msg_ref,
+    out_ref,
+    sums_ref,
+    row_out,
+    row_in,
+    col_out,
+    col_in,
+    cols,
+    buf_a,
+    buf_b,
+    row_send,
+    row_recv,
+    col_send,
+    col_recv,
+    send_a,
+    recv_a,
+    send_b,
+    recv_b,
+):
+    nx, ny = shape
+    tx = lax.axis_index("tx")
+    ty = lax.axis_index("ty")
+
+    barrier = pltpu.get_barrier_semaphore()
+    for d in range(1, nx):
+        pl.semaphore_signal(
+            barrier, inc=1, device_id=(lax.rem(tx + d, nx), ty), device_id_type=MESH
+        )
+    for d in range(1, ny):
+        pl.semaphore_signal(
+            barrier, inc=1, device_id=(tx, lax.rem(ty + d, ny)), device_id_type=MESH
+        )
+    if nx + ny > 2:
+        pl.semaphore_wait(barrier, nx + ny - 2)
+
+    def line(side, which):
+        out, into, send, recv, axis = which
+        at = (tx, ty)[axis] + 2 * side - 1
+        device = (at, ty) if axis == 0 else (tx, at)
+        return pltpu.make_async_remote_copy(
+            src_ref=out.at[side],
+            dst_ref=into.at[side],
+            send_sem=send.at[side],
+            recv_sem=recv.at[side],
+            device_id=device,
+            device_id_type=MESH,
+        )
+
+    rows = (row_out, row_in, row_send, row_recv, 0)
+    columns = (col_out, col_in, col_send, col_recv, 1)
+
+    def has(side, index, count):
+        return index > 0 if side == 0 else index < count - 1
+
+    row_out[0, :, 0:128] = west_ref[0:8, :]
+    row_out[0, :, 128 : 128 + SIDE] = grad_ref[0:8, :]
+    row_out[0, :, 128 + SIDE : 256 + SIDE] = east_ref[0:8, :]
+    row_out[1, :, 0:128] = west_ref[SIDE + 8 : SIDE + 16, :]
+    row_out[1, :, 128 : 128 + SIDE] = grad_ref[SIDE + 8 : SIDE + 16, :]
+    row_out[1, :, 128 + SIDE : 256 + SIDE] = east_ref[SIDE + 8 : SIDE + 16, :]
+    for side in range(2):
+        pl.when(has(side, tx, nx))(lambda side=side: line(side, rows).start())
+
+    def sums_copy(d, buf, send, recv, index, count, axis):
+        other = lax.rem(index + d, count)
+        return pltpu.make_async_remote_copy(
+            src_ref=buf.at[index],
+            dst_ref=buf.at[index],
+            send_sem=send.at[d],
+            recv_sem=recv.at[index],
+            device_id=(other, ty) if axis == 0 else (tx, other),
+            device_id_type=MESH,
+        )
+
+    def sums_wait(d, buf, send, recv, index, count, axis):
+        sender = lax.rem(index + d, count)
+        pltpu.make_async_remote_copy(
+            src_ref=buf.at[sender],
+            dst_ref=buf.at[sender],
+            send_sem=send.at[d],
+            recv_sem=recv.at[sender],
+            device_id=(sender, ty) if axis == 0 else (tx, sender),
+            device_id_type=MESH,
+        ).wait_recv()
+
+    along_x = (buf_a, send_a, recv_a, tx, nx, 0)
+    along_y = (buf_b, send_b, recv_b, ty, ny, 1)
+    buf_a[tx] = msg_ref[...]
+    for d in range(1, nx):
+        sums_copy(d, *along_x).start()
+
+    def copy(i, carry):
+        at = pl.multiple_of(i * 8, 8)
+        out_ref[pl.ds(at, 8), :] = grad_ref[pl.ds(at + 8, 8), :]
+        cols[0, pl.ds(at, 8), :] = west_ref[pl.ds(at + 8, 8), :]
+        cols[1, pl.ds(at, 8), :] = east_ref[pl.ds(at + 8, 8), :]
+        return carry
+
+    lax.fori_loop(0, SIDE // 8, copy, 0)
+    for side, row, first in ((0, 7, SIDE - 8), (1, 0, 0)):
+
+        @pl.when(has(1 - side, tx, nx))
+        def _(side=side, row=row, first=first):
+            line(side, rows).wait_recv()
+            got = row_in[side]
+            got = jnp.where(
+                lax.broadcasted_iota(jnp.int32, got.shape, 0) == row, got, 0.0
+            )
+            out_ref[first : first + 8, :] += got[:, 128 : 128 + SIDE]
+            cols[0, first : first + 8, :] += got[:, 0:128]
+            cols[1, first : first + 8, :] += got[:, 128 + SIDE : 256 + SIDE]
+
+    for q in range(4):
+        tile = slice(128 * q, 128 * q + 128)
+        col_out[0, :, tile] = cols[0, tile, :].T[0:8]
+        col_out[1, :, tile] = cols[1, tile, :].T[120:128]
+    for side in range(2):
+        pl.when(has(side, ty, ny))(lambda side=side: line(side, columns).start())
+
+    for d in range(1, nx):
+        sums_wait(d, *along_x)
+    value = buf_a[0]
+    for d in range(1, nx):
+        value = value + buf_a[d]
+    buf_b[ty] = value
+    for d in range(1, ny):
+        sums_copy(d, *along_y).start()
+
+    lane = lax.broadcasted_iota(jnp.int32, (128, 128), 1)
+    for side, row, first, spot in ((0, 0, SIDE - 128, 127), (1, 7, 0, 0)):
+
+        @pl.when(has(1 - side, ty, ny))
+        def _(side=side, row=row, first=first, spot=spot):
+            line(side, columns).wait_recv()
+            for q in range(4):
+                tile = slice(128 * q, 128 * q + 128)
+                got = jnp.broadcast_to(col_in[side, row : row + 1, tile], (128, 128)).T
+                out_ref[tile, first : first + 128] += jnp.where(lane == spot, got, 0.0)
+
+    for d in range(1, ny):
+        sums_wait(d, *along_y)
+    value = buf_b[0]
+    for d in range(1, ny):
+        value = value + buf_b[d]
+    sums_ref[...] = value * (float(SIDE * SIDE * nx * ny) ** (-0.5))
+    for side in range(2):
+        pl.when(has(side, tx, nx))(lambda side=side: line(side, rows).wait_send())
+        pl.when(has(side, ty, ny))(lambda side=side: line(side, columns).wait_send())
+    for d in range(1, nx):
+        sums_copy(d, *along_x).wait_send()
+    for d in range(1, ny):
+        sums_copy(d, *along_y).wait_send()
+
+
+def finish(grad, west, east, sums):
+    nx, ny = lax.axis_size("tx"), lax.axis_size("ty")
+    dma = pltpu.SemaphoreType.DMA
+    return pl.pallas_call(
+        functools.partial(finish_kernel, (nx, ny)),
+        out_shape=[
+            jax.ShapeDtypeStruct((SIDE, SIDE), f32),
+            jax.ShapeDtypeStruct((16, 128), f32),
+        ],
+        in_specs=[pl.BlockSpec(memory_space=pltpu.VMEM)] * 4,
+        out_specs=[pl.BlockSpec(memory_space=pltpu.VMEM)] * 2,
+        scratch_shapes=[
+            pltpu.VMEM((2, 8, SIDE + 256), f32),
+            pltpu.VMEM((2, 8, SIDE + 256), f32),
+            pltpu.VMEM((2, 8, SIDE), f32),
+            pltpu.VMEM((2, 8, SIDE), f32),
+            pltpu.VMEM((2, SIDE, 128), f32),
+            pltpu.VMEM((nx, 16, 128), f32),
+            pltpu.VMEM((ny, 16, 128), f32),
+            dma((2,)),
+            dma((2,)),
+            dma((2,)),
+            dma((2,)),
+            dma((nx,)),
+            dma((nx,)),
+            dma((ny,)),
+            dma((ny,)),
+        ],
+        compiler_params=pltpu.CompilerParams(
+            vmem_limit_bytes=VMEM_BYTES, collective_id=0, has_side_effects=True
+        ),
+        name="finish",
+    )(grad, west, east, sums)
 
 
 def solution(mesh):

time: 423 us -> 287 us (0.68); the launches traced: 414 us -> 286 us
  blocking collectives: 114 us -> 0 us
  starting transfers between devices: 34.4 us -> 23.1 us
  Pallas kernels: 220 us -> 230 us
  other arithmetic: 22.2 us -> 14.4 us
  local copies, waits for them, and re-layouts: 17.5 us -> 12.5 us
    psum x1 -> x0, blocking collectives: 114 us -> none  [local(): packed = lax.psum(packed, ('tx', 'ty')) * scale]
    pallas_call x0 -> x1, Pallas kernels: none -> 70.7 us  [finish(): pl.pallas_call(functools.partial(finish_kernel, (nx, ny)), out_shape=[jax...]
    pallas_call x1, Pallas kernels: 156 us -> 96.7 us  [cell_model(): pl.pallas_call(cell_kernel, out_shape=[jax.ShapeDtypeStruct((rows, SIDE),...]
    ppermute x4 -> x0, starting transfers between devices: 10.8 us -> none  [the longest x1 3.99 us: exchange_edges(): from_above = lax.ppermute(line(SIDE + 8), 'tx', up)]
  transfers between devices with their start and end apart: 12 -> 8, of which waited for: 2 -> 2; matrix products, arithmetic and copies ran while one was open for 6% -> 6% of each run, Pallas kernels for 2% -> 3%
where the time goes in v2:
time: 287 us; the launch traced here: 286 us
  Pallas kernels  230 us (80%)
  starting transfers between devices  23.1 us (8%)
  other arithmetic  14.4 us (5%)
  local copies, waits for them, and re-layouts  12.5 us (4%)
  waiting for transfers between devices  5.86 us (2%)
    pallas_call x1, Pallas kernels, cell_model(): pl.pallas_call(cell_kernel, out_shape=[jax.ShapeDtypeStruct((rows, SIDE),...  96.7 us
    pallas_call x1, Pallas kernels, finish(): pl.pallas_call(functools.partial(finish_kernel, (nx, ny)), out_shape=[jax...  70.7 us
    pallas_call x1, Pallas kernels, sparse_near(): pl.pallas_call(sparse_kernel, out_shape=jax.ShapeDtypeStruct((2, SIDE + 2...  52.4 us
    ppermute x4, starting transfers between devices, with_halo(): lax.ppermute(lax.slice_in_dim(shard, length - size, length, axis=dim), ax...  16.5 us
    pallas_call x1, Pallas kernels, to_block_table(): pl.pallas_call(block_kernel, out_shape=jax.ShapeDtypeStruct((NB * NB * 4,...  9.98 us
    ppermute x4, starting transfers between devices, with_halo(): after = lax.ppermute(lax.slice_in_dim(shard, 0, size, axis=dim), axis, down)  6.56 us
  transfers between devices with their start and end apart: 8, of which 2 were waited for; matrix products, arithmetic and copies ran while one was open for 6% of the time, Pallas kernels for 3%

profile of v2, /device:TPU:1, one launch (start us, length us, event | category | flops | bytes accessed | tf_op | source)
XLA Modules:
  0.0 286.4 jit_solution(10642042892914790334)
XLA Ops:
  0.6 0.0 copy-start.1
  0.6 1.5 fusion.22
  2.1 3.9 %collective-permute-start = (f32[1,512]{1,0:T(1,128)}, f32[1,512]{1,0:T(1,128)S(1)}, u32[]{:S(2)}, u32[]{:S(2)}) collective-permute-start(f32[1,512]{1,0:T(1,128)} %get-tuple-element.27), channel_id=1, source_target_pairs={{0,16},{16,32},{32,48},{48,64},{64,80},{80,96},{96,112},{1,17},{17... | collective-permute-start | bytes 6152 | tf_op jit(solution)/shard_map/ppermute | solution.py:361
  6.1 1.3 collective-permute-start.1
  7.4 10.0 %to_blocks.1 = bf16[4096,128]{1,0:T(8,128)(2,1)} custom-call(bf16[2,512,512]{2,1,0:T(8,128)(2,1)} %far_ref.1), custom_call_target="tpu_custom_call" | custom-call | tf_op jit(solution)/shard_map/to_blocks/pallas_call | solution.py:58
  17.3 2.1 fusion.21
  19.4 4.0 %collective-permute-start.4 = (bf16[12,8,16,128]{3,2,1,0:T(8,128)(2,1)}, bf16[12,8,16,128]{3,2,1,0:T(8,128)(2,1)S(1)}, u32[]{:S(2)}, u32[]{:S(2)}) collective-permute-start(bf16[12,8,16,128]{3,2,1,0:T(8,128)(2,1)} %bitcast.6), channel_id=1, source_target_pairs={{0,16},{16,32},{32,48},{48,64},{64,80},{80,96},{96,112},{1,17},{17... | collective-permute-start | bytes 1179656 | tf_op jit(solution)/shard_map/ppermute | solution.py:361
  23.4 0.0 copy-start.3
  23.4 1.4 collective-permute-start.5
  24.9 1.5 slice_bitcast_fusion.3
  26.4 0.1 fusion.20
  26.4 0.0 copy-done.3
  26.4 0.7 broadcast_multiply_fusion
  27.3 0.7 reduce-precision_bitcast_fusion.1
  28.0 0.7 broadcast_multiply_fusion.1
  28.7 0.0 copy-start.2
  28.7 3.9 %maximum_maximum_fusion.green_ref = bf16[8,512,512]{2,1,0:T(8,128)(2,1)} fusion(bf16[8,256,256]{2,1,0:T(8,128)(2,1)} %get-tuple-element.17, bf16[8,256,256]{2,1,0:T(8,128)(2,1)} %get-tuple-element.16, bf16[8,256,256]{2,1,0:T(8,128)(2,1)S(1)} %fusion.20), kind=kLoop, calls=%fused_computation | loop fusion | flops 16777216 | bytes 7340032 | tf_op jit(solution)/shard_map/concatenate | solution.py:374
  32.6 0.1 select_maximum_fusion.3
  32.7 0.1 copy.20
  32.8 0.7 fusion.14.w1_ref
  33.5 0.0 collective-permute-done
  33.5 0.0 collective-permute-done.1
  33.5 0.1 pad_maximum_fusion.7
  33.7 4.9 %collective-permute-start.2 = (f32[514,1]{1,0:T(8,128)S(1)}, f32[514,1]{1,0:T(8,128)S(1)}, u32[]{:S(2)}, u32[]{:S(2)}) collective-permute-start(f32[514,1]{1,0:T(8,128)S(1)} %get-tuple-element.23), channel_id=1, source_target_pairs={{0,1},{1,2},{2,3},{3,4},{4,5},{5,6},{6,7},{7,8},{8,9},{9,10},{10,1... | collective-permute-start | bytes 6176 | tf_op jit(solution)/shard_map/ppermute | solution.py:361
  38.6 1.9 collective-permute-start.3
  40.6 0.0 collective-permute-done.4
  40.6 0.0 collective-permute-done.5
  40.6 1.2 pad_maximum_fusion.4
  41.8 3.6 %collective-permute-start.6 = (bf16[56,3,16,128]{3,2,1,0:T(8,128)(2,1)S(1)}, bf16[56,3,16,128]{3,2,1,0:T(8,128)(2,1)S(1)}, u32[]{:S(2)}, u32[]{:S(2)}) collective-permute-start(bf16[56,3,16,128]{3,2,1,0:T(8,128)(2,1)S(1)} %get-tuple-element.18), channel_id=1, source_target_pairs={{0,1},{1,2},{2,3},{3,4},{4,5},{5,6},{6,7},{7,8},{8,9},{9,10},{10,1... | collective-permute-start | bytes 2064392 | tf_op jit(solution)/shard_map/ppermute | solution.py:361
  45.4 1.9 collective-permute-start.7
  47.3 0.6 fusion.16.v_ref
  48.0 0.6 pad.55.wout_ref
  48.5 0.0 collective-permute-done.2
  48.5 0.0 collective-permute-done.3
  48.6 0.5 select_maximum_fusion
  49.1 0.7 slice_bitcast_fusion.2
  49.7 2.1 pad_maximum_fusion.1.p3_ref
  51.8 1.4 collective-permute-done.6
  53.3 4.4 %collective-permute-done.7 = bf16[56,3,16,128]{3,2,1,0:T(8,128)(2,1)S(1)} collective-permute-done((bf16[56,3,16,128]{3,2,1,0:T(8,128)(2,1)S(1)}, bf16[56,3,16,128]{3,2,1,0:T(8,128)(2,1)S(1)}, u32[]{:S(2)}, u32[]{:S(2)}) %collective-permute-start.7) | collective-permute-done | bytes 688160 | tf_op jit(solution)/shard_map/ppermute | solution.py:364
  57.7 2.9 %pad_maximum_fusion = bf16[56,14,16,128]{3,2,1,0:T(8,128)(2,1)} fusion(bf16[56,3,16,128]{3,2,1,0:T(8,128)(2,1)S(1)} %collective-permute-done.7, bf16[12,8,16,128]{3,2,1,0:T(8,128)(2,1)} %collective-permute-done.5, bf16[32,8,16,128]{3,2,1,0:T(8,128)(2,1)S(1)} %bitcast.42, bf16[12,8,16,128]{3,2,1,0:T(8,128)(2,1)S(1)} %collective-permute-done.4, ...), kind=kLoop, calls=%fused_computation.1 | loop fusion | flops 6422528 | bytes 6422528 | tf_op jit(solution)/shard_map/concatenate | solution.py:365
  60.6 52.4 %sparse_near.1.near_ref = f32[2,544,512]{2,1,0:T(8,128)} custom-call(s32[24576]{0:T(1024)} %bitcast.44, s32[8]{0:T(128)} %bitcast.48, s32[48,1,512]{2,1,0:T(1,128)} %bitcast.45, bf16[12544,128]{1,0:T(8,128)(2,1)} %bitcast.43, bf16[8,512,512]{2,1,0:T(8,128)(2,1)} %maximum_maximum_fusion.green_ref), custom_call_target="tpu_custom_call" | custom-call | tf_op jit(solution)/shard_map/sparse_near/pallas_call | solution.py:151
  113.0 96.7 %cell_model.1 = (f32[528,512]{1,0:T(8,128)}, f32[528,128]{1,0:T(8,128)}, f32[528,128]{1,0:T(8,128)}, f32[16,128]{1,0:T(8,128)}) custom-call(f32[3,520,512]{2,1,0:T(8,128)} %pad_maximum_fusion.1.p3_ref, f32[2,544,512]{2,1,0:T(8,128)} %sparse_near.1.near_ref, bf16[256,96]{1,0:T(8,128)(2,1)} %fusion.14.w1_ref, bf16[96,256]{1,0:T(8,128)(2,1)} %fusion.16.v_ref, ...), custom_call_target="tpu_custom_call" | custom-call | tf_op jit(solution)/shard_map/cell_model/pallas_call | solution.py:328
  209.7 70.7 %finish.1 = (f32[512,512]{1,0:T(8,128)}, f32[16,128]{1,0:T(8,128)}) custom-call(f32[528,512]{1,0:T(8,128)} %get-tuple-element.10.grad_ref, f32[528,128]{1,0:T(8,128)} %get-tuple-element.11.west_ref, f32[528,128]{1,0:T(8,128)} %get-tuple-element.12.east_ref, f32[16,128]{1,0:T(8,128)} %get-tuple-element.13.msg_ref), custom_call_target="tpu_custom_call" | custom-call | tf_op jit(solution)/shard_map/finish/pallas_call | solution.py:601
  280.3 1.3 slice_bitcast_fusion.5
  281.6 0.7 slice_reduce_fusion
  282.3 1.2 slice_bitcast_fusion.6
  283.5 0.6 reshape_squeeze.3
  284.2 2.3 copy.31
  (22 shorter events, 0.2 us)
Async XLA Ops:
  0.6 24.2 %copy-start.1 = (bf16[8,2,256,256]{3,2,1,0:T(8,128)(2,1)S(1)}, bf16[8,2,256,256]{3,2,1,0:T(8,128)(2,1)}, u32[]{:S(2)}) copy-start(bf16[8,2,256,256]{3,2,1,0:T(8,128)(2,1)} %param.11) | copy-start | bytes 6291460
  2.1 31.4 %collective-permute-start = (f32[1,512]{1,0:T(1,128)}, f32[1,512]{1,0:T(1,128)S(1)}, u32[]{:S(2)}, u32[]{:S(2)}) collective-permute-start(f32[1,512]{1,0:T(1,128)} %get-tuple-element.27), channel_id=1, source_target_pairs={{0,16},{16,32},{32,48},{48,64},{64,80},{80,96},{96,112},{1,17},{17... | collective-permute-start | bytes 6152 | tf_op jit(solution)/shard_map/ppermute | solution.py:361
  6.1 27.5 %collective-permute-start.1 = (f32[1,512]{1,0:T(1,128)}, f32[1,512]{1,0:T(1,128)S(1)}, u32[]{:S(2)}, u32[]{:S(2)}) collective-permute-start(f32[1,512]{1,0:T(1,128)} %get-tuple-element.28), channel_id=1, source_target_pairs={{16,0},{32,16},{48,32},{64,48},{80,64},{96,80},{112,96},{17,1},{33... | collective-permute-start | bytes 6152 | tf_op jit(solution)/shard_map/ppermute | solution.py:364
  19.4 21.2 %collective-permute-start.4 = (bf16[12,8,16,128]{3,2,1,0:T(8,128)(2,1)}, bf16[12,8,16,128]{3,2,1,0:T(8,128)(2,1)S(1)}, u32[]{:S(2)}, u32[]{:S(2)}) collective-permute-start(bf16[12,8,16,128]{3,2,1,0:T(8,128)(2,1)} %bitcast.6), channel_id=1, source_target_pairs={{0,16},{16,32},{32,48},{48,64},{64,80},{80,96},{96,112},{1,17},{17... | collective-permute-start | bytes 1179656 | tf_op jit(solution)/shard_map/ppermute | solution.py:361
  23.4 3.0 %copy-start.3 = (s32[1,1,24576]{2,1,0:T(1,128)S(1)}, s32[1,1,24576]{2,1,0:T(1,128)}, u32[]{:S(2)}) copy-start(s32[1,1,24576]{2,1,0:T(1,128)} %param.13) | copy-start | bytes 294916
  23.4 17.1 %collective-permute-start.5 = (bf16[12,8,16,128]{3,2,1,0:T(8,128)(2,1)}, bf16[12,8,16,128]{3,2,1,0:T(8,128)(2,1)}, u32[]{:S(2)}, u32[]{:S(2)}) collective-permute-start(bf16[12,8,16,128]{3,2,1,0:T(8,128)(2,1)} %bitcast.8), channel_id=1, source_target_pairs={{16,0},{32,16},{48,32},{64,48},{80,64},{96,80},{112,96},{17,1},{33... | collective-permute-start | bytes 1179656 | tf_op jit(solution)/shard_map/ppermute | solution.py:364
  26.4 0.8 copy-start.4
  28.7 4.9 %copy-start.2 = (f32[512,512]{1,0:T(8,128)S(1)}, f32[512,512]{1,0:T(8,128)}, u32[]{:S(2)}) copy-start(f32[512,512]{1,0:T(8,128)} %param.10) | copy-start | bytes 3145732
  32.6 8.0 %copy-start = (bf16[4096,128]{1,0:T(8,128)(2,1)S(1)}, bf16[4096,128]{1,0:T(8,128)(2,1)}, u32[]{:S(2)}) copy-start(bf16[4096,128]{1,0:T(8,128)(2,1)} %to_blocks.1) | copy-start | bytes 3145732
  33.5 14.5 %copy-start.5 = (f32[2,64]{1,0:T(2,128)S(1)}, f32[2,64]{1,0:T(2,128)}, u32[]{:S(2)}) copy-start(f32[2,64]{1,0:T(2,128)} %param.17) | copy-start | bytes 1540
  33.7 14.9 %collective-permute-start.2 = (f32[514,1]{1,0:T(8,128)S(1)}, f32[514,1]{1,0:T(8,128)S(1)}, u32[]{:S(2)}, u32[]{:S(2)}) collective-permute-start(f32[514,1]{1,0:T(8,128)S(1)} %get-tuple-element.23), channel_id=1, source_target_pairs={{0,1},{1,2},{2,3},{3,4},{4,5},{5,6},{6,7},{7,8},{8,9},{9,10},{10,1... | collective-permute-start | bytes 6176 | tf_op jit(solution)/shard_map/ppermute | solution.py:361
  38.6 9.9 %collective-permute-start.3 = (f32[514,1]{1,0:T(8,128)S(1)}, f32[514,1]{1,0:T(8,128)S(1)}, u32[]{:S(2)}, u32[]{:S(2)}) collective-permute-start(f32[514,1]{1,0:T(8,128)S(1)} %get-tuple-element.24), channel_id=1, source_target_pairs={{1,0},{2,1},{3,2},{4,3},{5,4},{6,5},{7,6},{8,7},{9,8},{10,9},{11,1... | collective-permute-start | bytes 6176 | tf_op jit(solution)/shard_map/ppermute | solution.py:364
  41.8 11.5 %collective-permute-start.6 = (bf16[56,3,16,128]{3,2,1,0:T(8,128)(2,1)S(1)}, bf16[56,3,16,128]{3,2,1,0:T(8,128)(2,1)S(1)}, u32[]{:S(2)}, u32[]{:S(2)}) collective-permute-start(bf16[56,3,16,128]{3,2,1,0:T(8,128)(2,1)S(1)} %get-tuple-element.18), channel_id=1, source_target_pairs={{0,1},{1,2},{2,3},{3,4},{4,5},{5,6},{6,7},{7,8},{8,9},{9,10},{10,1... | collective-permute-start | bytes 2064392 | tf_op jit(solution)/shard_map/ppermute | solution.py:361
  45.4 12.3 %collective-permute-start.7 = (bf16[56,3,16,128]{3,2,1,0:T(8,128)(2,1)S(1)}, bf16[56,3,16,128]{3,2,1,0:T(8,128)(2,1)S(1)}, u32[]{:S(2)}, u32[]{:S(2)}) collective-permute-start(bf16[56,3,16,128]{3,2,1,0:T(8,128)(2,1)S(1)} %get-tuple-element.19), channel_id=1, source_target_pairs={{1,0},{2,1},{3,2},{4,3},{5,4},{6,5},{7,6},{8,7},{9,8},{10,9},{11,1... | collective-permute-start | bytes 2064392 | tf_op jit(solution)/shard_map/ppermute | solution.py:364

commit v3 on v2

--- a/solution.py
+++ b/solution.py
@@ -14,7 +14,7 @@
 EXT = NB + 2 * CONE
 GROUPS = 8
 CHUNK = 512
-UNROLL = 32
+PARTS = 1
 HIDDEN = 64
 PADROWS = 16
 SROWS = 24
@@ -25,50 +25,26 @@
 MESH = pl.DeviceIdType.MESH
 
 
-def swap_pieces(v):
-    sub = lax.broadcasted_iota(jnp.int32, (8, 128), 0)
+def swap_pieces(vectors):
     lane = lax.broadcasted_iota(jnp.int32, (8, 128), 1) // 16
     for d in (1, 2, 4):
-        low_s = (sub & d) == 0
-        low_l = (lane & d) == 0
-        up = pltpu.roll(pltpu.roll(v, 8 - d, 0), 16 * d, 1)
-        if d == 4:
-            down = up
-        else:
-            down = pltpu.roll(pltpu.roll(v, d, 0), 128 - 16 * d, 1)
-        v = jnp.where(low_s == low_l, v, jnp.where(low_s, up, down))
-    return v
-
-
-def block_kernel(far_ref, out_ref, flat):
-    def row(r, carry):
-        for c in range(2):
-            strip = far_ref[c, pl.ds(pl.multiple_of(r * BLK, BLK), BLK), :].astype(f32)
-            for xh in range(2):
-                for t in range(SIDE // 128):
-                    v = swap_pieces(strip[8 * xh : 8 * xh + 8, 128 * t : 128 * t + 128])
-                    flat[pl.ds(32 * t + 2 * c + xh, 8, stride=4), :] = v
-        out_ref[pl.ds(pl.multiple_of(r * 128, 128), 128), :] = flat[...].astype(bf16)
-        return carry
-
-    lax.fori_loop(0, NB, row, 0)
-
-
-def to_block_table(far):
-    return pl.pallas_call(
-        block_kernel,
-        out_shape=jax.ShapeDtypeStruct((NB * NB * 4, 128), bf16),
-        in_specs=[pl.BlockSpec(memory_space=pltpu.VMEM)],
-        out_specs=pl.BlockSpec(memory_space=pltpu.VMEM),
-        scratch_shapes=[pltpu.VMEM((128, 128), f32)],
-        compiler_params=pltpu.CompilerParams(vmem_limit_bytes=VMEM_BYTES),
-        name="to_blocks",
-    )(far)
+        mixed = []
+        for x in range(8):
+            if x & d:
+                moved = pltpu.roll(vectors[x ^ d], 128 - 16 * d, 1)
+                mixed.append(jnp.where((lane & d) == 0, moved, vectors[x]))
+            else:
+                moved = pltpu.roll(vectors[x ^ d], 16 * d, 1)
+                mixed.append(jnp.where((lane & d) == 0, vectors[x], moved))
+        vectors = mixed
+    return vectors
 
 
 def sparse_kernel(
-    dst_ref, ends_ref, src_ref, ext_ref, green_ref, near_ref, table, rows, rows16, seg, acc
+    dst_ref, ends_ref, src_ref, ext_ref, green_ref, near_ref, table, rows, rows16, stack, seg, acc
 ):
+    chunks = dst_ref.shape[0] // CHUNK
+
     def widen(i, carry):
         at = pl.ds(pl.multiple_of(i * 128, 128), 128)
         table[at, :] = ext_ref[at, :].astype(f32)
@@ -76,6 +52,20 @@
 
     lax.fori_loop(0, EXT * EXT * 4 // 128, widen, 0)
     acc[...] = jnp.zeros_like(acc)
+
+    def gather(base, first, count):
+        for q in range(first, first + count):
+            d = pl.multiple_of(dst_ref[base + q], 4)
+            rows[4 * q : 4 * q + 4, :] = table[pl.ds(d, 4), :]
+
+    def narrow():
+        for j in range(4):
+            rows16[:, 128 * j : 128 * j + 128] = rows[
+                pl.ds(j, CHUNK, stride=4), :
+            ].astype(bf16)
+
+    gather(0, 0, CHUNK)
+    narrow()
 
     def group(k, carry):
         start = jnp.where(k == 0, 0, ends_ref[jnp.maximum(k - 1, 0)])
@@ -83,74 +73,73 @@
         seg[...] = jnp.zeros_like(seg)
 
         def chunk(c, inner):
-            base = c * CHUNK
-
-            def gather(i, deep):
-                for j in range(UNROLL):
-                    q = i * UNROLL + j
-                    d = pl.multiple_of(dst_ref[base + q], 4)
-                    rows[pl.ds(pl.multiple_of(q * 4, 4), 4), :] = table[pl.ds(d, 4), :]
-                return deep
-
-            lax.fori_loop(0, CHUNK // UNROLL, gather, 0)
-            for j in range(4):
-                rows16[:, 128 * j : 128 * j + 128] = rows[
-                    pl.ds(j, CHUNK, stride=4), :
-                ].astype(bf16)
-            slot = base + lax.broadcasted_iota(jnp.int32, (1, CHUNK), 1)
+            ahead = jnp.minimum(c + 1, chunks - 1) * CHUNK
+            slot = c * CHUNK + lax.broadcasted_iota(jnp.int32, (1, CHUNK), 1)
             live = (slot >= start) & (slot < stop)
             source = jnp.where(live, src_ref[c], -1)
-            for m in range(4):
-                ids = lax.broadcasted_iota(jnp.int32, (256, CHUNK), 0) + 256 * m
+            for m in range(PARTS):
+                size = NB * NB // PARTS
+                ids = lax.broadcasted_iota(jnp.int32, (size, CHUNK), 0) + size * m
                 hot = jnp.where(ids == source, 1.0, 0.0).astype(bf16)
-                seg[256 * m : 256 * m + 256, :] += jnp.dot(
+                gather(ahead, CHUNK // PARTS * m, CHUNK // PARTS)
+                seg[size * m : size * m + size, :] += jnp.dot(
                     hot, rows16[...], preferred_element_type=f32
                 )
+            pl.when((c + 1) * CHUNK <= stop)(narrow)
             return inner
 
         lax.fori_loop(start // CHUNK, (stop + CHUNK - 1) // CHUNK, chunk, 0)
 
+        half = BLK * BLK
+        real = green_ref[k, 0]
+        imag = green_ref[k, 1]
+        stack[0:half, 0:half] = real
+        stack[0:half, half : 2 * half] = -imag
+        stack[half : 2 * half, 0:half] = imag
+        stack[half : 2 * half, half : 2 * half] = real
+
         def apply(m, inner):
-            at = pl.ds(pl.multiple_of(m * 256, 256), 256)
+            at = pl.ds(pl.multiple_of(m * 512, 512), 512)
             value = seg[at, :]
             high = value.astype(bf16)
             low = (value - high.astype(f32)).astype(bf16)
-            acc[at, :] += jnp.dot(high, green_ref[k], preferred_element_type=f32) + jnp.dot(
-                low, green_ref[k], preferred_element_type=f32
+            near = jnp.dot(high, stack[...], preferred_element_type=f32) + jnp.dot(
+                low, stack[...], preferred_element_type=f32
             )
+            for j in range(4):
+                acc[j, at, :] += near[:, 128 * j : 128 * j + 128]
             return inner
 
-        lax.fori_loop(0, 4, apply, 0)
+        lax.fori_loop(0, 2, apply, 0)
         return carry
 
     lax.fori_loop(0, GROUPS, group, 0)
 
-    def lay(r, carry):
-        for t in range(SIDE // 128):
-            for c in range(2):
-                for xh in range(2):
-                    j = 2 * c + xh
-                    v = acc[
-                        pl.ds(pl.multiple_of(r * 32 + 8 * t, 8), 8), 128 * j : 128 * j + 128
-                    ]
-                    near_ref[
-                        c,
-                        pl.ds(pl.multiple_of(r * 16 + 8 * xh + PADROWS, 8), 8),
-                        128 * t : 128 * t + 128,
-                    ] = swap_pieces(v)
-        return carry
-
-    lax.fori_loop(0, NB, lay, 0)
+    def lay(i, carry):
+        for j in range(4):
+            for t in range(SIDE // 128):
+                vectors = [
+                    acc[j, pl.ds(i * 256 + 8 * t + b, 8, stride=NB), :] for b in range(8)
+                ]
+                for x, v in enumerate(swap_pieces(vectors)):
+                    at = pl.ds(PADROWS + i * 128 + 8 * (j % 2) + x, 8, stride=BLK)
+                    near_ref[j // 2, t, at, :] = v
+        return carry
+
+    lax.fori_loop(0, NB // 8, lay, 0)
     for c in range(2):
-        near_ref[c, 0:PADROWS, :] = jnp.zeros((PADROWS, SIDE), f32)
-        near_ref[c, PADROWS + SIDE : 2 * PADROWS + SIDE, :] = jnp.zeros((PADROWS, SIDE), f32)
-
-
-def sparse_near(targets, ends, sources, ext, stacks):
+        for t in range(4):
+            near_ref[c, t, 0:PADROWS, :] = jnp.zeros((PADROWS, 128), f32)
+            near_ref[c, t, PADROWS + SIDE : 2 * PADROWS + SIDE, :] = jnp.zeros(
+                (PADROWS, 128), f32
+            )
+
+
+def sparse_near(targets, ends, sources, ext, green):
     slots = targets.shape[0]
     return pl.pallas_call(
         sparse_kernel,
-        out_shape=jax.ShapeDtypeStruct((2, SIDE + 2 * PADROWS, SIDE), f32),
+        out_shape=jax.ShapeDtypeStruct((2, 4, SIDE + 2 * PADROWS, 128), f32),
         in_specs=[
             pl.BlockSpec(memory_space=pltpu.SMEM),
             pl.BlockSpec(memory_space=pltpu.SMEM),
@@ -163,12 +152,19 @@
             pltpu.VMEM((EXT * EXT * 4, 128), f32),
             pltpu.VMEM((CHUNK * 4, 128), f32),
             pltpu.VMEM((CHUNK, 512), bf16),
+            pltpu.VMEM((512, 512), bf16),
             pltpu.VMEM((NB * NB, 512), f32),
-            pltpu.VMEM((NB * NB, 512), f32),
+            pltpu.VMEM((4, NB * NB, 128), f32),
         ],
         compiler_params=pltpu.CompilerParams(vmem_limit_bytes=VMEM_BYTES),
         name="sparse_near",
-    )(targets * 4, ends, sources.reshape(slots // CHUNK, 1, CHUNK), ext, stacks)
+    )(
+        jnp.clip(targets, 0, EXT * EXT - 1) * 4,
+        ends,
+        sources.reshape(slots // CHUNK, 1, CHUNK),
+        ext,
+        green,
+    )
 
 
 def split2(value):
@@ -205,6 +201,10 @@
 ):
     width = SIDE
 
+    def near_rows(c, first, count):
+        at = pl.ds(pl.multiple_of(first, 8), count)
+        return jnp.concatenate([near_ref[c, t, at, :] for t in range(4)], 1)
+
     def build(i, carry):
         r0 = pl.multiple_of(i * 8, 8)
         for b in range(3):
@@ -220,7 +220,7 @@
             )
         return carry
 
-    lax.fori_loop(0, (SIDE + 8) // 8, build, 0)
+    lax.fori_loop(0, (SIDE + 16) // 8, build, 0)
     total[...] = jnp.zeros_like(total)
     nh[...] = jnp.zeros_like(nh)
     gs[...] = jnp.zeros_like(gs)
@@ -231,11 +231,11 @@
 
     def strip(i, carry):
         r0 = pl.multiple_of(i * 8, 8)
-        n = [near_ref[c, pl.ds(pl.multiple_of(r0 + PADROWS, 8), 8), :] for c in range(2)]
-        deep = [p3_ref[b, pl.ds(r0, 16), :] for b in range(3)]
+        n = [near_rows(c, r0 + PADROWS, 8) for c in range(2)]
+        deep = [p3_ref[b, pl.ds(r0, 24), :] for b in range(3)]
         for a in range(3):
             for b in range(3):
-                feat = deep[b][a : a + 8]
+                feat = deep[b][7 + a : 15 + a]
                 for c in range(2):
                     put(gs, 10 * c + 3 * a + b, SROWS, n[c] * feat)
         for c in range(2):
@@ -243,7 +243,7 @@
         for half in range(2):
             left, right = [], []
             partial = [None, None]
-            feats = qs[pl.ds(r0 + 4 * half, 6)].reshape(96, width)
+            feats = qs[pl.ds(r0 + 4 * half + 7, 6)].reshape(96, width)
             h = jnp.tanh(jnp.dot(w1_ref[...], feats, preferred_element_type=f32))
             for pair in range(2):
                 pieces = []
@@ -301,7 +301,7 @@
 
     def combine(i, carry):
         parts = []
-        deep = [near_ref[c, pl.ds(pl.multiple_of(i * 8, 8), 24), :] for c in range(2)]
+        deep = [near_rows(c, i * 8, 24) for c in range(2)]
         for b in range(3):
             acc = None
             for a in range(3):
@@ -337,7 +337,7 @@
         out_specs=[pl.BlockSpec(memory_space=pltpu.VMEM)] * 4,
         scratch_shapes=[
             pltpu.VMEM((4, 128, 128), f32),
-            pltpu.VMEM((SIDE + 8, 16, SIDE), bf16),
+            pltpu.VMEM((SIDE + 16, 16, SIDE), bf16),
             pltpu.VMEM((4, 8 * SROWS, 128), f32),
             pltpu.VMEM((4, (SIDE + 2 * PADROWS) * SROWS, 128), f32),
             pltpu.VMEM((128, 128), f32),
@@ -348,30 +348,200 @@
     )(p3, near, first, back, out_weights)
 
 
-def neighbours(axis):
-    count = lax.axis_size(axis)
-    up = [(i, i + 1) for i in range(count - 1)]
-    return up, [(j, i) for i, j in up]
-
-
-def with_halo(shard, sides):
-    for axis, dim, size in sides:
-        up, down = neighbours(axis)
-        length = shard.shape[dim]
-        before = lax.ppermute(
-            lax.slice_in_dim(shard, length - size, length, axis=dim), axis, up
+AROUND = [(dx, dy) for dx in (-1, 0, 1) for dy in (-1, 0, 1) if (dx, dy) != (0, 0)]
+
+
+def front_kernel(
+    shape, far_ref, pillar_ref, ext_ref, p3_ref, field, flat, edge_in, turned, side, sends, recvs
+):
+    nx, ny = shape
+    tx = lax.axis_index("tx")
+    ty = lax.axis_index("ty")
+    barrier = pltpu.get_barrier_semaphore()
+    for dx, dy in AROUND:
+        pl.semaphore_signal(
+            barrier,
+            inc=1,
+            device_id=(lax.rem(tx + dx + nx, nx), lax.rem(ty + dy + ny, ny)),
+            device_id_type=MESH,
         )
-        after = lax.ppermute(lax.slice_in_dim(shard, 0, size, axis=dim), axis, down)
-        shard = jnp.concatenate([before, shard, after], axis=dim)
-    return shard
-
-
-def green_stack(green_table):
-    real_part = green_table[:, 0]
-    imag_part = green_table[:, 1]
-    upper_half = jnp.concatenate([real_part, -imag_part], axis=2)
-    lower_half = jnp.concatenate([imag_part, real_part], axis=2)
-    return jnp.concatenate([upper_half, lower_half], axis=1)
+
+    for q in range(4):
+        tile = slice(128 * q, 128 * q + 128)
+        turned[0, :, tile] = pillar_ref[tile, 0:128].T[0:8]
+        turned[1, :, tile] = pillar_ref[tile, SIDE - 128 : SIDE].T[120:128]
+    pl.semaphore_wait(barrier, len(AROUND))
+
+    def there(dx, dy):
+        fits = None
+        for delta, index, count in ((dx, tx, nx), (dy, ty, ny)):
+            if delta:
+                one = index > 0 if delta < 0 else index < count - 1
+                fits = one if fits is None else jnp.logical_and(fits, one)
+        return fits
+
+    def rim(delta, length, reach):
+        if delta < 0:
+            return (0, reach), (length, reach)
+        if delta > 0:
+            return (length - reach, reach), (-reach, reach)
+        return (0, length), (0, length)
+
+    def far_copy(n):
+        dx, dy = AROUND[n]
+        (x, wx), (ox, _) = rim(dx, NB, CONE)
+        (y, wy), (oy, _) = rim(dy, NB // 4, CONE // 4)
+        return pltpu.make_async_remote_copy(
+            src_ref=ext_ref.at[pl.ds(CONE + x, wx), pl.ds(CONE // 4 + y, wy)],
+            dst_ref=ext_ref.at[pl.ds(CONE + ox, wx), pl.ds(CONE // 4 + oy, wy)],
+            send_sem=sends.at[n],
+            recv_sem=recvs.at[n],
+            device_id=(tx + dx, ty + dy),
+            device_id_type=MESH,
+        )
+
+    def edge_copy(n):
+        dx, dy = AROUND[n]
+        if dy == 0:
+            source = pillar_ref.at[pl.ds(0 if dx < 0 else SIDE - 8, 8), :]
+        elif dx == 0:
+            source = turned.at[0 if dy < 0 else 1]
+        else:
+            source = pillar_ref.at[
+                pl.ds(0 if dx < 0 else SIDE - 8, 8), pl.ds(0 if dy < 0 else SIDE - 128, 128)
+            ]
+        wide = SIDE if dx == 0 or dy == 0 else 128
+        return pltpu.make_async_remote_copy(
+            src_ref=source,
+            dst_ref=edge_in.at[n, :, pl.ds(0, wide)],
+            send_sem=sends.at[8 + n],
+            recv_sem=recvs.at[8 + n],
+            device_id=(tx + dx, ty + dy),
+            device_id_type=MESH,
+        )
+
+    for n, (dx, dy) in enumerate(AROUND):
+        pl.when(there(dx, dy))(lambda n=n: edge_copy(n).start())
+
+    def spread(i, carry):
+        at = pl.ds(pl.multiple_of(i * BLK, BLK), BLK)
+        for c in range(2):
+            strip = far_ref[c, at, :].astype(f32)
+            for t in range(4):
+                field[c, t, at, :] = strip[:, 128 * t : 128 * t + 128]
+        return carry
+
+    lax.fori_loop(0, SIDE // BLK, spread, 0)
+
+    def turn(i, carry):
+        for j in range(4):
+            for t in range(4):
+                first = i * 128 + 8 * (j % 2)
+                vectors = [
+                    field[j // 2, t, pl.ds(first + x, 8, stride=BLK), :] for x in range(8)
+                ]
+                for b, v in enumerate(swap_pieces(vectors)):
+                    flat[pl.ds(i * 1024 + (8 * t + b) * 4 + j, 8, stride=128), :] = v
+        return carry
+
+    lax.fori_loop(0, NB // 8, turn, 0)
+
+    def pack(r, carry):
+        value = flat[pl.ds(pl.multiple_of(r * 128, 128), 128), :].astype(bf16)
+        ext_ref[CONE + r, CONE // 4 : CONE // 4 + NB // 4] = value.reshape(NB // 4, 16, 128)
+        return carry
+
+    lax.fori_loop(0, NB, pack, 0)
+    for n, (dx, dy) in enumerate(AROUND):
+        pl.when(there(dx, dy))(lambda n=n: far_copy(n).start())
+
+    for n, (dx, dy) in enumerate(AROUND):
+
+        @pl.when(jnp.logical_not(there(dx, dy)))
+        def _(n=n, dx=dx, dy=dy):
+            edge_in[7 - n] = jnp.zeros((8, SIDE), f32)
+            x = {-1: 0, 0: CONE, 1: CONE + NB}[dx]
+            y = {-1: 0, 0: CONE // 4, 1: (CONE + NB) // 4}[dy]
+            wy = CONE // 4 if dy else NB // 4
+
+            def clear(i, carry):
+                ext_ref[x + i, y : y + wy] = jnp.zeros((wy, 16, 128), bf16)
+                return carry
+
+            lax.fori_loop(0, CONE if dx else NB, clear, 0)
+
+    for n, (dx, dy) in enumerate(AROUND):
+        pl.when(there(dx, dy))(lambda n=n: edge_copy(7 - n).wait_recv())
+    at_of = {place: n for n, place in enumerate(AROUND)}
+
+    def got(dx, dy):
+        return edge_in.at[7 - at_of[(dx, dy)]]
+
+    for s, dy in ((0, -1), (1, 1)):
+        lane = 127 if s == 0 else 0
+        side[s, 0:8, :] = jnp.broadcast_to(got(-1, dy)[:, lane : lane + 1], (8, 128))
+        side[s, SIDE + 8 : SIDE + 16, :] = jnp.broadcast_to(
+            got(1, dy)[:, lane : lane + 1], (8, 128)
+        )
+        row = 7 if s == 0 else 0
+        for q in range(4):
+            tile = slice(128 * q, 128 * q + 128)
+            side[s, 8 + 128 * q : 136 + 128 * q, :] = jnp.broadcast_to(
+                got(0, dy)[row : row + 1, tile], (128, 128)
+            ).T
+
+    lanes = lax.broadcasted_iota(jnp.int32, (8, SIDE), 1)
+
+    def shifted(at, value):
+        p3_ref[1, at, :] = value
+        west = jnp.concatenate([side[0, at, :]] * 4, 1)
+        east = jnp.concatenate([side[1, at, :]] * 4, 1)
+        p3_ref[0, at, :] = jnp.where(lanes == 0, west, pltpu.roll(value, 1, 1))
+        p3_ref[2, at, :] = jnp.where(lanes == SIDE - 1, east, pltpu.roll(value, SIDE - 1, 1))
+
+    def interior(i, carry):
+        r0 = pl.multiple_of(i * 8, 8)
+        shifted(pl.ds(r0 + 8, 8), pillar_ref[pl.ds(r0, 8), :])
+        return carry
+
+    lax.fori_loop(0, SIDE // 8, interior, 0)
+    shifted(pl.ds(0, 8), got(-1, 0)[...])
+    shifted(pl.ds(SIDE + 8, 8), got(1, 0)[...])
+
+    for n, (dx, dy) in enumerate(AROUND):
+        pl.when(there(dx, dy))(lambda n=n: far_copy(7 - n).wait_recv())
+    for n, (dx, dy) in enumerate(AROUND):
+
+        @pl.when(there(dx, dy))
+        def _(n=n):
+            far_copy(n).wait_send()
+            edge_copy(n).wait_send()
+
+
+def front(far, pillar):
+    nx, ny = lax.axis_size("tx"), lax.axis_size("ty")
+    return pl.pallas_call(
+        functools.partial(front_kernel, (nx, ny)),
+        out_shape=[
+            jax.ShapeDtypeStruct((EXT, EXT // 4, 16, 128), bf16),
+            jax.ShapeDtypeStruct((3, SIDE + 16, SIDE), f32),
+        ],
+        in_specs=[pl.BlockSpec(memory_space=pltpu.VMEM)] * 2,
+        out_specs=[pl.BlockSpec(memory_space=pltpu.VMEM)] * 2,
+        scratch_shapes=[
+            pltpu.VMEM((2, 4, SIDE, 128), f32),
+            pltpu.VMEM((NB * NB * 4, 128), f32),
+            pltpu.VMEM((8, 8, SIDE), f32),
+            pltpu.VMEM((2, 8, SIDE), f32),
+            pltpu.VMEM((2, SIDE + 16, 128), f32),
+            pltpu.SemaphoreType.DMA((16,)),
+            pltpu.SemaphoreType.DMA((16,)),
+        ],
+        compiler_params=pltpu.CompilerParams(
+            vmem_limit_bytes=VMEM_BYTES, collective_id=1, has_side_effects=True
+        ),
+        name="front",
+    )(far, pillar)
 
 
 def rounded(value):
@@ -410,16 +580,14 @@
 
 
 def local(far_adjoint, pillar, green_blocks, pair_src, pair_dst, group_end, w_in, b_in, w_out):
-    own = to_block_table(far_adjoint).reshape(NB, NB // 4, 16, 128)
-    ext = with_halo(own, (("tx", 0, CONE), ("ty", 1, CONE // 4)))
-    ext = ext.reshape(EXT * EXT * 4, 128)
+    ext, p3 = front(far_adjoint, pillar)
     near = sparse_near(
-        pair_dst.reshape(-1), group_end.reshape(-1), pair_src.reshape(-1), ext,
-        green_stack(green_blocks),
+        pair_dst.reshape(-1),
+        group_end.reshape(-1),
+        pair_src.reshape(-1),
+        ext.reshape(EXT * EXT * 4, 128),
+        green_blocks,
     )
-    wide = with_halo(pillar, (("tx", 0, 1), ("ty", 1, 1)))
-    wide = jnp.pad(wide, ((0, 6), (0, 0)))
-    p3 = jnp.stack([wide[:, b : b + SIDE] for b in range(3)])
     grad, west, east, sums = cell_model(
         p3,
         near,

time: 287 us -> 230 us (0.80)
  starting transfers between devices: 23.1 us -> 0 us
  other arithmetic: 14.4 us -> 3.22 us
  Pallas kernels: 230 us -> 219 us
  waiting for transfers between devices: 5.86 us -> 0 us
  local copies, waits for them, and re-layouts: 12.5 us -> 6.81 us
    ppermute x8 -> x0, starting transfers between devices: 23.1 us -> none  [the longest x4 16.5 us: with_halo(): lax.ppermute(lax.slice_in_dim(shard, length - size, length, axis=dim), ax...]
    pallas_call x1, Pallas kernels: 70.7 us -> 53.4 us  [finish(): pl.pallas_call(functools.partial(finish_kernel, (nx, ny)), out_shape=[jax...]
    concatenate x3 -> x0, other arithmetic: 7.33 us -> none  [the longest x1 3.9 us: green_stack(): return jnp.concatenate([upper_half, lower_half], axis=1)]
    pallas_call x2, Pallas kernels: 62.4 us -> 69.2 us  [the longest x1 39.1 us: sparse_near(): pl.pallas_call(sparse_kernel, out_shape=jax.ShapeDtypeStruct((2, 4, SIDE...]
    ppermute x8 -> x0, waiting for transfers between devices: 5.86 us -> none  [the longest x4 4.4 us: with_halo(): after = lax.ppermute(lax.slice_in_dim(shard, 0, size, axis=dim), axis, down)]
    slice x2 -> x0, local copies, waits for them, and re-layouts: 3.56 us -> none  [with_halo(): lax.slice_in_dim(shard, length - size, length, axis=dim)]
  transfers between devices with their start and end apart: 8 -> 0, of which waited for: 2 -> 0; matrix products, arithmetic and copies ran while one was open for 6% -> 0% of each run, Pallas kernels for 3% -> 0%
where the time goes in v3:
time: 230 us
  Pallas kernels  219 us (95%)
  local copies, waits for them, and re-layouts  6.81 us (3%)
  other arithmetic  3.22 us (1%)
    pallas_call x1, Pallas kernels, cell_model(): pl.pallas_call(cell_kernel, out_shape=[jax.ShapeDtypeStruct((rows, SIDE),...  96.5 us
    pallas_call x1, Pallas kernels, finish(): pl.pallas_call(functools.partial(finish_kernel, (nx, ny)), out_shape=[jax...  53.4 us
    pallas_call x1, Pallas kernels, sparse_near(): pl.pallas_call(sparse_kernel, out_shape=jax.ShapeDtypeStruct((2, 4, SIDE...  39.1 us
    pallas_call x1, Pallas kernels, front(): pl.pallas_call(functools.partial(front_kernel, (nx, ny)), out_shape=[jax....  30.2 us

profile of v3, /device:TPU:1, one launch (start us, length us, event | category | flops | bytes accessed | tf_op | source)
XLA Modules:
  0.0 229.9 jit_solution(7674769059151826374)
XLA Ops:
  0.6 30.2 %front.1 = (bf16[56,14,16,128]{3,2,1,0:T(8,128)(2,1)}, f32[3,528,512]{2,1,0:T(8,128)}) custom-call(bf16[2,512,512]{2,1,0:T(8,128)(2,1)} %far_ref.1, f32[512,512]{1,0:T(8,128)} %pillar_ref.1), custom_call_target="tpu_custom_call" | custom-call | tf_op jit(solution)/shard_map/front/pallas_call | solution.py:523
  30.8 1.7 clamp_multiply_fusion
  32.5 0.0 copy-start.2
  32.5 0.0 copy-start
  32.5 0.0 copy-start.1
  32.5 39.1 %sparse_near.1.near_ref = f32[2,4,544,128]{3,2,1,0:T(8,128)} custom-call(s32[24576]{0:T(1024)} %bitcast.23, s32[8]{0:T(128)} %bitcast.27, s32[48,1,512]{2,1,0:T(1,128)} %bitcast.24, bf16[12544,128]{1,0:T(8,128)(2,1)} %bitcast.22, bf16[8,2,256,256]{3,2,1,0:T(8,128)(2,1)} %green_ref.1), custom_call_target="tpu_custom_call" | custom-call | tf_op jit(solution)/shard_map/sparse_near/pallas_call | solution.py:140
  71.6 0.0 copy-done.2
  71.6 0.0 copy-done
  71.7 0.1 copy.16
  71.8 0.7 fusion.9.w1_ref
  72.6 0.0 copy-done.1
  72.6 0.1 select_maximum_fusion.1
  72.7 0.6 fusion.11.v_ref
  73.3 0.6 pad.50.wout_ref
  73.9 96.5 %cell_model.1 = (f32[528,512]{1,0:T(8,128)}, f32[528,128]{1,0:T(8,128)}, f32[528,128]{1,0:T(8,128)}, f32[16,128]{1,0:T(8,128)}) custom-call(f32[3,528,512]{2,1,0:T(8,128)} %get-tuple-element.12.p3_ref, f32[2,4,544,128]{3,2,1,0:T(8,128)} %sparse_near.1.near_ref, bf16[256,96]{1,0:T(8,128)(2,1)} %fusion.9.w1_ref, bf16[96,256]{1,0:T(8,128)(2,1)} %fusion.11.v_ref, ...), custom_call_target="tpu_custom_call" | custom-call | tf_op jit(solution)/shard_map/cell_model/pallas_call | solution.py:328
  170.4 53.4 %finish.1 = (f32[512,512]{1,0:T(8,128)}, f32[16,128]{1,0:T(8,128)}) custom-call(f32[528,512]{1,0:T(8,128)} %get-tuple-element.14.grad_ref, f32[528,128]{1,0:T(8,128)} %get-tuple-element.15.west_ref, f32[528,128]{1,0:T(8,128)} %get-tuple-element.16.east_ref, f32[16,128]{1,0:T(8,128)} %get-tuple-element.17.msg_ref), custom_call_target="tpu_custom_call" | custom-call | tf_op jit(solution)/shard_map/finish/pallas_call | solution.py:769
  223.8 1.3 slice_bitcast_fusion
  225.1 1.2 slice_bitcast_fusion.1
  226.3 0.7 slice_reduce_fusion
  227.0 0.6 reshape_squeeze.3
  227.6 2.3 copy.25
  (16 shorter events, 0.2 us)
Async XLA Ops:
  32.5 39.1 %copy-start.2 = (f32[64]{0:T(128)S(1)}, f32[64]{0:T(128)}, u32[]{:S(2)}) copy-start(f32[64]{0:T(128)} %param.16) | copy-start | bytes 772
  32.5 39.1 %copy-start = (f32[64,9]{0,1:T(8,128)S(1)}, f32[64,9]{0,1:T(8,128)}, u32[]{:S(2)}) copy-start(f32[64,9]{0,1:T(8,128)} %param.15) | copy-start | bytes 6916
  32.5 40.1 %copy-start.1 = (f32[2,64]{1,0:T(2,128)S(1)}, f32[2,64]{1,0:T(2,128)}, u32[]{:S(2)}) copy-start(f32[2,64]{1,0:T(2,128)} %param.17) | copy-start | bytes 1540

commit v4 on v3

--- a/solution.py
+++ b/solution.py
@@ -55,8 +55,8 @@
 
     def gather(base, first, count):
         for q in range(first, first + count):
-            d = pl.multiple_of(dst_ref[base + q], 4)
-            rows[4 * q : 4 * q + 4, :] = table[pl.ds(d, 4), :]
+            d = dst_ref[base + q] * 4
+            rows[4 * q : 4 * q + 4, :] = table[pl.ds(pl.multiple_of(d, 4), 4), :]
 
     def narrow():
         for j in range(4):
@@ -159,7 +159,7 @@
         compiler_params=pltpu.CompilerParams(vmem_limit_bytes=VMEM_BYTES),
         name="sparse_near",
     )(
-        jnp.clip(targets, 0, EXT * EXT - 1) * 4,
+        targets,
         ends,
         sources.reshape(slots // CHUNK, 1, CHUNK),
         ext,
@@ -198,6 +198,8 @@
     ps,
     total,
     nh,
+    first_buf,
+    second_buf,
 ):
     width = SIDE
 
@@ -220,7 +222,7 @@
             )
         return carry
 
-    lax.fori_loop(0, (SIDE + 16) // 8, build, 0)
+    lax.fori_loop(0, 3, build, 0)
     total[...] = jnp.zeros_like(total)
     nh[...] = jnp.zeros_like(nh)
     gs[...] = jnp.zeros_like(gs)
@@ -228,74 +230,6 @@
     for t in range(4):
         ps[t, 0 : PADROWS * SROWS, :] = zero_rows
         ps[t, (PADROWS + SIDE) * SROWS : (2 * PADROWS + SIDE) * SROWS, :] = zero_rows
-
-    def strip(i, carry):
-        r0 = pl.multiple_of(i * 8, 8)
-        n = [near_rows(c, r0 + PADROWS, 8) for c in range(2)]
-        deep = [p3_ref[b, pl.ds(r0, 24), :] for b in range(3)]
-        for a in range(3):
-            for b in range(3):
-                feat = deep[b][7 + a : 15 + a]
-                for c in range(2):
-                    put(gs, 10 * c + 3 * a + b, SROWS, n[c] * feat)
-        for c in range(2):
-            put(gs, 10 * c + 9, SROWS, n[c])
-        for half in range(2):
-            left, right = [], []
-            partial = [None, None]
-            feats = qs[pl.ds(r0 + 4 * half + 7, 6)].reshape(96, width)
-            h = jnp.tanh(jnp.dot(w1_ref[...], feats, preferred_element_type=f32))
-            for pair in range(2):
-                pieces = []
-                for r in range(2 * pair, 2 * pair + 2):
-                    j = 4 * half + r
-                    hr = h[HIDDEN * r : HIDDEN * r + HIDDEN]
-                    u = 1.0 - hr * hr
-                    u1 = u.astype(bf16)
-                    u2 = (u - u1.astype(f32)).astype(bf16)
-                    pieces += [u1, u2]
-                    for c in range(2):
-                        for t in range(4):
-                            tile = slice(128 * t, 128 * t + 128)
-                            term = n[c][j : j + 1, tile] * hr[:, tile]
-                            partial[c] = term if partial[c] is None else partial[c] + term
-                    g = jnp.concatenate(
-                        [gs[t, SROWS * j : SROWS * j + SROWS, :] for t in range(4)], 1
-                    )
-                    g1, g2 = split2(g)
-                    left.append(jnp.concatenate([u1, u2], 0))
-                    right.append(jnp.concatenate([g1, g2], 0).astype(bf16))
-                slope = jnp.dot(
-                    v_ref[...], jnp.concatenate(pieces, 0), preferred_element_type=f32
-                )
-                for r in range(2):
-                    j = 4 * half + 2 * pair + r
-                    one = (
-                        slope[2 * SROWS * r : 2 * SROWS * r + SROWS]
-                        + slope[2 * SROWS * r + SROWS : 2 * SROWS * r + 2 * SROWS]
-                    )
-                    at = pl.ds(pl.multiple_of((r0 + PADROWS + j) * SROWS, 8), SROWS)
-                    for t in range(4):
-                        ps[t, at, :] = one[:, 128 * t : 128 * t + 128]
-            total[:, 0 : 2 * SROWS] += lax.dot_general(
-                jnp.concatenate(left, 1),
-                jnp.concatenate(right, 1),
-                (((1,), (1,)), ((), ())),
-                preferred_element_type=f32,
-            )
-            for c in range(2):
-                nh[HIDDEN * c : HIDDEN * c + HIDDEN, :] += partial[c]
-        return carry
-
-    lax.fori_loop(0, SIDE // 8, strip, 0)
-    turned = total[...].T
-    turned = turned + pltpu.roll(turned, HIDDEN, 1)
-    pulled = turned[0:SROWS] + turned[SROWS : 2 * SROWS]
-    first = wout_ref[0:1, :] * pulled[0:10] + wout_ref[1:2, :] * pulled[10:20]
-    second = jnp.sum(nh[...].T, axis=0, keepdims=True)
-    sums_ref[...] = jnp.zeros_like(sums_ref)
-    sums_ref[0:10, :] = first
-    sums_ref[10:11, :] = second
 
     lane = lax.broadcasted_iota(jnp.int32, (8, width), 1)
 
@@ -320,7 +254,109 @@
         east_ref[at, :] = parts[2][:, width - 128 : width]
         return carry
 
-    lax.fori_loop(0, SIDE // 8 + 2, combine, 0)
+    def strip(i, carry):
+        r0 = pl.multiple_of(i * 8, 8)
+        n = [near_rows(c, r0 + PADROWS, 8) for c in range(2)]
+        deep = [p3_ref[b, pl.ds(r0, 24), :] for b in range(3)]
+        for a in range(3):
+            for b in range(3):
+                feat = deep[b][7 + a : 15 + a]
+                for c in range(2):
+                    put(gs, 10 * c + 3 * a + b, SROWS, n[c] * feat)
+        for c in range(2):
+            put(gs, 10 * c + 9, SROWS, n[c])
+
+        def make_next():
+            build(jnp.minimum(i + 3, SIDE // 8 + 1), 0)
+
+        def finish_last():
+            combine(jnp.maximum(i - 1, 0), 0)
+
+        after = [near_rows(c, r0 + PADROWS + 8, 8)[0:4] for c in range(2)]
+        step(r0, 0, r0 + 4, [n[c][4:8] for c in range(2)], first_buf, second_buf, make_next)
+        step(r0, 4, r0 + 8, after, second_buf, first_buf, finish_last)
+        return carry
+
+    def hidden(x0):
+        feats = qs[pl.ds(x0 + 7, 6)].reshape(96, width)
+        return jnp.dot(w1_ref[...], feats, preferred_element_type=f32)
+
+    def activate(z, r, n, into, partial):
+        hr = jnp.tanh(z[HIDDEN * r : HIDDEN * r + HIDDEN])
+        u = 1.0 - hr * hr
+        u1 = u.astype(bf16)
+        into[2 * HIDDEN * r : 2 * HIDDEN * r + HIDDEN, :] = u1
+        into[2 * HIDDEN * r + HIDDEN : 2 * HIDDEN * r + 2 * HIDDEN, :] = (
+            u - u1.astype(f32)
+        ).astype(bf16)
+        for c in range(2):
+            for t in range(4):
+                tile = slice(128 * t, 128 * t + 128)
+                term = n[c][r : r + 1, tile] * hr[:, tile]
+                partial[c] = term if partial[c] is None else partial[c] + term
+
+    def back(r0, j, pair, held):
+        slope = jnp.dot(
+            v_ref[...],
+            held[4 * HIDDEN * pair : 4 * HIDDEN * pair + 4 * HIDDEN, :],
+            preferred_element_type=f32,
+        )
+        for r in range(2):
+            one = (
+                slope[2 * SROWS * r : 2 * SROWS * r + SROWS]
+                + slope[2 * SROWS * r + SROWS : 2 * SROWS * r + 2 * SROWS]
+            )
+            at = pl.ds(pl.multiple_of((r0 + PADROWS + j + 2 * pair + r) * SROWS, 8), SROWS)
+            for t in range(4):
+                ps[t, at, :] = one[:, 128 * t : 128 * t + 128]
+
+    def sums(j, pair, held):
+        left, right = [], []
+        for r in range(2 * pair, 2 * pair + 2):
+            first = SROWS * (j + r)
+            g = jnp.concatenate([gs[t, first : first + SROWS, :] for t in range(4)], 1)
+            left.append(held[2 * HIDDEN * r : 2 * HIDDEN * r + 2 * HIDDEN, :])
+            right.append(jnp.concatenate(split2(g), 0).astype(bf16))
+        return lax.dot_general(
+            jnp.concatenate(left, 1),
+            jnp.concatenate(right, 1),
+            (((1,), (1,)), ((), ())),
+            preferred_element_type=f32,
+        )
+
+    def step(r0, j, x0, n, held, into, extra):
+        partial = [None, None]
+        z = hidden(x0)
+        activate(z, 0, n, into, partial)
+        back(r0, j, 0, held)
+        activate(z, 1, n, into, partial)
+        one = sums(j, 0, held)
+        activate(z, 2, n, into, partial)
+        back(r0, j, 1, held)
+        activate(z, 3, n, into, partial)
+        extra()
+        two = sums(j, 1, held)
+        total[:, 0 : 2 * SROWS] += one + two
+        for c in range(2):
+            nh[HIDDEN * c : HIDDEN * c + HIDDEN, :] += partial[c]
+
+    partial = [None, None]
+    z = hidden(0)
+    for r in range(4):
+        activate(z, r, [near_rows(c, PADROWS, 8) for c in range(2)], first_buf, partial)
+    for c in range(2):
+        nh[HIDDEN * c : HIDDEN * c + HIDDEN, :] += partial[c]
+    lax.fori_loop(0, SIDE // 8, strip, 0)
+    turned = total[...].T
+    turned = turned + pltpu.roll(turned, HIDDEN, 1)
+    pulled = turned[0:SROWS] + turned[SROWS : 2 * SROWS]
+    first = wout_ref[0:1, :] * pulled[0:10] + wout_ref[1:2, :] * pulled[10:20]
+    second = jnp.sum(nh[...].T, axis=0, keepdims=True)
+    sums_ref[...] = jnp.zeros_like(sums_ref)
+    sums_ref[0:10, :] = first
+    sums_ref[10:11, :] = second
+
+    lax.fori_loop(SIDE // 8 - 1, SIDE // 8 + 2, combine, 0)
 
 
 def cell_model(p3, near, first, back, out_weights):
@@ -342,6 +378,8 @@
             pltpu.VMEM((4, (SIDE + 2 * PADROWS) * SROWS, 128), f32),
             pltpu.VMEM((128, 128), f32),
             pltpu.VMEM((128, 128), f32),
+            pltpu.VMEM((8 * HIDDEN, SIDE), bf16),
+            pltpu.VMEM((8 * HIDDEN, SIDE), bf16),
         ],
         compiler_params=pltpu.CompilerParams(vmem_limit_bytes=VMEM_BYTES),
         name="cell_model",

time: 230 us -> 200 us (0.87)
  Pallas kernels: 219 us -> 190 us
    pallas_call x1, Pallas kernels: 96.5 us -> 71.2 us  [cell_model(): pl.pallas_call(cell_kernel, out_shape=[jax.ShapeDtypeStruct((rows, SIDE),...]
    pallas_call x1, Pallas kernels: 53.4 us -> 50.6 us  [finish(): pl.pallas_call(functools.partial(finish_kernel, (nx, ny)), out_shape=[jax...]
where the time goes in v4:
time: 200 us; the launch traced here: 199 us
  Pallas kernels  190 us (95%)
  local copies, waits for them, and re-layouts  6.82 us (3%)
    pallas_call x1, Pallas kernels, cell_model(): pl.pallas_call(cell_kernel, out_shape=[jax.ShapeDtypeStruct((rows, SIDE),...  71.2 us
    pallas_call x1, Pallas kernels, finish(): pl.pallas_call(functools.partial(finish_kernel, (nx, ny)), out_shape=[jax...  50.6 us
    pallas_call x1, Pallas kernels, sparse_near(): pl.pallas_call(sparse_kernel, out_shape=jax.ShapeDtypeStruct((2, 4, SIDE...  38.4 us
    pallas_call x1, Pallas kernels, front(): pl.pallas_call(functools.partial(front_kernel, (nx, ny)), out_shape=[jax....  30.2 us

profile of v4, /device:TPU:1, one launch (start us, length us, event | category | flops | bytes accessed | tf_op | source)
XLA Modules:
  0.0 199.3 jit_solution(14042846884273965137)
XLA Ops:
  0.6 30.2 %front.1 = (bf16[56,14,16,128]{3,2,1,0:T(8,128)(2,1)}, f32[3,528,512]{2,1,0:T(8,128)}) custom-call(bf16[2,512,512]{2,1,0:T(8,128)(2,1)} %far_ref.1, f32[512,512]{1,0:T(8,128)} %pillar_ref.1), custom_call_target="tpu_custom_call" | custom-call | tf_op jit(solution)/shard_map/front/pallas_call | solution.py:561
  30.8 0.0 copy-start.2
  30.8 0.0 copy-start
  30.8 0.0 copy-start.1
  30.8 38.4 %sparse_near.1.near_ref = f32[2,4,544,128]{3,2,1,0:T(8,128)} custom-call(s32[24576]{0:T(1024)} %bitcast.23, s32[8]{0:T(128)} %bitcast.27, s32[48,1,512]{2,1,0:T(1,128)} %bitcast.24, bf16[12544,128]{1,0:T(8,128)(2,1)} %bitcast.22, bf16[8,2,256,256]{3,2,1,0:T(8,128)(2,1)} %green_ref.1), custom_call_target="tpu_custom_call" | custom-call | tf_op jit(solution)/shard_map/sparse_near/pallas_call | solution.py:140
  69.2 0.0 copy-done.2
  69.2 0.0 copy-done
  69.4 0.1 copy.16
  69.5 0.7 fusion.9.w1_ref
  70.2 0.0 copy-done.1
  70.2 0.1 select_maximum_fusion.1
  70.3 0.6 fusion.11.v_ref
  70.9 0.6 pad.50.wout_ref
  71.5 71.2 %cell_model.1 = (f32[528,512]{1,0:T(8,128)}, f32[528,128]{1,0:T(8,128)}, f32[528,128]{1,0:T(8,128)}, f32[16,128]{1,0:T(8,128)}) custom-call(f32[3,528,512]{2,1,0:T(8,128)} %get-tuple-element.12.p3_ref, f32[2,4,544,128]{3,2,1,0:T(8,128)} %sparse_near.1.near_ref, bf16[256,96]{1,0:T(8,128)(2,1)} %fusion.9.w1_ref, bf16[96,256]{1,0:T(8,128)(2,1)} %fusion.11.v_ref, ...), custom_call_target="tpu_custom_call" | custom-call | tf_op jit(solution)/shard_map/cell_model/pallas_call | solution.py:364
  142.7 50.6 %finish.1 = (f32[512,512]{1,0:T(8,128)}, f32[16,128]{1,0:T(8,128)}) custom-call(f32[528,512]{1,0:T(8,128)} %get-tuple-element.14.grad_ref, f32[528,128]{1,0:T(8,128)} %get-tuple-element.15.west_ref, f32[528,128]{1,0:T(8,128)} %get-tuple-element.16.east_ref, f32[16,128]{1,0:T(8,128)} %get-tuple-element.17.msg_ref), custom_call_target="tpu_custom_call" | custom-call | tf_op jit(solution)/shard_map/finish/pallas_call | solution.py:807
  193.3 1.3 slice_bitcast_fusion
  194.6 1.2 slice_bitcast_fusion.1
  195.7 0.7 slice_reduce_fusion
  196.4 0.6 reshape_squeeze.3
  197.1 2.3 %copy.25 = f32[512,512]{1,0:T(8,128)} copy(f32[512,512]{1,0:T(8,128)} %get-tuple-element.29) | data formatting | bytes 2097152
  (16 shorter events, 0.2 us)
Async XLA Ops:
  30.8 38.4 %copy-start.2 = (f32[64]{0:T(128)S(1)}, f32[64]{0:T(128)}, u32[]{:S(2)}) copy-start(f32[64]{0:T(128)} %param.16) | copy-start | bytes 772
  30.8 38.4 %copy-start = (f32[64,9]{0,1:T(8,128)S(1)}, f32[64,9]{0,1:T(8,128)}, u32[]{:S(2)}) copy-start(f32[64,9]{0,1:T(8,128)} %param.15) | copy-start | bytes 6916
  30.8 39.4 %copy-start.1 = (f32[2,64]{1,0:T(2,128)S(1)}, f32[2,64]{1,0:T(2,128)}, u32[]{:S(2)}) copy-start(f32[2,64]{1,0:T(2,128)} %param.17) | copy-start | bytes 1540

commit v5 on v4

--- a/solution.py
+++ b/solution.py
@@ -182,16 +182,187 @@
     return jnp.concatenate(tiles, 1)
 
 
+def greet(nx, ny, tx, ty):
+    barrier = pltpu.get_barrier_semaphore()
+    for d in range(1, nx):
+        pl.semaphore_signal(
+            barrier, inc=1, device_id=(lax.rem(tx + d, nx), ty), device_id_type=MESH
+        )
+    for d in range(1, ny):
+        pl.semaphore_signal(
+            barrier, inc=1, device_id=(tx, lax.rem(ty + d, ny)), device_id_type=MESH
+        )
+
+
+def finish(
+    shape,
+    grad_ref,
+    west_ref,
+    east_ref,
+    message,
+    out_ref,
+    first_ref,
+    bias_ref,
+    second_ref,
+    row_out,
+    row_in,
+    col_out,
+    col_in,
+    cols,
+    buf_a,
+    buf_b,
+    row_send,
+    row_recv,
+    col_send,
+    col_recv,
+    send_a,
+    recv_a,
+    send_b,
+    recv_b,
+):
+    nx, ny = shape
+    tx = lax.axis_index("tx")
+    ty = lax.axis_index("ty")
+
+    pl.semaphore_wait(pltpu.get_barrier_semaphore(), nx + ny - 2)
+
+    def line(side, which):
+        out, into, send, recv, axis = which
+        at = (tx, ty)[axis] + 2 * side - 1
+        device = (at, ty) if axis == 0 else (tx, at)
+        return pltpu.make_async_remote_copy(
+            src_ref=out.at[side],
+            dst_ref=into.at[side],
+            send_sem=send.at[side],
+            recv_sem=recv.at[side],
+            device_id=device,
+            device_id_type=MESH,
+        )
+
+    rows = (row_out, row_in, row_send, row_recv, 0)
+    columns = (col_out, col_in, col_send, col_recv, 1)
+
+    def has(side, index, count):
+        return index > 0 if side == 0 else index < count - 1
+
+    def sums_copy(d, buf, send, recv, index, count, axis):
+        other = lax.rem(index + d, count)
+        return pltpu.make_async_remote_copy(
+            src_ref=buf.at[index],
+            dst_ref=buf.at[index],
+            send_sem=send.at[d],
+            recv_sem=recv.at[index],
+            device_id=(other, ty) if axis == 0 else (tx, other),
+            device_id_type=MESH,
+        )
+
+    def sums_wait(d, buf, send, recv, index, count, axis):
+        sender = lax.rem(index + d, count)
+        pltpu.make_async_remote_copy(
+            src_ref=buf.at[sender],
+            dst_ref=buf.at[sender],
+            send_sem=send.at[d],
+            recv_sem=recv.at[sender],
+            device_id=(sender, ty) if axis == 0 else (tx, sender),
+            device_id_type=MESH,
+        ).wait_recv()
+
+    along_x = (buf_a, send_a, recv_a, tx, nx, 0)
+    along_y = (buf_b, send_b, recv_b, ty, ny, 1)
+    buf_a[tx] = message
+    for d in range(1, nx):
+        sums_copy(d, *along_x).start()
+
+    row_out[0, :, 0:128] = west_ref[0:8, :]
+    row_out[0, :, 128 : 128 + SIDE] = grad_ref[0:8, :]
+    row_out[0, :, 128 + SIDE : 256 + SIDE] = east_ref[0:8, :]
+    row_out[1, :, 0:128] = west_ref[SIDE + 8 : SIDE + 16, :]
+    row_out[1, :, 128 : 128 + SIDE] = grad_ref[SIDE + 8 : SIDE + 16, :]
+    row_out[1, :, 128 + SIDE : 256 + SIDE] = east_ref[SIDE + 8 : SIDE + 16, :]
+    for side in range(2):
+        pl.when(has(side, tx, nx))(lambda side=side: line(side, rows).start())
+
+    def copy(i, carry):
+        at = pl.multiple_of(i * 8, 8)
+        out_ref[pl.ds(at, 8), :] = grad_ref[pl.ds(at + 8, 8), :]
+        cols[0, pl.ds(at, 8), :] = west_ref[pl.ds(at + 8, 8), :]
+        cols[1, pl.ds(at, 8), :] = east_ref[pl.ds(at + 8, 8), :]
+        return carry
+
+    lax.fori_loop(0, SIDE // 8, copy, 0)
+    for d in range(1, nx):
+        sums_wait(d, *along_x)
+    value = buf_a[0]
+    for d in range(1, nx):
+        value = value + buf_a[d]
+    buf_b[ty] = value
+    for d in range(1, ny):
+        sums_copy(d, *along_y).start()
+
+    for side, row, first in ((0, 7, SIDE - 8), (1, 0, 0)):
+
+        @pl.when(has(1 - side, tx, nx))
+        def _(side=side, row=row, first=first):
+            line(side, rows).wait_recv()
+            got = row_in[side]
+            got = jnp.where(
+                lax.broadcasted_iota(jnp.int32, got.shape, 0) == row, got, 0.0
+            )
+            out_ref[first : first + 8, :] += got[:, 128 : 128 + SIDE]
+            cols[0, first : first + 8, :] += got[:, 0:128]
+            cols[1, first : first + 8, :] += got[:, 128 + SIDE : 256 + SIDE]
+
+    for q in range(4):
+        tile = slice(128 * q, 128 * q + 128)
+        col_out[0, :, tile] = cols[0, tile, :].T[0:8]
+        col_out[1, :, tile] = cols[1, tile, :].T[120:128]
+    for side in range(2):
+        pl.when(has(side, ty, ny))(lambda side=side: line(side, columns).start())
+
+    lane = lax.broadcasted_iota(jnp.int32, (128, 128), 1)
+    for side, row, first, spot in ((0, 0, SIDE - 128, 127), (1, 7, 0, 0)):
+
+        @pl.when(has(1 - side, ty, ny))
+        def _(side=side, row=row, first=first, spot=spot):
+            line(side, columns).wait_recv()
+            for q in range(4):
+                tile = slice(128 * q, 128 * q + 128)
+                got = jnp.broadcast_to(col_in[side, row : row + 1, tile], (128, 128)).T
+                out_ref[tile, first : first + 128] += jnp.where(lane == spot, got, 0.0)
+
+    for d in range(1, ny):
+        sums_wait(d, *along_y)
+    value = buf_b[0]
+    for d in range(1, ny):
+        value = value + buf_b[d]
+    value = value * (float(SIDE * SIDE * nx * ny) ** (-0.5))
+    first_ref[...] = value.T[0:HIDDEN, 0:9]
+    bias_ref[...] = value[9:10, 0:HIDDEN]
+    second_ref[0:1, :] = value[10:11, 0:HIDDEN]
+    second_ref[1:2, :] = pltpu.roll(value, HIDDEN, 1)[10:11, 0:HIDDEN]
+    for side in range(2):
+        pl.when(has(side, tx, nx))(lambda side=side: line(side, rows).wait_send())
+        pl.when(has(side, ty, ny))(lambda side=side: line(side, columns).wait_send())
+    for d in range(1, nx):
+        sums_copy(d, *along_x).wait_send()
+    for d in range(1, ny):
+        sums_copy(d, *along_y).wait_send()
+
+
 def cell_kernel(
+    shape,
     p3_ref,
     near_ref,
     w1_ref,
     v_ref,
     wout_ref,
+    out_ref,
+    first_ref,
+    bias_ref,
+    second_ref,
     grad_ref,
     west_ref,
     east_ref,
-    sums_ref,
     q32,
     qs,
     gs,
@@ -200,8 +371,11 @@
     nh,
     first_buf,
     second_buf,
+    *exchange,
 ):
     width = SIDE
+    nx, ny = shape
+    greet(nx, ny, lax.axis_index("tx"), lax.axis_index("ty"))
 
     def near_rows(c, first, count):
         at = pl.ds(pl.multiple_of(first, 8), count)
@@ -347,41 +521,72 @@
     for c in range(2):
         nh[HIDDEN * c : HIDDEN * c + HIDDEN, :] += partial[c]
     lax.fori_loop(0, SIDE // 8, strip, 0)
+    lax.fori_loop(SIDE // 8 - 1, SIDE // 8 + 2, combine, 0)
     turned = total[...].T
     turned = turned + pltpu.roll(turned, HIDDEN, 1)
     pulled = turned[0:SROWS] + turned[SROWS : 2 * SROWS]
     first = wout_ref[0:1, :] * pulled[0:10] + wout_ref[1:2, :] * pulled[10:20]
     second = jnp.sum(nh[...].T, axis=0, keepdims=True)
-    sums_ref[...] = jnp.zeros_like(sums_ref)
-    sums_ref[0:10, :] = first
-    sums_ref[10:11, :] = second
-
-    lax.fori_loop(SIDE // 8 - 1, SIDE // 8 + 2, combine, 0)
+    message = jnp.concatenate([first, second, jnp.zeros((5, 128), f32)], 0)
+    finish(
+        shape,
+        grad_ref,
+        west_ref,
+        east_ref,
+        message,
+        out_ref,
+        first_ref,
+        bias_ref,
+        second_ref,
+        *exchange,
+    )
 
 
 def cell_model(p3, near, first, back, out_weights):
+    nx, ny = lax.axis_size("tx"), lax.axis_size("ty")
+    dma = pltpu.SemaphoreType.DMA
     rows = SIDE + 16
     return pl.pallas_call(
-        cell_kernel,
+        functools.partial(cell_kernel, (nx, ny)),
         out_shape=[
-            jax.ShapeDtypeStruct((rows, SIDE), f32),
-            jax.ShapeDtypeStruct((rows, 128), f32),
-            jax.ShapeDtypeStruct((rows, 128), f32),
-            jax.ShapeDtypeStruct((16, 128), f32),
+            jax.ShapeDtypeStruct((SIDE, SIDE), f32),
+            jax.ShapeDtypeStruct((HIDDEN, 9), f32),
+            jax.ShapeDtypeStruct((1, HIDDEN), f32),
+            jax.ShapeDtypeStruct((2, HIDDEN), f32),
         ],
         in_specs=[pl.BlockSpec(memory_space=pltpu.VMEM)] * 5,
         out_specs=[pl.BlockSpec(memory_space=pltpu.VMEM)] * 4,
         scratch_shapes=[
+            pltpu.VMEM((rows, SIDE), f32),
+            pltpu.VMEM((rows, 128), f32),
+            pltpu.VMEM((rows, 128), f32),
             pltpu.VMEM((4, 128, 128), f32),
-            pltpu.VMEM((SIDE + 16, 16, SIDE), bf16),
+            pltpu.VMEM((rows, 16, SIDE), bf16),
             pltpu.VMEM((4, 8 * SROWS, 128), f32),
             pltpu.VMEM((4, (SIDE + 2 * PADROWS) * SROWS, 128), f32),
             pltpu.VMEM((128, 128), f32),
             pltpu.VMEM((128, 128), f32),
             pltpu.VMEM((8 * HIDDEN, SIDE), bf16),
             pltpu.VMEM((8 * HIDDEN, SIDE), bf16),
+            pltpu.VMEM((2, 8, SIDE + 256), f32),
+            pltpu.VMEM((2, 8, SIDE + 256), f32),
+            pltpu.VMEM((2, 8, SIDE), f32),
+            pltpu.VMEM((2, 8, SIDE), f32),
+            pltpu.VMEM((2, SIDE, 128), f32),
+            pltpu.VMEM((nx, 16, 128), f32),
+            pltpu.VMEM((ny, 16, 128), f32),
+            dma((2,)),
+            dma((2,)),
+            dma((2,)),
+            dma((2,)),
+            dma((nx,)),
+            dma((nx,)),
+            dma((ny,)),
+            dma((ny,)),
         ],
-        compiler_params=pltpu.CompilerParams(vmem_limit_bytes=VMEM_BYTES),
+        compiler_params=pltpu.CompilerParams(
+            vmem_limit_bytes=VMEM_BYTES, collective_id=0, has_side_effects=True
+        ),
         name="cell_model",
     )(p3, near, first, back, out_weights)
 
@@ -626,214 +831,14 @@
         ext.reshape(EXT * EXT * 4, 128),
         green_blocks,
     )
-    grad, west, east, sums = cell_model(
+    grad, grad_in, grad_bias, grad_out = cell_model(
         p3,
         near,
         first_weights(w_in, b_in),
         back_weights(w_in, w_out),
         jnp.pad(w_out, ((0, 6), (0, HIDDEN))),
     )
-    grad, sums = finish(grad, west, east, sums)
-    return (
-        grad,
-        sums[0:9, 0:HIDDEN].T,
-        sums[9, 0:HIDDEN],
-        sums[10].reshape(2, HIDDEN),
-    )
-
-
-def finish_kernel(
-    shape,
-    grad_ref,
-    west_ref,
-    east_ref,
-    msg_ref,
-    out_ref,
-    sums_ref,
-    row_out,
-    row_in,
-    col_out,
-    col_in,
-    cols,
-    buf_a,
-    buf_b,
-    row_send,
-    row_recv,
-    col_send,
-    col_recv,
-    send_a,
-    recv_a,
-    send_b,
-    recv_b,
-):
-    nx, ny = shape
-    tx = lax.axis_index("tx")
-    ty = lax.axis_index("ty")
-
-    barrier = pltpu.get_barrier_semaphore()
-    for d in range(1, nx):
-        pl.semaphore_signal(
-            barrier, inc=1, device_id=(lax.rem(tx + d, nx), ty), device_id_type=MESH
-        )
-    for d in range(1, ny):
-        pl.semaphore_signal(
-            barrier, inc=1, device_id=(tx, lax.rem(ty + d, ny)), device_id_type=MESH
-        )
-    if nx + ny > 2:
-        pl.semaphore_wait(barrier, nx + ny - 2)
-
-    def line(side, which):
-        out, into, send, recv, axis = which
-        at = (tx, ty)[axis] + 2 * side - 1
-        device = (at, ty) if axis == 0 else (tx, at)
-        return pltpu.make_async_remote_copy(
-            src_ref=out.at[side],
-            dst_ref=into.at[side],
-            send_sem=send.at[side],
-            recv_sem=recv.at[side],
-            device_id=device,
-            device_id_type=MESH,
-        )
-
-    rows = (row_out, row_in, row_send, row_recv, 0)
-    columns = (col_out, col_in, col_send, col_recv, 1)
-
-    def has(side, index, count):
-        return index > 0 if side == 0 else index < count - 1
-
-    row_out[0, :, 0:128] = west_ref[0:8, :]
-    row_out[0, :, 128 : 128 + SIDE] = grad_ref[0:8, :]
-    row_out[0, :, 128 + SIDE : 256 + SIDE] = east_ref[0:8, :]
-    row_out[1, :, 0:128] = west_ref[SIDE + 8 : SIDE + 16, :]
-    row_out[1, :, 128 : 128 + SIDE] = grad_ref[SIDE + 8 : SIDE + 16, :]
-    row_out[1, :, 128 + SIDE : 256 + SIDE] = east_ref[SIDE + 8 : SIDE + 16, :]
-    for side in range(2):
-        pl.when(has(side, tx, nx))(lambda side=side: line(side, rows).start())
-
-    def sums_copy(d, buf, send, recv, index, count, axis):
-        other = lax.rem(index + d, count)
-        return pltpu.make_async_remote_copy(
-            src_ref=buf.at[index],
-            dst_ref=buf.at[index],
-            send_sem=send.at[d],
-            recv_sem=recv.at[index],
-            device_id=(other, ty) if axis == 0 else (tx, other),
-            device_id_type=MESH,
-        )
-
-    def sums_wait(d, buf, send, recv, index, count, axis):
-        sender = lax.rem(index + d, count)
-        pltpu.make_async_remote_copy(
-            src_ref=buf.at[sender],
-            dst_ref=buf.at[sender],
-            send_sem=send.at[d],
-            recv_sem=recv.at[sender],
-            device_id=(sender, ty) if axis == 0 else (tx, sender),
-            device_id_type=MESH,
-        ).wait_recv()
-
-    along_x = (buf_a, send_a, recv_a, tx, nx, 0)
-    along_y = (buf_b, send_b, recv_b, ty, ny, 1)
-    buf_a[tx] = msg_ref[...]
-    for d in range(1, nx):
-        sums_copy(d, *along_x).start()
-
-    def copy(i, carry):
-        at = pl.multiple_of(i * 8, 8)
-        out_ref[pl.ds(at, 8), :] = grad_ref[pl.ds(at + 8, 8), :]
-        cols[0, pl.ds(at, 8), :] = west_ref[pl.ds(at + 8, 8), :]
-        cols[1, pl.ds(at, 8), :] = east_ref[pl.ds(at + 8, 8), :]
-        return carry
-
-    lax.fori_loop(0, SIDE // 8, copy, 0)
-    for side, row, first in ((0, 7, SIDE - 8), (1, 0, 0)):
-
-        @pl.when(has(1 - side, tx, nx))
-        def _(side=side, row=row, first=first):
-            line(side, rows).wait_recv()
-            got = row_in[side]
-            got = jnp.where(
-                lax.broadcasted_iota(jnp.int32, got.shape, 0) == row, got, 0.0
-            )
-            out_ref[first : first + 8, :] += got[:, 128 : 128 + SIDE]
-            cols[0, first : first + 8, :] += got[:, 0:128]
-            cols[1, first : first + 8, :] += got[:, 128 + SIDE : 256 + SIDE]
-
-    for q in range(4):
-        tile = slice(128 * q, 128 * q + 128)
-        col_out[0, :, tile] = cols[0, tile, :].T[0:8]
-        col_out[1, :, tile] = cols[1, tile, :].T[120:128]
-    for side in range(2):
-        pl.when(has(side, ty, ny))(lambda side=side: line(side, columns).start())
-
-    for d in range(1, nx):
-        sums_wait(d, *along_x)
-    value = buf_a[0]
-    for d in range(1, nx):
-        value = value + buf_a[d]
-    buf_b[ty] = value
-    for d in range(1, ny):
-        sums_copy(d, *along_y).start()
-
-    lane = lax.broadcasted_iota(jnp.int32, (128, 128), 1)
-    for side, row, first, spot in ((0, 0, SIDE - 128, 127), (1, 7, 0, 0)):
-
-        @pl.when(has(1 - side, ty, ny))
-        def _(side=side, row=row, first=first, spot=spot):
-            line(side, columns).wait_recv()
-            for q in range(4):
-                tile = slice(128 * q, 128 * q + 128)
-                got = jnp.broadcast_to(col_in[side, row : row + 1, tile], (128, 128)).T
-                out_ref[tile, first : first + 128] += jnp.where(lane == spot, got, 0.0)
-
-    for d in range(1, ny):
-        sums_wait(d, *along_y)
-    value = buf_b[0]
-    for d in range(1, ny):
-        value = value + buf_b[d]
-    sums_ref[...] = value * (float(SIDE * SIDE * nx * ny) ** (-0.5))
-    for side in range(2):
-        pl.when(has(side, tx, nx))(lambda side=side: line(side, rows).wait_send())
-        pl.when(has(side, ty, ny))(lambda side=side: line(side, columns).wait_send())
-    for d in range(1, nx):
-        sums_copy(d, *along_x).wait_send()
-    for d in range(1, ny):
-        sums_copy(d, *along_y).wait_send()
-
-
-def finish(grad, west, east, sums):
-    nx, ny = lax.axis_size("tx"), lax.axis_size("ty")
-    dma = pltpu.SemaphoreType.DMA
-    return pl.pallas_call(
-        functools.partial(finish_kernel, (nx, ny)),
-        out_shape=[
-            jax.ShapeDtypeStruct((SIDE, SIDE), f32),
-            jax.ShapeDtypeStruct((16, 128), f32),
-        ],
-        in_specs=[pl.BlockSpec(memory_space=pltpu.VMEM)] * 4,
-        out_specs=[pl.BlockSpec(memory_space=pltpu.VMEM)] * 2,
-        scratch_shapes=[
-            pltpu.VMEM((2, 8, SIDE + 256), f32),
-            pltpu.VMEM((2, 8, SIDE + 256), f32),
-            pltpu.VMEM((2, 8, SIDE), f32),
-            pltpu.VMEM((2, 8, SIDE), f32),
-            pltpu.VMEM((2, SIDE, 128), f32),
-            pltpu.VMEM((nx, 16, 128), f32),
-            pltpu.VMEM((ny, 16, 128), f32),
-            dma((2,)),
-            dma((2,)),
-            dma((2,)),
-            dma((2,)),
-            dma((nx,)),
-            dma((nx,)),
-            dma((ny,)),
-            dma((ny,)),
-        ],
-        compiler_params=pltpu.CompilerParams(
-            vmem_limit_bytes=VMEM_BYTES, collective_id=0, has_side_effects=True
-        ),
-        name="finish",
-    )(grad, west, east, sums)
+    return grad, grad_in, grad_bias.reshape(HIDDEN), grad_out
 
 
 def solution(mesh):

time: 200 us -> 194 us (0.970)
  Pallas kernels: 190 us -> 184 us
    pallas_call x2 -> x1, Pallas kernels: 122 us -> 116 us  [cell_model(): pl.pallas_call(functools.partial(cell_kernel, (nx, ny)), out_shape=[jax.S...]
    unnamed x7 -> x10, local copies, waits for them, and re-layouts: 2.28 us -> 6.03 us
where the time goes in v5:
time: 194 us
  Pallas kernels  184 us (95%)
  local copies, waits for them, and re-layouts  6.77 us (3%)
    pallas_call x1, Pallas kernels, cell_model(): pl.pallas_call(functools.partial(cell_kernel, (nx, ny)), out_shape=[jax.S...  116 us
    pallas_call x1, Pallas kernels, sparse_near(): pl.pallas_call(sparse_kernel, out_shape=jax.ShapeDtypeStruct((2, 4, SIDE...  38.5 us
    pallas_call x1, Pallas kernels, front(): pl.pallas_call(functools.partial(front_kernel, (nx, ny)), out_shape=[jax....  30.2 us
    unnamed x10, local copies, waits for them, and re-layouts  6.03 us

profile of v5, /device:TPU:1, one launch (start us, length us, event | category | flops | bytes accessed | tf_op | source)
XLA Modules:
  0.0 193.5 jit_solution(10530249685438331569)
XLA Ops:
  0.6 30.2 %front.1 = (bf16[56,14,16,128]{3,2,1,0:T(8,128)(2,1)}, f32[3,528,512]{2,1,0:T(8,128)}) custom-call(bf16[2,512,512]{2,1,0:T(8,128)(2,1)} %far_ref.1, f32[512,512]{1,0:T(8,128)} %pillar_ref.1), custom_call_target="tpu_custom_call" | custom-call | tf_op jit(solution)/shard_map/front/pallas_call | solution.py:766
  30.8 0.0 copy-start.2
  30.8 0.0 copy-start
  30.8 0.0 copy-start.1
  30.8 38.5 %sparse_near.1.near_ref = f32[2,4,544,128]{3,2,1,0:T(8,128)} custom-call(s32[24576]{0:T(1024)} %bitcast.20, s32[8]{0:T(128)} %bitcast.24, s32[48,1,512]{2,1,0:T(1,128)} %bitcast.21, bf16[12544,128]{1,0:T(8,128)(2,1)} %bitcast.19, bf16[8,2,256,256]{3,2,1,0:T(8,128)(2,1)} %green_ref.1), custom_call_target="tpu_custom_call" | custom-call | tf_op jit(solution)/shard_map/sparse_near/pallas_call | solution.py:140
  69.3 0.0 copy-done.2
  69.3 0.0 copy-done
  69.5 0.1 copy.17
  69.6 0.7 fusion.9.w1_ref
  70.3 0.0 copy-done.1
  70.3 0.1 select_maximum_fusion.1
  70.4 0.6 fusion.11.v_ref
  71.0 0.6 pad.50.wout_ref
  71.6 115.9 %cell_model.1 = (f32[512,512]{1,0:T(8,128)}, f32[64,9]{1,0:T(8,128)}, f32[1,64]{1,0:T(1,128)}, f32[2,64]{1,0:T(2,128)}) custom-call(f32[3,528,512]{2,1,0:T(8,128)} %get-tuple-element.10.p3_ref, f32[2,4,544,128]{3,2,1,0:T(8,128)} %sparse_near.1.near_ref, bf16[256,96]{1,0:T(8,128)(2,1)} %fusion.9.w1_ref, bf16[96,256]{1,0:T(8,128)(2,1)} %fusion.11.v_ref, ...), custom_call_target="tpu_custom_call" | custom-call | tf_op jit(solution)/shard_map/cell_model/pallas_call | solution.py:549
  187.5 1.4 copy.21
  188.9 2.3 %copy.29 = f32[512,512]{1,0:T(8,128)} copy(f32[512,512]{1,0:T(8,128)} %get-tuple-element.33) | data formatting | bytes 2097152
  191.2 1.1 copy.30
  192.3 1.2 copy.31
  (16 shorter events, 0.2 us)
Async XLA Ops:
  30.8 38.5 %copy-start.2 = (f32[64]{0:T(128)S(1)}, f32[64]{0:T(128)}, u32[]{:S(2)}) copy-start(f32[64]{0:T(128)} %param.16) | copy-start | bytes 772
  30.8 38.5 %copy-start = (f32[64,9]{0,1:T(8,128)S(1)}, f32[64,9]{0,1:T(8,128)}, u32[]{:S(2)}) copy-start(f32[64,9]{0,1:T(8,128)} %param.15) | copy-start | bytes 6916
  30.8 39.5 %copy-start.1 = (f32[2,64]{1,0:T(2,128)S(1)}, f32[2,64]{1,0:T(2,128)}, u32[]{:S(2)}) copy-start(f32[2,64]{1,0:T(2,128)} %param.17) | copy-start | bytes 1540

commit v6 on v5

--- a/solution.py
+++ b/solution.py
@@ -201,9 +201,7 @@
     east_ref,
     message,
     out_ref,
-    first_ref,
-    bias_ref,
-    second_ref,
+    sums_ref,
     row_out,
     row_in,
     col_out,
@@ -336,10 +334,7 @@
     for d in range(1, ny):
         value = value + buf_b[d]
     value = value * (float(SIDE * SIDE * nx * ny) ** (-0.5))
-    first_ref[...] = value.T[0:HIDDEN, 0:9]
-    bias_ref[...] = value[9:10, 0:HIDDEN]
-    second_ref[0:1, :] = value[10:11, 0:HIDDEN]
-    second_ref[1:2, :] = pltpu.roll(value, HIDDEN, 1)[10:11, 0:HIDDEN]
+    sums_ref[...] = value
     for side in range(2):
         pl.when(has(side, tx, nx))(lambda side=side: line(side, rows).wait_send())
         pl.when(has(side, ty, ny))(lambda side=side: line(side, columns).wait_send())
@@ -357,9 +352,7 @@
     v_ref,
     wout_ref,
     out_ref,
-    first_ref,
-    bias_ref,
-    second_ref,
+    sums_ref,
     grad_ref,
     west_ref,
     east_ref,
@@ -535,9 +528,7 @@
         east_ref,
         message,
         out_ref,
-        first_ref,
-        bias_ref,
-        second_ref,
+        sums_ref,
         *exchange,
     )
 
@@ -550,12 +541,10 @@
         functools.partial(cell_kernel, (nx, ny)),
         out_shape=[
             jax.ShapeDtypeStruct((SIDE, SIDE), f32),
-            jax.ShapeDtypeStruct((HIDDEN, 9), f32),
-            jax.ShapeDtypeStruct((1, HIDDEN), f32),
-            jax.ShapeDtypeStruct((2, HIDDEN), f32),
+            jax.ShapeDtypeStruct((16, 128), f32),
         ],
         in_specs=[pl.BlockSpec(memory_space=pltpu.VMEM)] * 5,
-        out_specs=[pl.BlockSpec(memory_space=pltpu.VMEM)] * 4,
+        out_specs=[pl.BlockSpec(memory_space=pltpu.VMEM)] * 2,
         scratch_shapes=[
             pltpu.VMEM((rows, SIDE), f32),
             pltpu.VMEM((rows, 128), f32),
@@ -595,7 +584,21 @@
 
 
 def front_kernel(
-    shape, far_ref, pillar_ref, ext_ref, p3_ref, field, flat, edge_in, turned, side, sends, recvs
+    shape,
+    far_ref,
+    pillar_ref,
+    ext_ref,
+    p3_ref,
+    field,
+    flat,
+    order,
+    pieces,
+    placed,
+    edge_in,
+    turned,
+    side,
+    sends,
+    recvs,
 ):
     nx, ny = shape
     tx = lax.axis_index("tx")
@@ -613,7 +616,19 @@
         tile = slice(128 * q, 128 * q + 128)
         turned[0, :, tile] = pillar_ref[tile, 0:128].T[0:8]
         turned[1, :, tile] = pillar_ref[tile, SIDE - 128 : SIDE].T[120:128]
-    pl.semaphore_wait(barrier, len(AROUND))
+
+    def mark(x, carry):
+        r = lax.broadcasted_iota(jnp.int32, (128, 128), 0)
+        spot = (r // 16) * 128 + x * 16 + r % 16
+        lane = lax.broadcasted_iota(jnp.int32, (128, 128), 1)
+        at = pl.ds(pl.multiple_of(x * 128, 128), 128)
+        for b in range(8):
+            order[at, 128 * b : 128 * b + 128] = jnp.where(
+                spot == lane + 128 * b, 1.0, 0.0
+            ).astype(bf16)
+        return carry
+
+    lax.fori_loop(0, 8, mark, 0)
 
     def there(dx, dy):
         fits = None
@@ -663,6 +678,7 @@
             device_id_type=MESH,
         )
 
+    pl.semaphore_wait(barrier, len(AROUND))
     for n, (dx, dy) in enumerate(AROUND):
         pl.when(there(dx, dy))(lambda n=n: edge_copy(n).start())
 
@@ -676,15 +692,27 @@
 
     lax.fori_loop(0, SIDE // BLK, spread, 0)
 
+    def collect(i, carry):
+        for j in range(4):
+            for t in range(0, 4, 2):
+                at = pl.ds(pl.multiple_of(i * 128 + 32 * j + 8 * t, 16), 16)
+                for x in range(8):
+                    first = i * 128 + 8 * (j % 2) + x
+                    two = [field[j // 2, t + s, pl.ds(first, 8, stride=BLK), :] for s in (0, 1)]
+                    pieces[at, 128 * x : 128 * x + 128] = jnp.concatenate(two, 0).astype(bf16)
+        return carry
+
+    lax.fori_loop(0, NB // 8, collect, 0)
+    placed[...] = jnp.dot(pieces[...], order[...], preferred_element_type=f32)
+
     def turn(i, carry):
         for j in range(4):
             for t in range(4):
-                first = i * 128 + 8 * (j % 2)
-                vectors = [
-                    field[j // 2, t, pl.ds(first + x, 8, stride=BLK), :] for x in range(8)
-                ]
-                for b, v in enumerate(swap_pieces(vectors)):
-                    flat[pl.ds(i * 1024 + (8 * t + b) * 4 + j, 8, stride=128), :] = v
+                at = pl.ds(pl.multiple_of(i * 128 + 32 * j + 8 * t, 8), 8)
+                for b in range(8):
+                    flat[pl.ds(i * 1024 + (8 * t + b) * 4 + j, 8, stride=128), :] = placed[
+                        at, 128 * b : 128 * b + 128
+                    ]
         return carry
 
     lax.fori_loop(0, NB // 8, turn, 0)
@@ -774,6 +802,9 @@
         scratch_shapes=[
             pltpu.VMEM((2, 4, SIDE, 128), f32),
             pltpu.VMEM((NB * NB * 4, 128), f32),
+            pltpu.VMEM((1024, 1024), bf16),
+            pltpu.VMEM((512, 1024), bf16),
+            pltpu.VMEM((512, 1024), f32),
             pltpu.VMEM((8, 8, SIDE), f32),
             pltpu.VMEM((2, 8, SIDE), f32),
             pltpu.VMEM((2, SIDE + 16, 128), f32),
@@ -831,14 +862,40 @@
         ext.reshape(EXT * EXT * 4, 128),
         green_blocks,
     )
-    grad, grad_in, grad_bias, grad_out = cell_model(
+    grad, sums = cell_model(
         p3,
         near,
         first_weights(w_in, b_in),
         back_weights(w_in, w_out),
         jnp.pad(w_out, ((0, 6), (0, HIDDEN))),
     )
-    return grad, grad_in, grad_bias.reshape(HIDDEN), grad_out
+    grad, grad_in, grad_bias, grad_out = hand_out(grad, sums)
+    return grad, grad_in.T, grad_bias.reshape(HIDDEN), grad_out
+
+
+def hand_out_kernel(grad_ref, sums_ref, out_ref, first_ref, bias_ref, second_ref):
+    out_ref[...] = grad_ref[...]
+    value = sums_ref[...]
+    first_ref[...] = value[0:9, 0:HIDDEN]
+    bias_ref[...] = value[9:10, 0:HIDDEN]
+    second_ref[0:1, :] = value[10:11, 0:HIDDEN]
+    second_ref[1:2, :] = pltpu.roll(value, HIDDEN, 1)[10:11, 0:HIDDEN]
+
+
+def hand_out(grad, sums):
+    return pl.pallas_call(
+        hand_out_kernel,
+        out_shape=[
+            jax.ShapeDtypeStruct((SIDE, SIDE), f32),
+            jax.ShapeDtypeStruct((9, HIDDEN), f32),
+            jax.ShapeDtypeStruct((1, HIDDEN), f32),
+            jax.ShapeDtypeStruct((2, HIDDEN), f32),
+        ],
+        in_specs=[pl.BlockSpec(memory_space=pltpu.VMEM)] * 2,
+        out_specs=[pl.BlockSpec(memory_space=pltpu.VMEM)] * 4,
+        compiler_params=pltpu.CompilerParams(vmem_limit_bytes=VMEM_BYTES),
+        name="hand_out",
+    )(grad, sums)
 
 
 def solution(mesh):

time: 194 us -> 184 us (0.948)
  local copies, waits for them, and re-layouts: 6.77 us -> 0.75 us
  Pallas kernels: 184 us -> 180 us
    unnamed x10 -> x6, local copies, waits for them, and re-layouts: 6.03 us -> 0.02 us
    pallas_call x1, Pallas kernels: 116 us -> 111 us  [cell_model(): pl.pallas_call(functools.partial(cell_kernel, (nx, ny)), out_shape=[jax.S...]
    pallas_call x1, Pallas kernels: 30.2 us -> 27.6 us  [front(): pl.pallas_call(functools.partial(front_kernel, (nx, ny)), out_shape=[jax....]
    pallas_call x0 -> x1, Pallas kernels: none -> 2.27 us  [hand_out(): pl.pallas_call(hand_out_kernel, out_shape=[jax.ShapeDtypeStruct((SIDE, SI...]
where the time goes in v6:
time: 184 us; the launch traced here: 183 us
  Pallas kernels  180 us (98%)
    pallas_call x1, Pallas kernels, cell_model(): pl.pallas_call(functools.partial(cell_kernel, (nx, ny)), out_shape=[jax.S...  111 us
    pallas_call x1, Pallas kernels, sparse_near(): pl.pallas_call(sparse_kernel, out_shape=jax.ShapeDtypeStruct((2, 4, SIDE...  39.2 us
    pallas_call x1, Pallas kernels, front(): pl.pallas_call(functools.partial(front_kernel, (nx, ny)), out_shape=[jax....  27.6 us

profile of v6, /device:TPU:1, one launch (start us, length us, event | category | flops | bytes accessed | tf_op | source)
XLA Modules:
  0.0 183.5 jit_solution(6528409630034775710)
XLA Ops:
  0.6 27.6 %front.1 = (bf16[56,14,16,128]{3,2,1,0:T(8,128)(2,1)}, f32[3,528,512]{2,1,0:T(8,128)}) custom-call(bf16[2,512,512]{2,1,0:T(8,128)(2,1)} %far_ref.1, f32[512,512]{1,0:T(8,128)} %pillar_ref.1), custom_call_target="tpu_custom_call" | custom-call | tf_op jit(solution)/shard_map/front/pallas_call | solution.py:794
  28.3 0.0 copy-start.2
  28.3 0.0 copy-start
  28.3 0.0 copy-start.1
  28.3 39.2 %sparse_near.1.near_ref = f32[2,4,544,128]{3,2,1,0:T(8,128)} custom-call(s32[24576]{0:T(1024)} %bitcast.21, s32[8]{0:T(128)} %bitcast.25, s32[48,1,512]{2,1,0:T(1,128)} %bitcast.22, bf16[12544,128]{1,0:T(8,128)(2,1)} %bitcast.20, bf16[8,2,256,256]{3,2,1,0:T(8,128)(2,1)} %green_ref.1), custom_call_target="tpu_custom_call" | custom-call | tf_op jit(solution)/shard_map/sparse_near/pallas_call | solution.py:140
  67.5 0.0 copy-done.2
  67.6 0.0 copy-done
  67.7 0.1 copy.16
  67.8 0.7 fusion.9.w1_ref
  68.6 0.0 copy-done.1
  68.6 0.1 select_maximum_fusion.1
  68.7 0.6 fusion.11.v_ref
  69.3 0.6 pad.50.wout_ref
  69.9 111.3 %cell_model.1 = (f32[512,512]{1,0:T(8,128)}, f32[16,128]{1,0:T(8,128)}) custom-call(f32[3,528,512]{2,1,0:T(8,128)} %get-tuple-element.12.p3_ref, f32[2,4,544,128]{3,2,1,0:T(8,128)} %sparse_near.1.near_ref, bf16[256,96]{1,0:T(8,128)(2,1)} %fusion.9.w1_ref, bf16[96,256]{1,0:T(8,128)(2,1)} %fusion.11.v_ref, f32[8,128]{1,0:T(8,128)} %pad.50.wout_ref), custom_call_target="tpu_custom_call" | custom-call | tf_op jit(solution)/shard_map/cell_model/pallas_call | solution.py:540
  181.2 2.3 %hand_out.1 = (f32[512,512]{1,0:T(8,128)}, f32[9,64]{1,0:T(8,128)}, f32[1,64]{1,0:T(1,128)}, f32[2,64]{1,0:T(2,128)}) custom-call(f32[512,512]{1,0:T(8,128)} %get-tuple-element.14.grad_ref, f32[16,128]{1,0:T(8,128)} %get-tuple-element.15.sums_ref), custom_call_target="tpu_custom_call" | custom-call | tf_op jit(solution)/shard_map/hand_out/pallas_call | solution.py:886
  (16 shorter events, 0.2 us)
Async XLA Ops:
  28.3 39.3 %copy-start.2 = (f32[64]{0:T(128)S(1)}, f32[64]{0:T(128)}, u32[]{:S(2)}) copy-start(f32[64]{0:T(128)} %param.16) | copy-start | bytes 772
  28.3 39.3 %copy-start = (f32[64,9]{0,1:T(8,128)S(1)}, f32[64,9]{0,1:T(8,128)}, u32[]{:S(2)}) copy-start(f32[64,9]{0,1:T(8,128)} %param.15) | copy-start | bytes 6916
  28.3 40.3 %copy-start.1 = (f32[2,64]{1,0:T(2,128)S(1)}, f32[2,64]{1,0:T(2,128)}, u32[]{:S(2)}) copy-start(f32[2,64]{1,0:T(2,128)} %param.17) | copy-start | bytes 1540

commit v7 on v6

--- a/solution.py
+++ b/solution.py
@@ -14,7 +14,6 @@
 EXT = NB + 2 * CONE
 GROUPS = 8
 CHUNK = 512
-PARTS = 1
 HIDDEN = 64
 PADROWS = 16
 SROWS = 24
@@ -41,7 +40,7 @@
 
 
 def sparse_kernel(
-    dst_ref, ends_ref, src_ref, ext_ref, green_ref, near_ref, table, rows, rows16, stack, seg, acc
+    dst_ref, ends_ref, src_ref, ext_ref, green_ref, near_ref, table, rows, even, odd, stack, seg, acc
 ):
     chunks = dst_ref.shape[0] // CHUNK
 
@@ -52,43 +51,42 @@
 
     lax.fori_loop(0, EXT * EXT * 4 // 128, widen, 0)
     acc[...] = jnp.zeros_like(acc)
+    seg[...] = jnp.zeros_like(seg)
 
     def gather(base, first, count):
         for q in range(first, first + count):
             d = dst_ref[base + q] * 4
             rows[4 * q : 4 * q + 4, :] = table[pl.ds(pl.multiple_of(d, 4), 4), :]
 
-    def narrow():
+    def narrow(into):
         for j in range(4):
-            rows16[:, 128 * j : 128 * j + 128] = rows[
+            into[:, 128 * j : 128 * j + 128] = rows[
                 pl.ds(j, CHUNK, stride=4), :
             ].astype(bf16)
 
     gather(0, 0, CHUNK)
-    narrow()
-
-    def group(k, carry):
+    narrow(even)
+
+    def group(k, parity):
         start = jnp.where(k == 0, 0, ends_ref[jnp.maximum(k - 1, 0)])
         stop = ends_ref[k]
-        seg[...] = jnp.zeros_like(seg)
-
-        def chunk(c, inner):
-            ahead = jnp.minimum(c + 1, chunks - 1) * CHUNK
+
+        def visit(c, held, into):
             slot = c * CHUNK + lax.broadcasted_iota(jnp.int32, (1, CHUNK), 1)
             live = (slot >= start) & (slot < stop)
             source = jnp.where(live, src_ref[c], -1)
-            for m in range(PARTS):
-                size = NB * NB // PARTS
-                ids = lax.broadcasted_iota(jnp.int32, (size, CHUNK), 0) + size * m
-                hot = jnp.where(ids == source, 1.0, 0.0).astype(bf16)
-                gather(ahead, CHUNK // PARTS * m, CHUNK // PARTS)
-                seg[size * m : size * m + size, :] += jnp.dot(
-                    hot, rows16[...], preferred_element_type=f32
-                )
-            pl.when((c + 1) * CHUNK <= stop)(narrow)
-            return inner
-
-        lax.fori_loop(start // CHUNK, (stop + CHUNK - 1) // CHUNK, chunk, 0)
+            ids = lax.broadcasted_iota(jnp.int32, (NB * NB, CHUNK), 0)
+            hot = jnp.where(ids == source, 1.0, 0.0).astype(bf16)
+            gather(jnp.minimum(c + 1, chunks - 1) * CHUNK, 0, CHUNK)
+            seg[...] += jnp.dot(hot, held[...], preferred_element_type=f32)
+            narrow(into)
+
+        def chunk(c, parity):
+            pl.when(parity == 0)(lambda: visit(c, even, odd))
+            pl.when(parity == 1)(lambda: visit(c, odd, even))
+            return jnp.where((c + 1) * CHUNK <= stop, 1 - parity, parity)
+
+        parity = lax.fori_loop(start // CHUNK, (stop + CHUNK - 1) // CHUNK, chunk, parity)
 
         half = BLK * BLK
         real = green_ref[k, 0]
@@ -101,6 +99,7 @@
         def apply(m, inner):
             at = pl.ds(pl.multiple_of(m * 512, 512), 512)
             value = seg[at, :]
+            seg[at, :] = jnp.zeros((512, 512), f32)
             high = value.astype(bf16)
             low = (value - high.astype(f32)).astype(bf16)
             near = jnp.dot(high, stack[...], preferred_element_type=f32) + jnp.dot(
@@ -111,7 +110,7 @@
             return inner
 
         lax.fori_loop(0, 2, apply, 0)
-        return carry
+        return parity
 
     lax.fori_loop(0, GROUPS, group, 0)
 
@@ -151,6 +150,7 @@
         scratch_shapes=[
             pltpu.VMEM((EXT * EXT * 4, 128), f32),
             pltpu.VMEM((CHUNK * 4, 128), f32),
+            pltpu.VMEM((CHUNK, 512), bf16),
             pltpu.VMEM((CHUNK, 512), bf16),
             pltpu.VMEM((512, 512), bf16),
             pltpu.VMEM((NB * NB, 512), f32),
@@ -518,7 +518,10 @@
     turned = total[...].T
     turned = turned + pltpu.roll(turned, HIDDEN, 1)
     pulled = turned[0:SROWS] + turned[SROWS : 2 * SROWS]
-    first = wout_ref[0:1, :] * pulled[0:10] + wout_ref[1:2, :] * pulled[10:20]
+    first = (
+        wout_ref[0:1, :] * pulled[0:10, 0:HIDDEN] + wout_ref[1:2, :] * pulled[10:20, 0:HIDDEN]
+    )
+    first = jnp.concatenate([first, jnp.zeros((10, 128 - HIDDEN), f32)], 1)
     second = jnp.sum(nh[...].T, axis=0, keepdims=True)
     message = jnp.concatenate([first, second, jnp.zeros((5, 128), f32)], 0)
     finish(
@@ -678,9 +681,6 @@
             device_id_type=MESH,
         )
 
-    pl.semaphore_wait(barrier, len(AROUND))
-    for n, (dx, dy) in enumerate(AROUND):
-        pl.when(there(dx, dy))(lambda n=n: edge_copy(n).start())
 
     def spread(i, carry):
         at = pl.ds(pl.multiple_of(i * BLK, BLK), BLK)
@@ -723,6 +723,9 @@
         return carry
 
     lax.fori_loop(0, NB, pack, 0)
+    pl.semaphore_wait(barrier, len(AROUND))
+    for n, (dx, dy) in enumerate(AROUND):
+        pl.when(there(dx, dy))(lambda n=n: edge_copy(n).start())
     for n, (dx, dy) in enumerate(AROUND):
         pl.when(there(dx, dy))(lambda n=n: far_copy(n).start())
 
@@ -867,7 +870,7 @@
         near,
         first_weights(w_in, b_in),
         back_weights(w_in, w_out),
-        jnp.pad(w_out, ((0, 6), (0, HIDDEN))),
+        w_out,
     )
     grad, grad_in, grad_bias, grad_out = hand_out(grad, sums)
     return grad, grad_in.T, grad_bias.reshape(HIDDEN), grad_out

time: 184 us -> 179 us (0.973)
  Pallas kernels: 180 us -> 177 us
    pallas_call x1, Pallas kernels: 111 us -> 104 us  [cell_model(): pl.pallas_call(functools.partial(cell_kernel, (nx, ny)), out_shape=[jax.S...]
    pallas_call x1, Pallas kernels: 39.2 us -> 45.3 us  [sparse_near(): pl.pallas_call(sparse_kernel, out_shape=jax.ShapeDtypeStruct((2, 4, SIDE...]
    pallas_call x1, Pallas kernels: 27.6 us -> 25.6 us  [front(): pl.pallas_call(functools.partial(front_kernel, (nx, ny)), out_shape=[jax....]
where the time goes in v7:
time: 179 us
  Pallas kernels  177 us (99%)
    pallas_call x1, Pallas kernels, cell_model(): pl.pallas_call(functools.partial(cell_kernel, (nx, ny)), out_shape=[jax.S...  104 us
    pallas_call x1, Pallas kernels, sparse_near(): pl.pallas_call(sparse_kernel, out_shape=jax.ShapeDtypeStruct((2, 4, SIDE...  45.3 us
    pallas_call x1, Pallas kernels, front(): pl.pallas_call(functools.partial(front_kernel, (nx, ny)), out_shape=[jax....  25.6 us

profile of v7, /device:TPU:1, one launch (start us, length us, event | category | flops | bytes accessed | tf_op | source)
XLA Modules:
  0.0 179.2 jit_solution(10319358870151616962)
XLA Ops:
  0.6 25.6 %front.1 = (bf16[56,14,16,128]{3,2,1,0:T(8,128)(2,1)}, f32[3,528,512]{2,1,0:T(8,128)}) custom-call(bf16[2,512,512]{2,1,0:T(8,128)(2,1)} %far_ref.1, f32[512,512]{1,0:T(8,128)} %pillar_ref.1), custom_call_target="tpu_custom_call" | custom-call | tf_op jit(solution)/shard_map/front/pallas_call | solution.py:797
  26.2 0.0 copy-start.2
  26.3 0.0 copy-start
  26.3 0.0 copy-start.1
  26.3 45.3 %sparse_near.1.near_ref = f32[2,4,544,128]{3,2,1,0:T(8,128)} custom-call(s32[24576]{0:T(1024)} %bitcast.21, s32[8]{0:T(128)} %bitcast.25, s32[48,1,512]{2,1,0:T(1,128)} %bitcast.22, bf16[12544,128]{1,0:T(8,128)(2,1)} %bitcast.20, bf16[8,2,256,256]{3,2,1,0:T(8,128)(2,1)} %green_ref.1), custom_call_target="tpu_custom_call" | custom-call | tf_op jit(solution)/shard_map/sparse_near/pallas_call | solution.py:139
  71.6 0.0 copy-done.2
  71.7 0.0 copy-done
  71.8 0.1 copy.16
  71.9 0.7 fusion.9.w1_ref
  72.6 0.0 copy-done.1
  72.7 0.1 select_maximum_fusion.1
  72.8 0.6 fusion.11.v_ref
  73.4 103.6 %cell_model.1 = (f32[512,512]{1,0:T(8,128)}, f32[16,128]{1,0:T(8,128)}) custom-call(f32[3,528,512]{2,1,0:T(8,128)} %get-tuple-element.12.p3_ref, f32[2,4,544,128]{3,2,1,0:T(8,128)} %sparse_near.1.near_ref, bf16[256,96]{1,0:T(8,128)(2,1)} %fusion.9.w1_ref, bf16[96,256]{1,0:T(8,128)(2,1)} %fusion.11.v_ref, f32[2,64]{1,0:T(2,128)} %wout_ref.1), custom_call_target="tpu_custom_call" | custom-call | tf_op jit(solution)/shard_map/cell_model/pallas_call | solution.py:543
  176.9 2.3 %hand_out.1 = (f32[512,512]{1,0:T(8,128)}, f32[9,64]{1,0:T(8,128)}, f32[1,64]{1,0:T(1,128)}, f32[2,64]{1,0:T(2,128)}) custom-call(f32[512,512]{1,0:T(8,128)} %get-tuple-element.14.grad_ref, f32[16,128]{1,0:T(8,128)} %get-tuple-element.15.sums_ref), custom_call_target="tpu_custom_call" | custom-call | tf_op jit(solution)/shard_map/hand_out/pallas_call | solution.py:889
  (16 shorter events, 0.2 us)
Async XLA Ops:
  26.2 45.4 %copy-start.2 = (f32[64]{0:T(128)S(1)}, f32[64]{0:T(128)}, u32[]{:S(2)}) copy-start(f32[64]{0:T(128)} %param.16) | copy-start | bytes 772
  26.3 45.4 %copy-start = (f32[64,9]{0,1:T(8,128)S(1)}, f32[64,9]{0,1:T(8,128)}, u32[]{:S(2)}) copy-start(f32[64,9]{0,1:T(8,128)} %param.15) | copy-start | bytes 6916
  26.3 46.4 %copy-start.1 = (f32[2,64]{1,0:T(2,128)S(1)}, f32[2,64]{1,0:T(2,128)}, u32[]{:S(2)}) copy-start(f32[2,64]{1,0:T(2,128)} %wout_ref.1) | copy-start | bytes 1540

commit v8 on v7

--- a/solution.py
+++ b/solution.py
@@ -96,20 +96,15 @@
         stack[half : 2 * half, 0:half] = imag
         stack[half : 2 * half, half : 2 * half] = real
 
-        def apply(m, inner):
-            at = pl.ds(pl.multiple_of(m * 512, 512), 512)
-            value = seg[at, :]
-            seg[at, :] = jnp.zeros((512, 512), f32)
-            high = value.astype(bf16)
-            low = (value - high.astype(f32)).astype(bf16)
-            near = jnp.dot(high, stack[...], preferred_element_type=f32) + jnp.dot(
-                low, stack[...], preferred_element_type=f32
-            )
-            for j in range(4):
-                acc[j, at, :] += near[:, 128 * j : 128 * j + 128]
-            return inner
-
-        lax.fori_loop(0, 2, apply, 0)
+        value = seg[...]
+        seg[...] = jnp.zeros_like(seg)
+        high = value.astype(bf16)
+        low = (value - high.astype(f32)).astype(bf16)
+        near = jnp.dot(high, stack[...], preferred_element_type=f32) + jnp.dot(
+            low, stack[...], preferred_element_type=f32
+        )
+        for j in range(4):
+            acc[j] += near[:, 128 * j : 128 * j + 128]
         return parity
 
     lax.fori_loop(0, GROUPS, group, 0)

time: 179 us -> 178 us (level); the launches traced: 179 us -> 176 us
  Pallas kernels: 177 us -> 173 us
    pallas_call x1, Pallas kernels: 45.3 us -> 37.2 us  [sparse_near(): pl.pallas_call(sparse_kernel, out_shape=jax.ShapeDtypeStruct((2, 4, SIDE...]
    pallas_call x1, Pallas kernels: 104 us -> 108 us  [cell_model(): pl.pallas_call(functools.partial(cell_kernel, (nx, ny)), out_shape=[jax.S...]
where the time goes in v8:
time: 178 us; the launch traced here: 176 us
  Pallas kernels  173 us (97%)
    pallas_call x1, Pallas kernels, cell_model(): pl.pallas_call(functools.partial(cell_kernel, (nx, ny)), out_shape=[jax.S...  108 us
    pallas_call x1, Pallas kernels, sparse_near(): pl.pallas_call(sparse_kernel, out_shape=jax.ShapeDtypeStruct((2, 4, SIDE...  37.2 us
    pallas_call x1, Pallas kernels, front(): pl.pallas_call(functools.partial(front_kernel, (nx, ny)), out_shape=[jax....  25.6 us

profile of v8, /device:TPU:1, one launch (start us, length us, event | category | flops | bytes accessed | tf_op | source)
XLA Modules:
  0.0 175.7 jit_solution(16306340527535489392)
XLA Ops:
  0.6 25.6 %front.1 = (bf16[56,14,16,128]{3,2,1,0:T(8,128)(2,1)}, f32[3,528,512]{2,1,0:T(8,128)}) custom-call(bf16[2,512,512]{2,1,0:T(8,128)(2,1)} %far_ref.1, f32[512,512]{1,0:T(8,128)} %pillar_ref.1), custom_call_target="tpu_custom_call" | custom-call | tf_op jit(solution)/shard_map/front/pallas_call | solution.py:792
  26.2 0.0 copy-start.2
  26.3 0.0 copy-start
  26.3 0.0 copy-start.1
  26.3 37.2 %sparse_near.1.near_ref = f32[2,4,544,128]{3,2,1,0:T(8,128)} custom-call(s32[24576]{0:T(1024)} %bitcast.21, s32[8]{0:T(128)} %bitcast.25, s32[48,1,512]{2,1,0:T(1,128)} %bitcast.22, bf16[12544,128]{1,0:T(8,128)(2,1)} %bitcast.20, bf16[8,2,256,256]{3,2,1,0:T(8,128)(2,1)} %green_ref.1), custom_call_target="tpu_custom_call" | custom-call | tf_op jit(solution)/shard_map/sparse_near/pallas_call | solution.py:134
  63.4 0.0 copy-done.2
  63.5 0.0 copy-done
  63.6 0.1 copy.16
  63.7 0.7 fusion.9.w1_ref
  64.5 0.0 copy-done.1
  64.5 0.1 select_maximum_fusion.1
  64.6 0.6 fusion.11.v_ref
  65.2 108.2 %cell_model.1 = (f32[512,512]{1,0:T(8,128)}, f32[16,128]{1,0:T(8,128)}) custom-call(f32[3,528,512]{2,1,0:T(8,128)} %get-tuple-element.12.p3_ref, f32[2,4,544,128]{3,2,1,0:T(8,128)} %sparse_near.1.near_ref, bf16[256,96]{1,0:T(8,128)(2,1)} %fusion.9.w1_ref, bf16[96,256]{1,0:T(8,128)(2,1)} %fusion.11.v_ref, f32[2,64]{1,0:T(2,128)} %wout_ref.1), custom_call_target="tpu_custom_call" | custom-call | tf_op jit(solution)/shard_map/cell_model/pallas_call | solution.py:538
  173.4 2.3 %hand_out.1 = (f32[512,512]{1,0:T(8,128)}, f32[9,64]{1,0:T(8,128)}, f32[1,64]{1,0:T(1,128)}, f32[2,64]{1,0:T(2,128)}) custom-call(f32[512,512]{1,0:T(8,128)} %get-tuple-element.14.grad_ref, f32[16,128]{1,0:T(8,128)} %get-tuple-element.15.sums_ref), custom_call_target="tpu_custom_call" | custom-call | tf_op jit(solution)/shard_map/hand_out/pallas_call | solution.py:884
  (16 shorter events, 0.2 us)
Async XLA Ops:
  26.2 37.2 %copy-start.2 = (f32[64]{0:T(128)S(1)}, f32[64]{0:T(128)}, u32[]{:S(2)}) copy-start(f32[64]{0:T(128)} %param.16) | copy-start | bytes 772
  26.3 37.2 %copy-start = (f32[64,9]{0,1:T(8,128)S(1)}, f32[64,9]{0,1:T(8,128)}, u32[]{:S(2)}) copy-start(f32[64,9]{0,1:T(8,128)} %param.15) | copy-start | bytes 6916
  26.3 38.2 %copy-start.1 = (f32[2,64]{1,0:T(2,128)S(1)}, f32[2,64]{1,0:T(2,128)}, u32[]{:S(2)}) copy-start(f32[2,64]{1,0:T(2,128)} %wout_ref.1) | copy-start | bytes 1540
